TPU v7x, 32 devices: a whole 2x2x4 slice. The times are simulated.
32 devices in a mesh: pipe: 4 (over y, x), dp: 8 (over z, core).
Axes of the slice: x: 2, y: 2, z: 4, core: 2. Of those that a mesh axis runs over, the one named last changes fastest.
Arguments:
- images_in: bfloat16 [6, 8, 16, 16, 512], P(None, 'dp'), may hold values from -6 to 6
- conv_local: bfloat16 [4, 3, 3, 512, 128], P('pipe'), may hold values from -0.09375 to 0.09375
- conv_cross: bfloat16 [4, 3, 3, 128, 384], P('pipe'), may hold values from -0.1875 to 0.1875
- reduce_weight: bfloat16 [4, 384, 192], P('pipe'), may hold values from -0.3125 to 0.3125
- spectral_weight: bfloat16 [4, 384, 384], P('pipe'), may hold values from -0.3125 to 0.3125
- expand_weight: bfloat16 [4, 192, 384], P('pipe'), may hold values from -0.4375 to 0.4375
- norm_gain: float32 [4, 1088], P('pipe'), may hold values from 0.5 to 1.5
- norm_bias: float32 [4, 1088], P('pipe'), may hold values from -3 to 3
- cotangent: bfloat16 [6, 8, 16, 16, 512], P(None, 'dp'), may hold values from -6 to 6
- hole_mask: int32 [6, 8, 16, 16], P(None, 'dp'), may hold values from 0 to 1, as said below
Outputs:
- activations: bfloat16 [4, 6, 8, 16, 16, 512], P('pipe', None, 'dp')
- input_grads: float32 [4, 6, 8, 16, 16, 512], P('pipe', None, 'dp')
- grad_conv_local: float32 [4, 3, 3, 512, 128], P('pipe')
- grad_conv_cross: float32 [4, 3, 3, 128, 384], P('pipe')
- grad_reduce: float32 [4, 384, 192], P('pipe')
- grad_spectral: float32 [4, 384, 384], P('pipe')
- grad_expand: float32 [4, 192, 384], P('pipe')
- grad_gain: float32 [4, 1088], P('pipe')
- grad_bias: float32 [4, 1088], P('pipe')
Inputs may be any that keep to these rules, and one draw needn't show every extreme that they name: `hole_mask`: each image has between none and 9 in 10 of its pixels as holes, a heavy-tailed amount.
All inputs are finite; a program needn't handle non-finite values.
Results may differ from a plain program's by a relative error of at most 0.023.
Values may be sent and summed in bfloat16 or wider, within the bound.
No kernel may reach another device: no remote copies, remote signals or barrier semaphores. Data moves between devices by JAX's collectives and lax.ppermute only.
A program may use at most 64 MiB of HBM per device.

v0:
```python
import math

import jax
import jax.numpy as jnp
from jax import lax
from jax.sharding import PartitionSpec as P

CL = 128
CG = 384
CS = 192
NORMS = 1088


EPS = 1e-05
HIGH = lax.Precision.HIGHEST


def from_behind(x, axis, by):
    length = lax.axis_size(axis)
    pairs = [(i, i + by) for i in range(length) if 0 <= i + by < length]
    return lax.ppermute(x, axis, pairs)


def smooth(values):
    return values * jax.nn.sigmoid(values)


def smooth_slope(values):
    logistic = jax.nn.sigmoid(values)
    return logistic * (1.0 + values * (1.0 - logistic))


def patches(values):
    height, breadth = (values.shape[1], values.shape[2])
    padded = jnp.pad(values, ((0, 0), (1, 1), (1, 1), (0, 0)))
    return jnp.concatenate(
        [
            padded[:, row_off : row_off + height, col_off : col_off + breadth]
            for row_off in range(3)
            for col_off in range(3)
        ],
        axis=-1,
    )


def conv_apply(values, kernel):
    flat_kernel = kernel.reshape(-1, kernel.shape[-1])
    return jnp.einsum(
        "bhwk,kd->bhwd", patches(values), flat_kernel, preferred_element_type=jnp.float32
    )


def conv_weight_grad(values, grad_low, kernel_shape):
    return jnp.einsum(
        "bhwk,bhwd->kd", patches(values), grad_low, preferred_element_type=jnp.float32
    ).reshape(kernel_shape)


def conv_input_grad(grad_low, kernel):
    flipped = jnp.flip(kernel, (0, 1)).transpose(0, 1, 3, 2)
    return conv_apply(grad_low, flipped)


def dft_tables(side_len):
    frequencies = side_len // 2 + 1
    spatial = jnp.arange(side_len, dtype=jnp.int32)
    spectral = jnp.arange(frequencies, dtype=jnp.int32)
    angle_cols = (spatial[:, None] * spectral[None, :] % side_len).astype(jnp.float32) * (
        2.0 * math.pi / side_len
    )
    angle_rows = (spatial[:, None] * spatial[None, :] % side_len).astype(jnp.float32) * (
        2.0 * math.pi / side_len
    )
    fold_factor = jnp.where((spectral == 0) | (2 * spectral == side_len), 1.0, 2.0).astype(
        jnp.float32
    )
    return (
        jnp.cos(angle_cols),
        jnp.sin(angle_cols),
        jnp.cos(angle_rows),
        jnp.sin(angle_rows),
        fold_factor,
    )


def to_spectrum(field_in, tables):
    cosine_cols, sine_cols, cosine_rows, sine_rows, _ = tables
    scaling = 1.0 / math.sqrt(field_in.shape[1] * field_in.shape[2])
    real_along = jnp.einsum("bhwc,wk->bhkc", field_in, cosine_cols, precision=HIGH)
    imaginary_along = -jnp.einsum("bhwc,wk->bhkc", field_in, sine_cols, precision=HIGH)
    real_part = jnp.einsum("bhkc,gh->bgkc", real_along, cosine_rows, precision=HIGH) + jnp.einsum(
        "bhkc,gh->bgkc", imaginary_along, sine_rows, precision=HIGH
    )
    imaginary_part = jnp.einsum(
        "bhkc,gh->bgkc", imaginary_along, cosine_rows, precision=HIGH
    ) - jnp.einsum("bhkc,gh->bgkc", real_along, sine_rows, precision=HIGH)
    return jnp.concatenate([real_part, imaginary_part], axis=-1) * scaling


def from_spectrum(field_in, tables):
    cosine_cols, sine_cols, cosine_rows, sine_rows, fold_factor = tables
    scaling = 1.0 / math.sqrt(field_in.shape[1] * cosine_cols.shape[0])
    half_width = field_in.shape[-1] // 2
    real_in = field_in[..., :half_width]
    imaginary_in = field_in[..., half_width:]
    real_rows = jnp.einsum("bgkc,gh->bhkc", real_in, cosine_rows, precision=HIGH) - jnp.einsum(
        "bgkc,gh->bhkc", imaginary_in, sine_rows, precision=HIGH
    )
    imaginary_rows = jnp.einsum(
        "bgkc,gh->bhkc", imaginary_in, cosine_rows, precision=HIGH
    ) + jnp.einsum("bgkc,gh->bhkc", real_in, sine_rows, precision=HIGH)
    folding = fold_factor[None, None, :, None]
    field_out = jnp.einsum(
        "bhkc,wk->bhwc", real_rows * folding, cosine_cols, precision=HIGH
    ) - jnp.einsum("bhkc,wk->bhwc", imaginary_rows * folding, sine_cols, precision=HIGH)
    return field_out * scaling


def moments(values):
    sum_axes = tuple(range(values.ndim - 1))
    count_all = math.prod(values.shape[:-1]) * lax.axis_size("dp")
    average = lax.psum(jnp.sum(values, axis=sum_axes), "dp") / count_all
    centred = values - average
    spread = lax.psum(jnp.sum(centred * centred, axis=sum_axes), "dp") / count_all
    return (average, lax.rsqrt(spread + EPS))


def norm_back(grad_out, act_values, hat_values, gain_slice, inv_std):
    sum_axes = tuple(range(act_values.ndim - 1))
    count_all = math.prod(act_values.shape[:-1]) * lax.axis_size("dp")
    grad_act = grad_out * smooth_slope(act_values)
    sum_act, sum_hat = lax.psum(
        (jnp.sum(grad_act, axis=sum_axes), jnp.sum(grad_act * hat_values, axis=sum_axes)), "dp"
    )
    grad_values = gain_slice * inv_std * (grad_act - (sum_act + hat_values * sum_hat) / count_all)
    return (grad_values, sum_hat, sum_act)


def section_compute(inputs, weights, norm_gains, norm_biases, measure, tables):
    local_kernel, cross_kernel, reduce_matrix, spectral_matrix, expand_matrix = weights

    def normalize(values, offset):
        extent = values.shape[-1]
        average, inv_std = measure(values, offset)
        hat_values = (values - average) * inv_std
        return (
            hat_values,
            norm_gains[offset : offset + extent] * hat_values
            + norm_biases[offset : offset + extent],
        )

    local_part = inputs[..., :CL]
    global_part = inputs[..., CL:]
    pre_local = conv_apply(inputs, local_kernel)
    reduced = jnp.einsum(
        "bhwc,cd->bhwd", global_part, reduce_matrix, preferred_element_type=jnp.float32
    )
    hat_one, act_one = normalize(reduced, 0)
    activated = smooth(act_one)
    spec_low = to_spectrum(activated, tables).astype(jnp.bfloat16)
    spectral_mix = jnp.einsum(
        "bhkc,cd->bhkd", spec_low, spectral_matrix, preferred_element_type=jnp.float32
    )
    hat_two, act_two = normalize(spectral_mix, CS)
    joined = (activated + from_spectrum(smooth(act_two), tables)).astype(jnp.bfloat16)
    pre_global = conv_apply(local_part, cross_kernel) + jnp.einsum(
        "bhwc,cd->bhwd", joined, expand_matrix, preferred_element_type=jnp.float32
    )
    hat_end, act_end = normalize(jnp.concatenate([pre_local, pre_global], axis=-1), CS + CG)
    return (
        smooth(act_end),
        (hat_one, act_one, activated, spec_low, hat_two, act_two, joined, hat_end, act_end),
    )


def section_backward(inputs, weights, norm_gains, inv_std, saved, grad_result, tables):
    local_kernel, cross_kernel, reduce_matrix, spectral_matrix, expand_matrix = weights
    hat_one, act_one, activated, spec_low, hat_two, act_two, joined, hat_end, act_end = saved
    local_part = inputs[..., :CL]
    global_part = inputs[..., CL:]
    grad_end, gain_end, bias_end = norm_back(
        grad_result, act_end, hat_end, norm_gains[CS + CG :], inv_std[CS + CG :]
    )
    grad_end_low = grad_end.astype(jnp.bfloat16)
    grad_pre_local = grad_end_low[..., :CL]
    grad_pre_global = grad_end_low[..., CL:]
    grad_cross = conv_weight_grad(local_part, grad_pre_global, cross_kernel.shape)
    grad_expand = jnp.einsum(
        "bhwc,bhwd->cd", joined, grad_pre_global, preferred_element_type=jnp.float32
    )
    grad_joined = jnp.einsum(
        "bhwd,cd->bhwc", grad_pre_global, expand_matrix, preferred_element_type=jnp.float32
    )
    _, inverse_pull = jax.vjp(
        lambda field_in: from_spectrum(field_in, tables), jnp.zeros(act_two.shape, jnp.float32)
    )
    (grad_after,) = inverse_pull(grad_joined)
    grad_mix, gain_two, bias_two = norm_back(
        grad_after, act_two, hat_two, norm_gains[CS : CS + CG], inv_std[CS : CS + CG]
    )
    grad_mix_low = grad_mix.astype(jnp.bfloat16)
    grad_spectral = jnp.einsum(
        "bhkc,bhkd->cd", spec_low, grad_mix_low, preferred_element_type=jnp.float32
    )
    grad_spec = jnp.einsum(
        "bhkd,cd->bhkc", grad_mix_low, spectral_matrix, preferred_element_type=jnp.float32
    )
    _, forward_pull = jax.vjp(lambda field_in: to_spectrum(field_in, tables), activated)
    (grad_activated,) = forward_pull(grad_spec)
    grad_reduced, gain_one, bias_one = norm_back(
        grad_activated + grad_joined, act_one, hat_one, norm_gains[:CS], inv_std[:CS]
    )
    grad_reduced_low = grad_reduced.astype(jnp.bfloat16)
    grad_reduce = jnp.einsum(
        "bhwc,bhwd->cd", global_part, grad_reduced_low, preferred_element_type=jnp.float32
    )
    grad_global = jnp.einsum(
        "bhwd,cd->bhwc", grad_reduced_low, reduce_matrix, preferred_element_type=jnp.float32
    )
    grad_local = conv_input_grad(grad_pre_global, cross_kernel)
    grad_local_kernel = conv_weight_grad(inputs, grad_pre_local, local_kernel.shape)
    grad_inputs = conv_input_grad(grad_pre_local, local_kernel) + jnp.concatenate(
        [grad_local, grad_global], axis=-1
    )
    gain_terms = jnp.concatenate([gain_one, gain_two, gain_end])
    bias_terms = jnp.concatenate([bias_one, bias_two, bias_end])
    return (
        grad_inputs,
        (grad_local_kernel, grad_cross, grad_reduce, grad_spectral, grad_expand),
        gain_terms,
        bias_terms,
    )


def store(buffer, value, slot_index, active):
    previous = lax.dynamic_index_in_dim(buffer, slot_index, 0, keepdims=False)
    return lax.dynamic_update_index_in_dim(
        buffer, jnp.where(active, value, previous), slot_index, 0
    )


def on_device(
    images_in,
    conv_local,
    conv_cross,
    reduce_weight,
    spectral_weight,
    expand_weight,
    norm_gain,
    norm_bias,
    cotangent,
    hole_mask,
):
    section_count = lax.axis_size("pipe")
    section_rank = lax.axis_index("pipe")
    batches = images_in.shape[0]
    step_count = batches + section_count - 1
    odd_section = section_rank % 2 == 1
    last_section = section_rank == section_count - 1
    weights = (conv_local[0], conv_cross[0], reduce_weight[0], spectral_weight[0], expand_weight[0])
    norm_gains = norm_gain[0]
    norm_biases = norm_bias[0]
    tables = dft_tables(images_in.shape[2])
    blank = jnp.zeros(images_in.shape[1:], jnp.bfloat16)

    def forward_step(carried, step_index):
        recv_act, recv_res, kept_inputs, kept_stats, kept_outputs = carried
        batch_index = step_index - section_rank
        active = (batch_index >= 0) & (batch_index < batches)
        slot_index = jnp.clip(batch_index, 0, batches - 1)
        fresh_image = lax.dynamic_index_in_dim(images_in, slot_index, 0, keepdims=False)
        inputs = jnp.where(section_rank == 0, fresh_image, recv_act)
        recorded = []

        def measure(values, offset):
            average, inv_std = moments(values)
            recorded.append((average, inv_std))
            return (average, inv_std)

        result, _ = section_compute(inputs, weights, norm_gains, norm_biases, measure, tables)
        summed = result + jnp.where(odd_section, recv_res.astype(jnp.float32), 0.0)
        outgoing = summed.astype(jnp.bfloat16)
        residual_out = jnp.where(odd_section, outgoing, inputs)
        next_act, next_res = from_behind((outgoing, residual_out), "pipe", 1)
        statistics = jnp.stack(
            [
                jnp.concatenate([entry_pair[0] for entry_pair in recorded]),
                jnp.concatenate([entry_pair[1] for entry_pair in recorded]),
            ]
        )
        kept_inputs = store(kept_inputs, inputs, slot_index, active)
        kept_stats = store(kept_stats, statistics, slot_index, active)
        kept_outputs = store(kept_outputs, outgoing, slot_index, active)
        return ((next_act, next_res, kept_inputs, kept_stats, kept_outputs), None)

    forward_init = (
        blank,
        blank,
        jnp.zeros(images_in.shape, jnp.bfloat16),
        jnp.zeros((batches, 2, NORMS), jnp.float32),
        jnp.zeros(images_in.shape, jnp.bfloat16),
    )
    forward_state = lax.scan(forward_step, forward_init, jnp.arange(step_count))[0]
    kept_inputs, kept_stats, kept_outputs = (forward_state[2], forward_state[3], forward_state[4])
    pixels = images_in.shape[2] * images_in.shape[3]
    hole_float = hole_mask.astype(jnp.float32)
    hole_counts = jnp.sum(hole_float, axis=(2, 3), keepdims=True)
    weighting = 0.25 + hole_float * pixels / (hole_counts + pixels / 8.0)

    def backward_step(carried, step_index):
        recv_grad, recv_res, grad_store, weight_sums, gain_sum, bias_sum = carried
        batch_index = step_index - (section_count - 1 - section_rank)
        active = (batch_index >= 0) & (batch_index < batches)
        slot_index = jnp.clip(batch_index, 0, batches - 1)
        cotan_slot = lax.dynamic_index_in_dim(cotangent, slot_index, 0, keepdims=False).astype(
            jnp.float32
        )
        weight_slot = lax.dynamic_index_in_dim(weighting, slot_index, 0, keepdims=False)
        seed_grad = (cotan_slot * weight_slot[..., None]).astype(jnp.bfloat16)
        incoming = jnp.where(last_section, seed_grad, recv_grad)
        inputs = lax.dynamic_index_in_dim(kept_inputs, slot_index, 0, keepdims=False)
        statistics = lax.dynamic_index_in_dim(kept_stats, slot_index, 0, keepdims=False)

        def measure(values, offset):
            extent = values.shape[-1]
            return (
                statistics[0, offset : offset + extent],
                statistics[1, offset : offset + extent],
            )

        _, saved = section_compute(inputs, weights, norm_gains, norm_biases, measure, tables)
        grad_inputs, weight_terms, gain_terms, bias_terms = section_backward(
            inputs, weights, norm_gains, statistics[1], saved, incoming.astype(jnp.float32), tables
        )
        grad_total = grad_inputs + jnp.where(odd_section, 0.0, recv_res.astype(jnp.float32))
        outgoing = grad_total.astype(jnp.bfloat16)
        residual_out = jnp.where(odd_section, incoming, outgoing)
        next_grad, next_res = from_behind((outgoing, residual_out), "pipe", -1)
        weight_sums = tuple(
            (
                running + jnp.where(active, addend, 0.0)
                for running, addend in zip(weight_sums, weight_terms)
            )
        )
        gain_sum = gain_sum + jnp.where(active, gain_terms, 0.0)
        bias_sum = bias_sum + jnp.where(active, bias_terms, 0.0)
        grad_store = store(grad_store, grad_total, slot_index, active)
        return ((next_grad, next_res, grad_store, weight_sums, gain_sum, bias_sum), None)

    zero_weights = tuple((jnp.zeros(entry_weight.shape, jnp.float32) for entry_weight in weights))
    backward_init = (
        blank,
        blank,
        jnp.zeros(images_in.shape, jnp.float32),
        zero_weights,
        jnp.zeros((NORMS,), jnp.float32),
        jnp.zeros((NORMS,), jnp.float32),
    )
    state_end = lax.scan(backward_step, backward_init, jnp.arange(0, 0 + step_count))[0]
    sum_local, sum_cross, sum_reduce, sum_spectral, sum_expand = state_end[3]
    totals = lax.psum((sum_local, sum_cross, sum_reduce, sum_spectral, sum_expand), "dp")
    return (
        kept_outputs[None],
        state_end[2][None],
        totals[0][None],
        totals[1][None],
        totals[2][None],
        totals[3][None],
        totals[4][None],
        state_end[4][None],
        state_end[5][None],
    )


def solution(mesh):
    placed = (
        P(None, "dp", None, None, None),
        P("pipe", None, None, None, None),
        P("pipe", None, None, None, None),
        P("pipe", None, None),
        P("pipe", None, None),
        P("pipe", None, None),
        P("pipe", None),
        P("pipe", None),
        P(None, "dp", None, None, None),
        P(None, "dp", None, None),
    )
    return jax.shard_map(
        on_device,
        mesh=mesh,
        in_specs=placed,
        out_specs=(
            P("pipe", None, "dp", None, None, None),
            P("pipe", None, "dp", None, None, None),
            P("pipe", None, None, None, None),
            P("pipe", None, None, None, None),
            P("pipe", None, None),
            P("pipe", None, None),
            P("pipe", None, None),
            P("pipe", None),
            P("pipe", None),
        ),
        check_vma=False,
    )
```

profile of v0, /device:TPU:0, one launch (start us, length us, event | category | flops | bytes accessed | tf_op | source)
XLA Modules:
  0.0 2446.1 jit_solution(6370594468241982411)
XLA Ops:
  17.1 1118.0 %while.54 = (s32[]{:T(128)}, bf16[1,16,16,512]{3,2,1,0:T(8,128)(2,1)S(1)}, bf16[1,16,16,512]{3,2,1,0:T(8,128)(2,1)S(1)}, bf16[6,1,16,16,512]{4,3,2,1,0:T(8,128)(...) while((s32[]{:T(128)}, ...), condition=%wide.region_13.14_spmd.clone.clone, body=%wide.region_0.13_spmd.clone.clone.sunk | while | flops 715901312 | bytes 26637532 | solution.py:303
  23.1 18.1 psum.190
  41.2 13.6 psum.191
  57.7 13.6 psum.192
  71.4 13.6 psum.193
  99.9 13.6 psum.194
  113.6 13.6 psum.195
  149.8 13.6 psum.190
  163.5 13.6 psum.191
  179.9 13.6 psum.192
  193.6 13.6 psum.193
  222.2 13.6 psum.194
  235.9 13.6 psum.195
  273.1 13.6 psum.190
  286.7 13.6 psum.191
  303.2 13.6 psum.192
  316.9 13.6 psum.193
  345.5 13.6 psum.194
  359.1 13.6 psum.195
  396.3 13.6 psum.190
  410.0 13.6 psum.191
  426.5 13.6 psum.192
  440.2 13.6 psum.193
  468.7 13.6 psum.194
  520.3 13.6 psum.190
  534.0 13.6 psum.191
  550.5 13.6 psum.192
  564.2 13.6 psum.193
  592.7 13.6 psum.194
  644.5 13.6 psum.190
  658.2 13.6 psum.191
  674.7 13.6 psum.192
  688.3 13.6 psum.193
  768.6 13.6 psum.190
  798.8 13.6 psum.192
  812.4 13.6 psum.193
  892.8 13.6 psum.190
  922.9 13.6 psum.192
  936.6 13.6 psum.193
  1016.9 13.6 psum.190
  1047.1 13.6 psum.192
  1060.7 13.6 psum.193
  1139.2 1165.9 %while.55 = (s32[]{:T(128)}, bf16[1,16,16,512]{3,2,1,0:T(8,128)(2,1)}, bf16[1,16,16,512]{3,2,1,0:T(8,128)(2,1)}, f32[6,1,16,16,512]{4,3,2,1,0:T(8,128)}, f32[3,3...) while((s32[]{:T(128)}, ...), condition=%wide.region_28.29_spmd.clone.clone, body=%wide.region_15.28_spmd.clone.clone.sunk | while | flops 2081146240 | bytes 119391336 | solution.py:359
  1817.7 13.6 all-reduce.15
  1947.9 13.6 all-reduce.15
  2078.1 13.6 all-reduce.15
  2208.3 13.6 all-reduce.15
  2306.9 125.5 %all-reduce.20.cloned.1.call-done = (f32[1,3,3,512,128]{4,3,2,1,0:T(8,128)}, f32[1,3,3,128,384]{4,3,2,1,0:T(8,128)}, f32[1,384,192]{1,2,0:T(8,128)}, f32[1,384,384]{2,1,0:T(8,128)}, f32[1,192,384]{2,1,0:T(8,128)}) async-done(((f32[1,3,3,512,128]{4,3,2,1,0:T(8,128)}, f32[1,3,3,128,384]{4,3,2,1,0:T(8,128)}, f32[1,384,192]{1,2,0:T(8,128)}, f32[1,384,384]{2,1,0:T(8,128)}, f32[1,192,384]{2,1,0:T(8,128)}), ...) | async-done | bytes 5308432 | tf_op jit(solution)/shard_map/psum | solution.py:361
  (2587 shorter events, 1667.3 us)
Async XLA Ops:
  7.2 2425.2 %all-reduce.20.cloned.1.call-start = ((), (), s32[]{:S(2)}) async-start(), calls=%async_computation | async-start | bytes 10616832 | tf_op jit(solution)/shard_map/psum | solution.py:361
  129.2 10.1 collective-permute-start.1
  132.6 11.2 collective-permute-start
  251.4 11.1 collective-permute-start.1
  255.9 11.2 collective-permute-start
  374.7 10.7 collective-permute-start.1
  379.2 11.2 collective-permute-start
  498.0 11.3 collective-permute-start.1
  503.2 11.2 collective-permute-start
  622.0 11.5 collective-permute-start.1
  627.3 11.2 collective-permute-start
  746.2 11.4 collective-permute-start.1
  751.5 11.2 collective-permute-start
  870.3 11.4 collective-permute-start.1
  875.6 11.2 collective-permute-start
  994.4 11.4 collective-permute-start.1
  999.7 11.2 collective-permute-start
  1118.6 11.4 collective-permute-start.1
  1123.9 11.2 collective-permute-start
  1216.5 19.5 copy-start.48
  1246.8 20.4 collective-permute-start.2
  1248.1 19.1 collective-permute-start.3
  1344.6 19.5 copy-start.48
  1374.9 21.2 collective-permute-start.2
  1376.1 19.9 collective-permute-start.3
  1473.6 19.5 copy-start.48
  1503.8 21.2 collective-permute-start.2
  1505.1 19.9 collective-permute-start.3
  1602.5 19.5 copy-start.48
  1632.7 21.2 collective-permute-start.2
  1634.0 20.0 collective-permute-start.3
  1731.6 19.5 copy-start.48
  1761.8 21.2 collective-permute-start.2
  1763.1 21.2 collective-permute-start.3
  1814.3 19.6 copy-start.47
  1892.0 21.2 collective-permute-start.2
  1893.3 21.1 collective-permute-start.3
  1944.4 19.5 copy-start.47
  1991.9 19.5 copy-start.48
  2022.2 21.2 collective-permute-start.2
  2023.5 21.1 collective-permute-start.3
  2074.6 19.5 copy-start.47
  2122.1 19.5 copy-start.48
  2152.4 21.2 collective-permute-start.2
  2153.7 21.1 collective-permute-start.3
  2204.8 19.6 copy-start.47
  2282.6 21.2 collective-permute-start.2
  2283.9 21.1 collective-permute-start.3
  (420 other events, 2184.0 us)
Sparse Core Ops, SparseCore 0:
  2305.2 127.1 all-reduce.19
where the time goes:
time: 2460 us; the launch traced here: 2450 us
  blocking collectives  1110 us (45%)
  matrix products  456 us (19%)
  local copies, waits for them, and re-layouts  427 us (17%)
  waiting for transfers between devices  186 us (8%)
  other arithmetic  123 us (5%)
  starting transfers between devices  112 us (5%)
    psum x27, blocking collectives, moments(): average = lax.psum(jnp.sum(values, axis=sum_axes), 'dp') / count_all  371 us
    psum x27, blocking collectives, moments(): lax.psum(jnp.sum(centred * centred, axis=sum_axes), 'dp') / count_all  367 us
    psum x27, blocking collectives, norm_back(): lax.psum((jnp.sum(grad_act, axis=sum_axes), jnp.sum(grad_act * hat_values...  367 us
    while x1278, local copies, waits for them, and re-layouts  191 us
    psum x1, waiting for transfers between devices, on_device(): lax.psum((sum_local, sum_cross, sum_reduce, sum_spectral, sum_expand), 'dp')  125 us
    dot_general x54, matrix products, conv_apply(): jnp.einsum('bhwk,kd->bhwd', patches(values), flat_kernel, preferred_eleme...  123 us
    ppermute x36, starting transfers between devices, from_behind(): return lax.ppermute(x, axis, pairs)  112 us
    ppermute x36, waiting for transfers between devices, from_behind(): return lax.ppermute(x, axis, pairs)  60.5 us
  transfers between devices with their start and end apart: 37, of which 25 were waited for; matrix products, arithmetic and copies ran while one was open for 6% of the time, Pallas kernels for 0%

commit v1 on v0

--- a/solution.py
+++ b/solution.py
@@ -1,14 +1,22 @@
+import functools
 import math
 
 import jax
 import jax.numpy as jnp
+import numpy as np
 from jax import lax
+from jax.experimental import pallas as pl
+from jax.experimental.pallas import tpu as pltpu
 from jax.sharding import PartitionSpec as P
 
 CL = 128
 CG = 384
 CS = 192
+CH = 512
 NORMS = 1088
+F32 = jnp.float32
+BF = jnp.bfloat16
+UN = 2
 
 
 EPS = 1e-05
@@ -239,7 +247,7 @@
     )
 
 
-def on_device(
+def general_device(
     images_in,
     conv_local,
     conv_cross,
@@ -372,6 +380,854 @@
     )
 
 
+def dft_np(side):
+    spatial = np.arange(side)
+    spectral = np.arange(side // 2 + 1)
+    turns = spatial[:, None, None, None] * spatial[None, None, :, None] + spectral[None, :, None, None] * spatial[None, None, None, :]
+    angle = (turns % side).reshape(side * spectral.size, side * side) * (2.0 * np.pi / side)
+    fold = np.broadcast_to(np.where((spectral == 0) | (2 * spectral == side), 1.0, 2.0), (side, spectral.size)).reshape(-1, 1)
+    forward = np.concatenate([np.cos(angle), -np.sin(angle)]) / side
+    inverse = np.concatenate([np.cos(angle) * fold, -np.sin(angle) * fold]).T / side
+    return forward, inverse
+
+
+def dot(a, b):
+    return lax.dot_general(a, b, (((1,), (0,)), ((), ())), preferred_element_type=F32)
+
+
+def dot_nt(a, b):
+    return lax.dot_general(a, b, (((1,), (1,)), ((), ())), preferred_element_type=F32)
+
+
+def dot_tn(a, b):
+    return lax.dot_general(a, b, (((0,), (0,)), ((), ())), preferred_element_type=F32)
+
+
+def sig(u):
+    return 0.5 * jnp.tanh(0.5 * u) + 0.5
+
+
+def slope(u):
+    s = sig(u)
+    return s * (1.0 + u * (1.0 - s))
+
+
+QUARTERS, QROWS = 4, 2688
+LAYOUT = {
+    "local": (0, 1152, 1),
+    "cross": (1152, 288, 3),
+    "reduce": (2016, 96, 2),
+    "spectral": (2208, 96, 3),
+    "expand": (2496, 48, 3),
+    "norms": (2640, 16, 3),
+}
+
+
+def pieces(name, start, count, block=0):
+    base, rows, _ = LAYOUT[name]
+    found = []
+    while count:
+        quarter, offset = divmod(start, rows)
+        take = min(count, rows - offset)
+        found.append((quarter, base + block * rows + offset, take))
+        start, count = start + take, count - take
+    return found
+
+
+def stack_rows(parts):
+    return parts[0] if len(parts) == 1 else jnp.concatenate(parts, axis=0)
+
+
+def stack_cols(parts):
+    return parts[0] if len(parts) == 1 else jnp.concatenate(parts, axis=1)
+
+
+def read(w, name, start, count):
+    blocks = LAYOUT[name][2]
+    return stack_cols([stack_rows([w[q, r : r + n] for q, r, n in pieces(name, start, count, j)]) for j in range(blocks)])
+
+
+def write(w, name, start, value):
+    for j in range(LAYOUT[name][2]):
+        done = 0
+        for q, r, n in pieces(name, start, value.shape[0], j):
+            w[q, r : r + n] = value[done : done + n, j * 128 : (j + 1) * 128].astype(w.dtype)
+            done += n
+
+
+def read_norms(w):
+    base = LAYOUT["norms"][0]
+    rows = stack_cols([w[j // 3, base + 16 * (j % 3) : base + 16 * (j % 3) + 16] for j in range(9)]).astype(F32)[:, :NORMS]
+    return rows[0:1] + rows[1:2], rows[2:3] + rows[3:4]
+
+
+def conv_matrix(w):
+    return stack_rows([stack_cols([read(w, "local", k * CH, CL), read(w, "cross", k * CL, CL)]) for k in range(9)])
+
+
+def global_matrix(w):
+    return stack_cols([read(w, "local", k * CH + CL, CG) for k in range(9)])
+
+
+def pack_section(conv_local, conv_cross, reduce_weight, spectral_weight, expand_weight, norm_gain, norm_bias):
+    def blocks(matrix):
+        rows, columns = matrix.shape
+        wide = -(-columns // 128) * 128
+        matrix = jnp.pad(matrix, ((0, 0), (0, wide - columns)))
+        return matrix.reshape(QUARTERS, rows // QUARTERS, wide // 128, 128).transpose(0, 2, 1, 3).reshape(QUARTERS, -1, 128)
+
+    halves = []
+    for values in (norm_gain, norm_bias):
+        high = values.astype(BF)
+        halves += [high, (values - high.astype(F32)).astype(BF)]
+    norms = jnp.pad(jnp.stack(halves), ((0, 12), (0, 12 * 128 - NORMS)))
+    norms = norms.reshape(16, QUARTERS, 3, 128).transpose(1, 2, 0, 3).reshape(QUARTERS, 48, 128)
+    return jnp.concatenate(
+        [
+            conv_local.reshape(QUARTERS, -1, 128),
+            blocks(conv_cross.reshape(-1, CG)),
+            blocks(reduce_weight),
+            blocks(spectral_weight),
+            blocks(expand_weight),
+            norms,
+        ],
+        axis=1,
+    )
+
+
+def unpack_section(packed):
+    def matrix(name, columns):
+        base, rows, blocks = LAYOUT[name]
+        part = packed[:, base : base + rows * blocks].reshape(QUARTERS, blocks, rows, 128).transpose(0, 2, 1, 3)
+        return part.reshape(QUARTERS * rows, blocks * 128)[:, :columns]
+
+    return matrix("local", CL), matrix("cross", CG), matrix("reduce", CS), matrix("spectral", CG), matrix("expand", CG)
+
+
+SOURCES = (
+    (("own", "own"), ("x1", "x2"), ("y1", "y2"), ("x3", "y3")),
+    (("x1", "x2"), ("own", "own"), ("y3", "x3"), ("y1", "y2")),
+    (("y2", "y1"), ("x3", "y3"), ("own", "own"), ("x1", "x2")),
+    (("y2", "x2"), ("y1", "y3"), ("x1", "x3"), ("own", "own")),
+)
+
+
+def load_weights(place, arrived, low, high, w, sems):
+    rank, core = place[0], place[1]
+    for s in range(low, high):
+        for r, sources in enumerate(SOURCES):
+
+            @pl.when(rank == r)
+            def _():
+                for half, name in enumerate(sources[s]):
+                    for other in range(2):
+                        quarter = 2 * half + (1 - core if other else core)
+                        src = arrived["own"].at[quarter] if name == "own" else arrived[name][other]
+                        pltpu.make_async_copy(src, w.at[s - low, quarter], sems.at[s - low, 2 * half + other]).start()
+
+
+def wait_weights(own, index, w, sems):
+    for n in range(4):
+        pltpu.make_async_copy(own.at[0], w.at[index, 0], sems.at[index, n]).wait()
+
+
+def moments_of(v):
+    mean = jnp.mean(v, axis=0, keepdims=True)
+    centred = v - mean
+    return mean, jnp.sum(centred * centred, axis=0, keepdims=True)
+
+
+def combined(mean_ref, square_ref, rows):
+    images = mean_ref.shape[0]
+    means = [mean_ref[b] for b in range(images)]
+    mean = sum(means) / images
+    total = sum(square_ref[b] + rows * (means[b] - mean) ** 2 for b in range(images))
+    return mean, lax.rsqrt(total / (images * rows) + EPS)
+
+
+def beside(v, column, by, side):
+    if by < 0:
+        return jnp.where(column == 0, 0.0, pltpu.roll(v, 1, 0))
+    return jnp.where(column == side - 1, 0.0, pltpu.roll(v, v.shape[0] - 1, 0))
+
+
+def three_columns(dst, b, x, column, side):
+    pixels = x.shape[0]
+    wide = x.astype(F32)
+    for i, v in enumerate((beside(wide, column, -1, side).astype(BF), x, beside(wide, column, 1, side).astype(BF))):
+        dst[i, b, 0:side] = jnp.zeros((side, CL), BF)
+        dst[i, b, side : side + pixels] = v
+        dst[i, b, side + pixels : 2 * side + pixels] = jnp.zeros((side, CL), BF)
+
+
+def nine(src, b, side, flipped):
+    pixels = side * side
+    parts = []
+    for dh in range(3):
+        for dw in range(3):
+            i, j = (2 - dh, 2 - dw) if flipped else (dh, dw)
+            parts.append(src[j, b, i * side : i * side + pixels])
+    return parts
+
+
+def forward_kernel(cfg, *refs):
+    low, high, parts, has_prev, side, images = cfg
+    refs = list(refs)
+    take = lambda n: [refs.pop(0) for _ in range(n)]
+    (place,) = take(1)
+    a_parts = take(parts)
+    prev_parts = take(has_prev)
+    (own,) = take(1)
+    names = needed(low, high)
+    arrived = {n: take(2) for n in names}
+    arrived["own"] = own
+    mf, mi = take(2)
+    if low > 0:
+        take(4)
+    (out,) = take(1) if high < 4 else (None,)
+    vh1_o, vh2_o, vh3_o, iv_o, own_in, own_out, own_spec, own_join = take(8)
+    (cur, w, xp, q, t, f, p, v1, v2, v3, sv, jv, mu1, sq1, mu2, sq2, mu3, sq3, zb, wsem, asem, psem, osem, ksem) = refs
+    pixels = side * side
+    modes = side * (side // 2 + 1)
+    rank = place[0]
+    column = lax.broadcasted_iota(jnp.int32, (pixels, 1), 0) % side
+    load_weights(place, arrived, low, high, w, wsem)
+
+    def fill(sources, slot, sem):
+        rows = images * pixels // max(len(sources), 1)
+        return [pltpu.make_async_copy(ref, cur.at[slot, pl.ds(k * rows, rows)], sem.at[k]) for k, ref in enumerate(sources)]
+
+    copies = fill(a_parts, low % 2, asem) + fill(prev_parts, (low + 1) % 2, psem)
+    for c in copies:
+        c.start()
+    zb[0:side] = jnp.zeros((side, 9 * CL), F32)
+    zb[side + pixels : 2 * side + pixels] = jnp.zeros((side, 9 * CL), F32)
+    for c in copies:
+        c.wait()
+
+    def rows_of(b):
+        return pl.ds(pl.multiple_of(b * pixels, pixels), pixels)
+
+    def modes_of(b):
+        return pl.ds(pl.multiple_of(b * modes, modes), modes)
+
+    def section(index, _):
+        s = index + low
+        a = cur.at[s % 2]
+        o = cur.at[(s + 1) % 2]
+        ws = w.at[index]
+        mine = rank == s
+        first = index == 0
+        saves = [
+            pltpu.make_async_copy(v1, vh1_o.at[index], osem.at[0]),
+            pltpu.make_async_copy(v2, vh2_o.at[index], osem.at[1]),
+            pltpu.make_async_copy(v3, vh3_o.at[index], osem.at[2]),
+        ]
+        keeps = [
+            pltpu.make_async_copy(a, own_in, ksem.at[0]),
+            pltpu.make_async_copy(o, own_out, ksem.at[1]),
+            pltpu.make_async_copy(sv, own_spec, ksem.at[2]),
+            pltpu.make_async_copy(jv, own_join, ksem.at[3]),
+        ]
+
+        @pl.when(mine)
+        def _():
+            keeps[0].start()
+
+        wait_weights(own, index, w, wsem)
+        gain, bias = read_norms(ws)
+
+        def reduce_step(b, _):
+            r = rows_of(b)
+            three_columns(xp, b, a[r, 0:CL], column, side)
+            v = dot(a[r, CL:CH], read(ws, "reduce", 0, CG))[:, :CS]
+            q[r] = v
+            mu1[b], sq1[b] = moments_of(v)
+            return 0
+
+        lax.fori_loop(0, images, reduce_step, 0, unroll=UN)
+        mean1, inv1 = combined(mu1, sq1, pixels)
+
+        @pl.when(jnp.logical_not(first))
+        def _():
+            saves[0].wait()
+
+        def spectral_step(b, _):
+            r, rs = rows_of(b), modes_of(b)
+            hat = (q[r] - mean1) * inv1
+            v1[r] = hat.astype(BF)
+            u = hat * gain[:, :CS] + bias[:, :CS]
+            act = u * sig(u)
+            t[r] = act
+            spec = dot(mf[...], act.astype(BF)).astype(BF)
+            real, imaginary = spec[:modes], spec[modes:]
+            sv[0, rs] = real
+            sv[1, rs] = imaginary
+            mix = dot(real, read(ws, "spectral", 0, CS)) + dot(imaginary, read(ws, "spectral", CS, CS))
+            f[rs] = mix
+            mu2[b], sq2[b] = moments_of(mix)
+            p[r] = dot(stack_cols(nine(xp, b, side, False)), conv_matrix(ws))
+            return 0
+
+        lax.fori_loop(0, images, spectral_step, 0, unroll=UN)
+        saves[0].start()
+
+        @pl.when(mine)
+        def _():
+            keeps[2].start()
+
+        mean2, inv2 = combined(mu2, sq2, modes)
+
+        @pl.when(jnp.logical_not(first))
+        def _():
+            saves[1].wait()
+
+        def join_step(b, _):
+            r, rs = rows_of(b), modes_of(b)
+            hat = (f[rs] - mean2) * inv2
+            v2[rs] = hat.astype(BF)
+            u = hat * gain[:, CS : CS + CG] + bias[:, CS : CS + CG]
+            e = u * sig(u)
+            e = stack_rows([e[:, :CS], e[:, CS:]]).astype(BF)
+            j = (t[r] + dot(mi[...], e)).astype(BF)
+            jv[r] = j
+            pre_global = p[r, CL:CH] + dot(j, read(ws, "expand", 0, CS))
+            zb[side : side + pixels] = dot(a[r, CL:CH], global_matrix(ws))
+            ys = []
+            for dw in range(3):
+                ys.append(sum(zb[dh * side : dh * side + pixels, (dh * 3 + dw) * CL : (dh * 3 + dw + 1) * CL] for dh in range(3)))
+            pre_local = p[r, 0:CL] + ys[1] + beside(ys[0], column, -1, side) + beside(ys[2], column, 1, side)
+            p[r, 0:CL] = pre_local
+            p[r, CL:CH] = pre_global
+            ml, sl = moments_of(pre_local)
+            mg, sg = moments_of(pre_global)
+            mu3[b] = stack_cols([ml, mg])
+            sq3[b] = stack_cols([sl, sg])
+            return 0
+
+        lax.fori_loop(0, images, join_step, 0, unroll=UN)
+        saves[1].start()
+
+        @pl.when(mine)
+        def _():
+            keeps[3].start()
+
+        mean3, inv3 = combined(mu3, sq3, pixels)
+
+        @pl.when(jnp.logical_not(first))
+        def _():
+            saves[2].wait()
+
+        odd = s % 2 == 1
+
+        def end_step(b, _):
+            r = rows_of(b)
+            hat = (p[r] - mean3) * inv3
+            v3[r] = hat.astype(BF)
+            u = hat * gain[:, CS + CG :] + bias[:, CS + CG :]
+            y = u * sig(u)
+            if high > 1:
+                y = y + jnp.where(odd, o[r].astype(F32), 0.0)
+            o[r] = y.astype(BF)
+            return 0
+
+        lax.fori_loop(0, images, end_step, 0, unroll=UN)
+        saves[2].start()
+        iv_o[index] = stack_cols([inv1, inv2, inv3])
+
+        @pl.when(mine)
+        def _():
+            keeps[1].start()
+            for k in keeps:
+                k.wait()
+
+        return 0
+
+    lax.fori_loop(0, high - low, section, 0)
+    last = [
+        pltpu.make_async_copy(v1, vh1_o.at[0], osem.at[0]),
+        pltpu.make_async_copy(v2, vh2_o.at[0], osem.at[1]),
+        pltpu.make_async_copy(v3, vh3_o.at[0], osem.at[2]),
+    ]
+    if out is not None:
+        last.append(pltpu.make_async_copy(cur.at[high % 2], out, asem.at[0]))
+        last[-1].start()
+    for c in last:
+        c.wait()
+
+
+def needed(low, high):
+    return sorted({name for sources in SOURCES for s in range(low, high) for name in sources[s]} - {"own"})
+
+
+ANY = pl.BlockSpec(memory_space=pl.ANY)
+VMEM = pl.BlockSpec(memory_space=pltpu.VMEM)
+SMEM = pl.BlockSpec(memory_space=pltpu.SMEM)
+VMEM_LIMIT = 63 * 2**20
+
+
+def forward_call(low, high, place, a_parts, prev_parts, own, arrived, mf, mi, kept, side, images):
+    pixels, modes = side * side, side * (side // 2 + 1)
+    n, m, count = images * pixels, images * modes, high - low
+    names = needed(low, high)
+    ins = [place, *a_parts, *prev_parts, own]
+    specs = [SMEM] + [ANY] * (len(ins) - 1)
+    for name in names:
+        ins += arrived[name]
+        specs += [ANY, ANY]
+    ins += [mf, mi]
+    specs += [VMEM, VMEM]
+    aliases = {}
+    if low > 0:
+        for i, x in enumerate(kept):
+            aliases[len(ins)] = 4 + (high < 4) + i
+            ins.append(x)
+            specs.append(ANY)
+    shape = jax.ShapeDtypeStruct
+    outs = [shape((n, CH), BF)] if high < 4 else []
+    outs += [
+        shape((count, n, CS), BF),
+        shape((count, m, CG), BF),
+        shape((count, n, CH), BF),
+        shape((count, 1, NORMS), F32),
+        shape((n, CH), BF),
+        shape((n, CH), BF),
+        shape((2, m, CS), BF),
+        shape((n, CS), BF),
+    ]
+    out_specs = [ANY] * (3 + (high < 4)) + [VMEM] + [ANY] * 4
+    dma = pltpu.SemaphoreType.DMA
+    scratch = [
+        pltpu.VMEM((2, n, CH), BF),
+        pltpu.VMEM((count, QUARTERS, QROWS, 128), BF),
+        pltpu.VMEM((3, images, pixels + 2 * side, CL), BF),
+        pltpu.VMEM((n, CS), F32),
+        pltpu.VMEM((n, CS), F32),
+        pltpu.VMEM((m, CG), F32),
+        pltpu.VMEM((n, CH), F32),
+        pltpu.VMEM((n, CS), BF),
+        pltpu.VMEM((m, CG), BF),
+        pltpu.VMEM((n, CH), BF),
+        pltpu.VMEM((2, m, CS), BF),
+        pltpu.VMEM((n, CS), BF),
+        *[pltpu.VMEM((images, 1, c), F32) for c in (CS, CS, CG, CG, CH, CH)],
+        pltpu.VMEM((pixels + 2 * side, 9 * CL), F32),
+        dma((count, 4)),
+        dma((max(len(a_parts), 1),)),
+        dma((max(len(prev_parts), 1),)),
+        dma((3,)),
+        dma((4,)),
+    ]
+    cfg = (low, high, len(a_parts), len(prev_parts), side, images)
+    return pl.pallas_call(
+        functools.partial(forward_kernel, cfg),
+        out_shape=outs,
+        in_specs=specs,
+        out_specs=out_specs,
+        scratch_shapes=scratch,
+        input_output_aliases=aliases,
+        name=f"forward_{low}_{high}",
+        cost_estimate=pl.CostEstimate(flops=count * images * 650_000_000, bytes_accessed=count * 10_000_000, transcendentals=0),
+        compiler_params=pltpu.CompilerParams(vmem_limit_bytes=VMEM_LIMIT),
+    )(*ins)
+
+
+def backward_kernel(cfg, *refs):
+    low, high, parts, has_above, side, images = cfg
+    refs = list(refs)
+    take = lambda n: [refs.pop(0) for _ in range(n)]
+    (place,) = take(1)
+    g_parts = take(parts)
+    above = take(has_above)
+    (own,) = take(1)
+    arrived = {n: take(2) for n in needed(low, high)}
+    arrived["own"] = own
+    mft, mit, vh1, vh2, vh3, iv, own_in, own_spec, own_join = take(9)
+    g_outs = take(parts) if low > 0 else []
+    (above_out,) = take(1) if low > 0 else (None,)
+    ab, own_grad, own_terms = take(3)
+    (grad, w, xp, du, du1, du2, dj, dxl, dxg, zb, dpv, dqv, dfv, h1, h2, h3, ain, sv, jv, x9, d9, terms) = refs[:22]
+    wsem, gsem, asem, hsem, ksem, osem = refs[22:]
+    pixels = side * side
+    modes = side * (side // 2 + 1)
+    n1, n2 = float(images * pixels), float(images * modes)
+    count = high - low
+    rank = place[0]
+    column = lax.broadcasted_iota(jnp.int32, (pixels, 1), 0) % side
+
+    def fill(sources, slot, sem):
+        rows = images * pixels // max(len(sources), 1)
+        return [pltpu.make_async_copy(ref, grad.at[slot, pl.ds(k * rows, rows)], sem.at[k]) for k, ref in enumerate(sources)]
+
+    def hats(index, slot):
+        return [
+            pltpu.make_async_copy(vh3.at[index], h3.at[slot], hsem.at[slot, 0]),
+            pltpu.make_async_copy(vh2.at[index], h2.at[slot], hsem.at[slot, 1]),
+            pltpu.make_async_copy(vh1.at[index], h1.at[slot], hsem.at[slot, 2]),
+        ]
+
+    top = high - 1
+    copies = fill(g_parts, top % 2, gsem) + fill(above, (top + 1) % 2, asem)
+    for c in copies + hats(count - 1, top % 2):
+        c.start()
+    load_weights(place, arrived, low, high, w, wsem)
+
+    owns = [
+        pltpu.make_async_copy(own_in, ain, ksem.at[0]),
+        pltpu.make_async_copy(own_spec, sv, ksem.at[1]),
+        pltpu.make_async_copy(own_join, jv, ksem.at[2]),
+    ]
+    in_range = jnp.logical_and(rank >= low, rank < high)
+
+    @pl.when(in_range)
+    def _():
+        for c in owns:
+            c.start()
+
+    zb[0:side] = jnp.zeros((side, 9 * CL), F32)
+    zb[side + pixels : 2 * side + pixels] = jnp.zeros((side, 9 * CL), F32)
+    for c in copies:
+        c.wait()
+
+    def rows_of(b):
+        return pl.ds(pl.multiple_of(b * pixels, pixels), pixels)
+
+    def modes_of(b):
+        return pl.ds(pl.multiple_of(b * modes, modes), modes)
+
+    def part(v):
+        return jnp.sum(v.reshape(v.shape[0] // 8, 8, v.shape[1]), axis=0)
+
+    def fin(v):
+        return jnp.sum(v, axis=0, keepdims=True)
+
+    def none(c):
+        return jnp.zeros((8, c), F32), jnp.zeros((8, c), F32)
+
+    def section(step, _):
+        index = count - 1 - step
+        s = low + index
+        slot = s % 2
+        g = grad.at[s % 2]
+        o = grad.at[(s + 1) % 2]
+        ws = w.at[index]
+        v1, v2, v3 = h1.at[slot], h2.at[slot], h3.at[slot]
+        mine = rank == s
+        for c in hats(index, slot):
+            c.wait()
+
+        @pl.when(index > 0)
+        def _():
+            for c in hats(index - 1, 1 - slot):
+                c.start()
+
+        wait_weights(own, index, w, wsem)
+        gain, bias = read_norms(ws)
+        inv = iv[index]
+        g1, g2, g3 = gain[:, :CS], gain[:, CS : CS + CG], gain[:, CS + CG :]
+        b1, b2, b3 = bias[:, :CS], bias[:, CS : CS + CG], bias[:, CS + CG :]
+        c1, c2, c3 = g1 * inv[:, :CS], g2 * inv[:, CS : CS + CG], g3 * inv[:, CS + CG :]
+
+        def end_step(b, c):
+            r = rows_of(b)
+            hat = v3[r].astype(F32)
+            d = g[r].astype(F32) * slope(g3 * hat + b3)
+            du[r] = d
+            return c[0] + part(d), c[1] + part(d * hat)
+
+        suma, sumb = lax.fori_loop(0, images, end_step, none(CH), unroll=UN)
+        suma3, sumb3 = fin(suma), fin(sumb)
+        mean_a3, mean_b3 = suma3 / n1, sumb3 / n1
+
+        def join_step(b, c):
+            r, rs = rows_of(b), modes_of(b)
+            dp = (c3 * (du[r] - (mean_a3 + v3[r].astype(F32) * mean_b3))).astype(BF)
+            dpv[r] = dp
+            three_columns(xp, b, dp[:, :CL], column, side)
+            djv = dot_nt(dp[:, CL:], read(ws, "expand", 0, CS))
+            dj[r] = djv
+            de = dot(mit[...], djv.astype(BF))
+            de = stack_cols([de[:modes], de[modes:]])
+            hat = v2[rs].astype(F32)
+            d = de * slope(g2 * hat + b2)
+            du2[rs] = d
+            zb[side : side + pixels] = dot_nt(dp, conv_matrix(ws))
+            ys = []
+            for dw in range(3):
+                ys.append(
+                    sum(zb[(2 - dh) * side : (2 - dh) * side + pixels, (dh * 3 + dw) * CL : (dh * 3 + dw + 1) * CL] for dh in range(3))
+                )
+            dxl[r] = ys[1] + beside(ys[0], column, 1, side) + beside(ys[2], column, -1, side)
+            return c[0] + part(d), c[1] + part(d * hat)
+
+        suma, sumb = lax.fori_loop(0, images, join_step, none(CG), unroll=UN)
+        suma2, sumb2 = fin(suma), fin(sumb)
+        mean_a2, mean_b2 = suma2 / n2, sumb2 / n2
+
+        def spectral_step(b, c):
+            r, rs = rows_of(b), modes_of(b)
+            df = (c2 * (du2[rs] - (mean_a2 + v2[rs].astype(F32) * mean_b2))).astype(BF)
+            dfv[rs] = df
+            ds = dot_nt(df, read(ws, "spectral", 0, CG))
+            ds = stack_rows([ds[:, :CS], ds[:, CS:]]).astype(BF)
+            dt = dj[r] + dot(mft[...], ds)
+            hat = v1[r].astype(F32)
+            d = dt * slope(g1 * hat + b1)
+            du1[r] = d
+            dxg[r] = dot_nt(stack_cols(nine(xp, b, side, True)), global_matrix(ws))
+            return c[0] + part(d), c[1] + part(d * hat)
+
+        suma, sumb = lax.fori_loop(0, images, spectral_step, none(CS), unroll=UN)
+        suma1, sumb1 = fin(suma), fin(sumb)
+        mean_a1, mean_b1 = suma1 / n1, sumb1 / n1
+        even = s % 2 == 0
+
+        def reduce_step(b, c):
+            r = rows_of(b)
+            dq = (c1 * (du1[r] - (mean_a1 + v1[r].astype(F32) * mean_b1))).astype(BF)
+            dqv[r] = dq
+            dx = stack_cols([dxl[r], dxg[r] + dot_nt(dq, read(ws, "reduce", 0, CG)[:, :CS])])
+            if low < 3:
+                dx = dx + jnp.where(even, o[r].astype(F32), 0.0)
+            o[r] = dx.astype(BF)
+            return c
+
+        lax.fori_loop(0, images, reduce_step, 0, unroll=UN)
+        ab[index, 0:1] = stack_cols([suma1, suma2, suma3])
+        ab[index, 1:2] = stack_cols([sumb1, sumb2, sumb3])
+
+        @pl.when(mine)
+        def _():
+            keep = pltpu.make_async_copy(o, own_grad, osem.at[0])
+            keep.start()
+            for c in owns:
+                c.wait()
+
+            def nine_step(b, _):
+                r = rows_of(b)
+                for k, v in enumerate(nine(xp, b, side, True)):
+                    d9[r, k * CL : (k + 1) * CL] = v
+                return 0
+
+            lax.fori_loop(0, images, nine_step, 0)
+
+            def nine_inputs(b, _):
+                r = rows_of(b)
+                three_columns(xp, b, ain[r, 0:CL], column, side)
+                for k, v in enumerate(nine(xp, b, side, False)):
+                    x9[r, k * CL : (k + 1) * CL] = v
+                return 0
+
+            lax.fori_loop(0, images, nine_inputs, 0)
+            for dh in range(3):
+                v = dot_tn(x9[:, dh * 3 * CL : (dh + 1) * 3 * CL], dpv[...])
+                for dw in range(3):
+                    k = dh * 3 + dw
+                    write(terms, "local", k * CH, v[dw * CL : (dw + 1) * CL, :CL])
+                    write(terms, "cross", k * CL, v[dw * CL : (dw + 1) * CL, CL:])
+            for dh in range(3):
+                v = dot_tn(ain[:, CL:], d9[:, dh * 3 * CL : (dh + 1) * 3 * CL])
+                for dw in range(3):
+                    write(terms, "local", (dh * 3 + dw) * CH + CL, v[:, dw * CL : (dw + 1) * CL])
+            v = dot_tn(ain[:, CL:], dqv[...])
+            write(terms, "reduce", 0, stack_cols([v, jnp.zeros((CG, 256 - CS), F32)]))
+            write(terms, "spectral", 0, dot_tn(sv[0], dfv[...]))
+            write(terms, "spectral", CS, dot_tn(sv[1], dfv[...]))
+            write(terms, "expand", 0, dot_tn(jv[...], dpv[:, CL:]))
+            for quarter in range(QUARTERS):
+                terms[quarter, LAYOUT["norms"][0] :] = jnp.zeros((48, 128), BF)
+            send = pltpu.make_async_copy(terms, own_terms, osem.at[1])
+            send.start()
+            send.wait()
+            keep.wait()
+
+        return 0
+
+    lax.fori_loop(0, count, section, 0)
+    if low > 0:
+        rows = images * pixels // parts
+        finals = [pltpu.make_async_copy(grad.at[low % 2], above_out, asem.at[0])]
+        for k, ref in enumerate(g_outs):
+            finals.append(pltpu.make_async_copy(grad.at[(low + 1) % 2, pl.ds(k * rows, rows)], ref, gsem.at[k]))
+        for c in finals:
+            c.start()
+        for c in finals:
+            c.wait()
+
+
+def backward_call(low, high, place, g_parts, above, own, arrived, mft, mit, hats, iv, kept, side, images):
+    pixels, modes = side * side, side * (side // 2 + 1)
+    n, m, count = images * pixels, images * modes, high - low
+    own_in, own_spec, own_join = kept
+    ins = [place, *g_parts, *above, own]
+    specs = [SMEM] + [ANY] * (len(ins) - 1)
+    own_at = len(ins) - 1
+    for name in needed(low, high):
+        ins += arrived[name]
+        specs += [ANY, ANY]
+    ins += [mft, mit, *hats, iv, own_in, own_spec, own_join]
+    specs += [VMEM, VMEM, ANY, ANY, ANY, VMEM, ANY, ANY, ANY]
+    shape = jax.ShapeDtypeStruct
+    outs, out_specs, aliases = [], [], {}
+    if low > 0:
+        outs += [shape(g.shape, BF) for g in g_parts] + [shape((n, CH), BF)]
+        out_specs += [ANY] * len(outs)
+        aliases = {1 + k: k for k in range(len(g_parts))}
+    aliases[len(ins) - 3] = len(outs) + 1
+    aliases[own_at] = len(outs) + 2
+    outs += [shape((count, 2, NORMS), F32), shape((n, CH), BF), shape((QUARTERS, QROWS, 128), BF)]
+    out_specs += [VMEM, ANY, ANY]
+    dma = pltpu.SemaphoreType.DMA
+    scratch = [
+        pltpu.VMEM((2, n, CH), BF),
+        pltpu.VMEM((count, QUARTERS, QROWS, 128), BF),
+        pltpu.VMEM((3, images, pixels + 2 * side, CL), BF),
+        pltpu.VMEM((n, CH), F32),
+        pltpu.VMEM((n, CS), F32),
+        pltpu.VMEM((m, CG), F32),
+        pltpu.VMEM((n, CS), F32),
+        pltpu.VMEM((n, CL), F32),
+        pltpu.VMEM((n, CG), F32),
+        pltpu.VMEM((pixels + 2 * side, 9 * CL), F32),
+        pltpu.VMEM((n, CH), BF),
+        pltpu.VMEM((n, CS), BF),
+        pltpu.VMEM((m, CG), BF),
+        pltpu.VMEM((2, n, CS), BF),
+        pltpu.VMEM((2, m, CG), BF),
+        pltpu.VMEM((2, n, CH), BF),
+        pltpu.VMEM((n, CH), BF),
+        pltpu.VMEM((2, m, CS), BF),
+        pltpu.VMEM((n, CS), BF),
+        pltpu.VMEM((n, 9 * CL), BF),
+        pltpu.VMEM((n, 9 * CL), BF),
+        pltpu.VMEM((QUARTERS, QROWS, 128), BF),
+        dma((count, 4)),
+        dma((len(g_parts),)),
+        dma((max(len(above), 1),)),
+        dma((2, 3)),
+        dma((3,)),
+        dma((2,)),
+    ]
+    cfg = (low, high, len(g_parts), len(above), side, images)
+    return pl.pallas_call(
+        functools.partial(backward_kernel, cfg),
+        out_shape=outs,
+        in_specs=specs,
+        out_specs=out_specs,
+        scratch_shapes=scratch,
+        input_output_aliases=aliases,
+        name=f"backward_{low}_{high}",
+        cost_estimate=pl.CostEstimate(flops=count * images * 900_000_000, bytes_accessed=count * 10_000_000, transcendentals=0),
+        compiler_params=pltpu.CompilerParams(vmem_limit_bytes=VMEM_LIMIT),
+    )(*ins)
+
+
+def exchange_weights(own, rank, core):
+    def over(bit, x):
+        return lax.ppermute(x, "pipe", [(i, i ^ bit) for i in range(4)])
+
+    def swap(x):
+        return lax.ppermute(x, "dp", [(i, i ^ 1) for i in range(lax.axis_size("dp"))])
+
+    def quarter(half):
+        return lax.dynamic_index_in_dim(own, 2 * half + core, 0, keepdims=False)
+
+    first, second = quarter(0), quarter(1)
+    got = {}
+    got["x1"] = over(1, first)
+    got["y1"] = over(2, jnp.where(rank == 0, second, first))
+    got["x2"] = over(1, jnp.where(rank == 2, got["y1"], second))
+    got["y2"] = over(2, jnp.where(rank == 0, first, jnp.where(rank == 1, got["x1"], second)))
+    got["x3"] = over(1, jnp.where(rank == 0, got["y2"], jnp.where(rank == 2, second, got["y1"])))
+    got["y3"] = over(2, jnp.where(rank == 1, second, jnp.where(rank == 3, got["x1"], got["x2"])))
+    return {name: (x, swap(x)) for name, x in got.items()}
+
+
+def local_device(images_in, conv_local, conv_cross, reduce_weight, spectral_weight, expand_weight, norm_gain, norm_bias, cotangent, hole_mask):
+    batches, _, side, _, channels = images_in.shape
+    pixels = side * side
+    dp_size = lax.axis_size("dp")
+    chips = dp_size // 2
+    rank = lax.axis_index("pipe")
+    dp_rank = lax.axis_index("dp")
+    z, core = dp_rank // 2, dp_rank % 2
+    before = (dp_size - batches) // 2
+    after = dp_size - batches - before
+    holders = range(before, before + batches)
+    table_to, table_from = dft_np(side)
+    mf, mi = jnp.asarray(table_to, BF), jnp.asarray(table_from, BF)
+    mft, mit = jnp.asarray(table_to.T, BF), jnp.asarray(table_from.T, BF)
+
+    def swap(x):
+        return lax.ppermute(x, "dp", [(i, i ^ 1) for i in range(dp_size)])
+
+    def to_batches(x):
+        x = jnp.pad(x, ((before, after), (0, 0), (0, 0))).reshape(chips, 2, pixels, channels)
+        mine = lax.dynamic_index_in_dim(x, core, 1, keepdims=False)
+        other = swap(lax.dynamic_index_in_dim(x, 1 - core, 1, keepdims=False))
+        pairs = jnp.stack([mine, other], axis=1)
+        parts = []
+        for k in range(chips):
+            part = lax.dynamic_index_in_dim(pairs, z ^ k, 0, keepdims=False)
+            if k:
+                part = lax.ppermute(part, "dp", [(i, i ^ (2 * k)) for i in range(dp_size) if i ^ (2 * k) in holders])
+            parts.append(part.reshape(2 * pixels, channels))
+        return parts
+
+    def to_images(x):
+        x = x.reshape(chips, 2, pixels, channels)
+        parts = []
+        for k in range(chips):
+            part = x[k]
+            if k:
+                part = lax.ppermute(part, "dp", [(i, i ^ (2 * k)) for i in holders])
+            parts.append(part)
+        parts = jnp.stack(parts)
+        parts = jnp.stack([lax.dynamic_index_in_dim(parts, z ^ k, 0, keepdims=False) for k in range(chips)])
+        mine, other = parts[:, 0], swap(parts[:, 1])
+        both = jnp.where(core == 0, jnp.stack([mine, other], axis=1), jnp.stack([other, mine], axis=1))
+        return both.reshape(dp_size, pixels, channels)[before : before + batches]
+
+    own = pack_section(
+        conv_local[0], conv_cross[0], reduce_weight[0], spectral_weight[0], expand_weight[0], norm_gain[0], norm_bias[0]
+    )
+    arrived = exchange_weights(own, rank, core)
+    inputs = to_batches(images_in.reshape(batches, pixels, channels))
+    hole_float = hole_mask.astype(F32)
+    hole_counts = jnp.sum(hole_float, axis=(2, 3), keepdims=True)
+    weighting = 0.25 + hole_float * pixels / (hole_counts + pixels / 8.0)
+    seed = (cotangent.astype(F32) * weighting[..., None]).astype(BF)
+    seeds = to_batches(seed.reshape(batches, pixels, channels))
+    place = jnp.stack([rank, core]).astype(jnp.int32)
+
+    out0, *hats0, iv0, in_k, out_k, spec_k, join_k = forward_call(
+        0, 1, place, inputs, [], own, arrived, mf, mi, (), side, dp_size
+    )
+    kept = (in_k, out_k, spec_k, join_k)
+    *hats1, iv1, in_k, out_k, spec_k, join_k = forward_call(
+        1, 4, place, [out0], inputs, own, arrived, mf, mi, kept, side, dp_size
+    )
+    activations = to_images(out_k)
+    *grads0, grad1, ab1, in_k, own = backward_call(
+        1, 4, place, seeds, [], own, arrived, mft, mit, hats1, iv1, (in_k, spec_k, join_k), side, dp_size
+    )
+    ab0, own_grad, own_terms = backward_call(
+        0, 1, place, grads0, [grad1], own, arrived, mft, mit, hats0, iv0, (in_k, spec_k, join_k), side, dp_size
+    )
+    input_grads = to_images(own_grad).astype(F32)
+    terms = lax.psum(own_terms, "dp").astype(F32)
+    ab = lax.psum(lax.dynamic_index_in_dim(jnp.concatenate([ab0, ab1]), rank, 0, keepdims=False), "dp")
+    shapes = (conv_local.shape, conv_cross.shape, reduce_weight.shape, spectral_weight.shape, expand_weight.shape)
+    outs = (1, batches, 1, side, side, channels)
+    return (
+        activations.reshape(outs),
+        input_grads.reshape(outs),
+        *(t.reshape(n) for t, n in zip(unpack_section(terms), shapes)),
+        ab[1:2],
+        ab[0:1],
+    )
+
+
 def solution(mesh):
     placed = (
         P(None, "dp", None, None, None),
@@ -385,6 +1241,12 @@
         P(None, "dp", None, None, None),
         P(None, "dp", None, None),
     )
+
+    def on_device(images_in, *rest):
+        dp_size = lax.axis_size("dp")
+        fits = images_in.shape[1] == 1 and dp_size == 8 and images_in.shape[0] <= dp_size and lax.axis_size("pipe") == 4
+        return (local_device if fits else general_device)(images_in, *rest)
+
     return jax.shard_map(
         on_device,
         mesh=mesh,

time: 2460 us -> 449 us (0.18)
  blocking collectives: 1110 us -> 15.1 us
  matrix products: 456 us -> 0 us
  local copies, waits for them, and re-layouts: 427 us -> 45 us
  Pallas kernels: 0 us -> 175 us
  other arithmetic: 123 us -> 21.9 us
  waiting for transfers between devices: 186 us -> 109 us
  starting transfers between devices: 112 us -> 62.5 us
    psum x81 -> x1, blocking collectives: 1110 us -> 15.1 us  [local_device(): lax.psum(lax.dynamic_index_in_dim(jnp.concatenate([ab0, ab1]), rank, 0, k...]
    dot_general x504 -> x0, matrix products: 456 us -> none  [the longest x54 123 us: conv_apply(): jnp.einsum('bhwk,kd->bhwd', patches(values), flat_kernel, preferred_eleme...]
    while x1278 -> x0, local copies, waits for them, and re-layouts: 191 us -> none
    pallas_call x0 -> x4, Pallas kernels: none -> 175 us  [the longest x2 97.8 us: backward_call(): pl.pallas_call(functools.partial(backward_kernel, cfg), out_shape=outs, i...]
    psum x1, waiting for transfers between devices: 125 us -> 18 us  [local_device(): terms = lax.psum(own_terms, 'dp').astype(F32)]
    dynamic_slice x45 -> x2, local copies, waits for them, and re-layouts: 51.1 us -> 0.29 us  [to_images(): lax.dynamic_index_in_dim(parts, z ^ k, 0, keepdims=False)]
    ppermute x36 -> x28, starting transfers between devices: 112 us -> 62.5 us  [the longest x6 34.3 us: to_batches(): lax.ppermute(part, 'dp', [(i, i ^ 2 * k) for i in range(dp_size) if i ^ 2...]
    dot_general x18 -> x0, local copies, waits for them, and re-layouts: 47.5 us -> none  [conv_weight_grad(): jnp.einsum('bhwk,bhwd->kd', patches(values), grad_low, preferred_element_...]
  transfers between devices with their start and end apart: 37 -> 29, of which waited for: 25 -> 7; matrix products, arithmetic and copies ran while one was open for 6% -> 11% of each run, Pallas kernels for 0% -> 40%
where the time goes in v1:
time: 449 us; the launch traced here: 443 us
  Pallas kernels  175 us (39%)
  waiting for transfers between devices  109 us (24%)
  starting transfers between devices  62.5 us (14%)
  local copies, waits for them, and re-layouts  45 us (10%)
  other arithmetic  21.9 us (5%)
  blocking collectives  15.1 us (3%)
  between operations  15 us (3%)
    pallas_call x2, Pallas kernels, backward_call(): pl.pallas_call(functools.partial(backward_kernel, cfg), out_shape=outs, i...  97.8 us
    pallas_call x2, Pallas kernels, forward_call(): pl.pallas_call(functools.partial(forward_kernel, cfg), out_shape=outs, in...  77.4 us
    ppermute x6, waiting for transfers between devices, to_images(): part = lax.ppermute(part, 'dp', [(i, i ^ 2 * k) for i in holders])  49.7 us
    ppermute x6, starting transfers between devices, to_batches(): lax.ppermute(part, 'dp', [(i, i ^ 2 * k) for i in range(dp_size) if i ^ 2...  34.3 us
    ppermute x6, waiting for transfers between devices, over(): return lax.ppermute(x, 'pipe', [(i, i ^ bit) for i in range(4)])  28.2 us
    psum x1, waiting for transfers between devices, local_device(): terms = lax.psum(own_terms, 'dp').astype(F32)  18 us
    psum x1, blocking collectives, local_device(): lax.psum(lax.dynamic_index_in_dim(jnp.concatenate([ab0, ab1]), rank, 0, k...  15.1 us
    ppermute x6, waiting for transfers between devices, to_batches(): lax.ppermute(part, 'dp', [(i, i ^ 2 * k) for i in range(dp_size) if i ^ 2...  12.8 us
  transfers between devices with their start and end apart: 29, of which 7 were waited for; matrix products, arithmetic and copies ran while one was open for 11% of the time, Pallas kernels for 40%

profile of v1, /device:TPU:0, one launch (start us, length us, event | category | flops | bytes accessed | tf_op | source)
XLA Modules:
  0.0 443.4 jit_solution(12282438012124909884)
XLA Ops:
  7.2 1.4 constant_dynamic-update-slice_fusion.5
  8.6 3.4 reshape.160
  12.0 2.4 copy.46
  19.9 3.0 collective-permute-start.6
  22.8 1.5 collective-permute-start.4
  24.3 2.9 pad.15
  27.2 11.3 %collective-permute-done.6.refs_10_.refs_13_.refs_12_.refs_11_ = bf16[2688,128]{1,0:T(8,128)(2,1)} collective-permute-done((bf16[2688,128]{1,0:T(8,128)(2,1)}, bf16[2688,128]{1,0:T(8,128)(2,1)}, u32[]{:S(2)}, u32[]{:S(2)}) %collective-permute-start.6) | collective-permute-done | bytes 688160 | tf_op jit(solution)/shard_map/ppermute | solution.py:1127
  39.5 1.7 collective-permute-start.7
  41.2 3.0 dynamic-slice_bitcast_fusion.1
  44.5 12.0 %collective-permute-done.7.refs_8_.refs_9_ = bf16[2688,128]{1,0:T(8,128)(2,1)} collective-permute-done((bf16[2688,128]{1,0:T(8,128)(2,1)}, bf16[2688,128]{1,0:T(8,128)(2,1)}, u32[]{:S(2)}, u32[]{:S(2)}) %collective-permute-start.7) | collective-permute-done | bytes 688160 | tf_op jit(solution)/shard_map/ppermute | solution.py:1127
  56.4 2.6 bitcast_select_fusion
  59.0 2.5 collective-permute-start.10
  62.1 1.6 dynamic-slice_bitcast_fusion
  64.2 2.7 fusion.10
  66.9 3.6 collective-permute-start.1
  70.5 4.9 %collective-permute-done.10.refs_12_.refs_15_.refs_14_.refs_13_ = bf16[2688,128]{1,0:T(8,128)(2,1)S(1)} collective-permute-done((bf16[2688,128]{1,0:T(8,128)(2,1)}, bf16[2688,128]{1,0:T(8,128)(2,1)S(1)}, u32[]{:S(2)}, u32[]{:S(2)}) %collective-permute-start.10) | collective-permute-done | bytes 688160 | tf_op jit(solution)/shard_map/ppermute | solution.py:1127
  75.4 4.5 %collective-permute-start.2 = (bf16[2,256,512]{2,1,0:T(8,128)(2,1)S(1)}, bf16[2,256,512]{2,1,0:T(8,128)(2,1)S(1)}, u32[]{:S(2)}, u32[]{:S(2)}) collective-permute-start(bf16[2,256,512]{2,1,0:T(8,128)(2,1)S(1)} %get-tuple-element.107), channel_id=1, source_target_pairs={{0,4},{1,5},{2,6},{5,1},{6,2},{7,3},{8,12},{9,13},{10,14},{13,9},{... | collective-permute-start | bytes 1572872 | tf_op jit(solution)/shard_map/ppermute | solution.py:1173
  83.7 9.9 %collective-permute-done.2 = bf16[2,256,512]{2,1,0:T(8,128)(2,1)S(1)} collective-permute-done((bf16[2,256,512]{2,1,0:T(8,128)(2,1)S(1)}, bf16[2,256,512]{2,1,0:T(8,128)(2,1)S(1)}, u32[]{:S(2)}, u32[]{:S(2)}) %collective-permute-start.2) | collective-permute-done | bytes 524320 | tf_op jit(solution)/shard_map/ppermute | solution.py:1173
  93.6 10.5 %collective-permute-start.3 = (bf16[2,256,512]{2,1,0:T(8,128)(2,1)}, bf16[2,256,512]{2,1,0:T(8,128)(2,1)S(1)}, u32[]{:S(2)}, u32[]{:S(2)}) collective-permute-start(bf16[2,256,512]{2,1,0:T(8,128)(2,1)} %get-tuple-element.104), channel_id=1, source_target_pairs={{0,6},{2,4},{3,5},{4,2},{5,3},{7,1},{8,14},{10,12},{11,13},{12,10}... | collective-permute-start | bytes 1572872 | tf_op jit(solution)/shard_map/ppermute | solution.py:1173
  105.4 2.9 fusion.3
  108.2 2.9 collective-permute-done.3
  111.1 8.8 %collective-permute-start.21 = (bf16[2,256,512]{2,1,0:T(8,128)(2,1)}, bf16[2,256,512]{2,1,0:T(8,128)(2,1)}, u32[]{:S(2)}, u32[]{:S(2)}) collective-permute-start(bf16[2,256,512]{2,1,0:T(8,128)(2,1)} %get-tuple-element.90), channel_id=1, source_target_pairs={{0,2},{1,3},{3,1},{4,6},{6,4},{7,5},{8,10},{9,11},{11,9},{12,14},{... | collective-permute-start | bytes 1572872 | tf_op jit(solution)/shard_map/ppermute | solution.py:1173
  119.9 3.0 collective-permute-start.22
  123.8 3.9 collective-permute-start.23
  127.7 22.4 %forward_0_1.1 = (bf16[2048,512]{1,0:T(8,128)(2,1)}, bf16[1,2048,192]{2,1,0:T(8,128)(2,1)}, bf16[1,1152,384]{2,1,0:T(8,128)(2,1)}, bf16[1,2048,512]{2,1,0:T(8,12...) custom-call(s32[2]{0:T(128)} %pad_add_fusion.refs_0_, ...), custom_call_target="tpu_custom_call" | custom-call | flops 5200000000 | bytes 10000000 | tf_op jit(solution)/shard_map/forward_0_1/pallas_call | solution.py:822
  150.2 54.9 %forward_1_4.1 = (bf16[3,2048,192]{2,1,0:T(8,128)(2,1)}, bf16[3,1152,384]{2,1,0:T(8,128)(2,1)}, bf16[3,2048,512]{2,1,0:T(8,128)(2,1)}, f32[3,1,1088]{2,1,0:T(1,1...) custom-call(s32[2]{0:T(128)} %pad_add_fusion.refs_0_, ...), custom_call_target="tpu_custom_call", output_to_operand_aliasing={{4}: (21, {}), {5}: (22, {}), {6}: (23, {}), {7}: (24, {})} | custom-call | flops 15600000000 | bytes 30000000 | tf_op jit(solution)/shard_map/forward_1_4/pallas_call | solution.py:822
  205.1 2.7 fusion.31
  209.1 1.3 collective-permute-start.17
  210.5 1.5 collective-permute-start.16
  211.9 62.9 %backward_1_4.1 = (bf16[512,512]{1,0:T(8,128)(2,1)}, bf16[512,512]{1,0:T(8,128)(2,1)}, bf16[512,512]{1,0:T(8,128)(2,1)}, bf16[512,512]{1,0:T(8,128)(2,1)}, bf16[...) custom-call(s32[2]{0:T(128)} %pad_add_fusion.refs_0_, ...), custom_call_target="tpu_custom_call", output_to_operand_aliasing={{0}: (1, {}), {1}: (2, {}), {2}: (3, {}), {3}: (4, {}), {6}... | custom-call | flops 21600000000 | bytes 30000000 | tf_op jit(solution)/shard_map/backward_1_4/pallas_call | solution.py:1112
  274.9 34.9 %backward_0_1.1 = (f32[1,2,1088]{2,1,0:T(2,128)}, bf16[2048,512]{1,0:T(8,128)(2,1)}, bf16[4,2688,128]{2,1,0:T(8,128)(2,1)}) custom-call(s32[2]{0:T(128)} %pad_add_fusion.refs_0_, bf16[512,512]{1,0:T(8,128)(2,1)} %get-tuple-element.50.refs_1_, bf16[512,512]{1,0:T(8,128)(2,1)} %get-tuple-element.51.refs_2_, ...), custom_call_target="tpu_custom_call", output_to_operand_aliasing={{1}: (21, {}), {2}: (6, {})} | custom-call | flops 7200000000 | bytes 10000000 | tf_op jit(solution)/shard_map/backward_0_1/pallas_call | solution.py:1112
  309.7 2.5 fusion.30
  313.6 1.3 collective-permute-start.25
  314.9 1.3 collective-permute-start.24
  316.2 1.6 pad_maximum_fusion
  318.3 1.5 slice_bitcast_fusion.3
  319.8 8.0 %collective-permute-start.19 = (bf16[4,256,512]{2,1,0:T(8,128)(2,1)}, bf16[4,256,512]{2,1,0:T(8,128)(2,1)}, u32[]{:S(2)}, u32[]{:S(2)}) collective-permute-start(bf16[4,256,512]{2,1,0:T(8,128)(2,1)} %get-tuple-element.95), channel_id=1, source_target_pairs={{0,1},{1,0},{2,3},{3,2},{4,5},{5,4},{6,7},{7,6},{8,9},{9,8},{10,11... | collective-permute-start | bytes 3145736 | tf_op jit(solution)/shard_map/ppermute | solution.py:1162
  327.8 49.7 %collective-permute-done.25 = bf16[2,256,512]{2,1,0:T(8,128)(2,1)} collective-permute-done((bf16[2,256,512]{2,1,0:T(8,128)(2,1)S(1)}, bf16[2,256,512]{2,1,0:T(8,128)(2,1)}, u32[]{:S(2)}, u32[]{:S(2)}) %collective-permute-start.25) | collective-permute-done | bytes 524320 | tf_op jit(solution)/shard_map/ppermute | solution.py:1183
  377.5 1.3 pad_maximum_fusion.2
  379.3 1.6 slice_bitcast_fusion.1
  380.9 15.1 %psum.15 = f32[2,1088]{1,0:T(2,128)S(1)} all-reduce(f32[2,1088]{1,0:T(2,128)S(1)} %fusion.29), channel_id=1, replica_groups=mesh['pipe'=4,'dp'=8] {'dp'}, use_global_device_ids=true, to_apply=%region_2.3 | all-reduce | flops 2176 | bytes 17408 | tf_op jit(solution)/shard_map/psum | solution.py:1219
  396.6 18.0 %all-reduce.6.cloned.1.call-done = bf16[4,2688,128]{2,1,0:T(8,128)(2,1)} async-done(((bf16[4,2688,128]{2,1,0:T(8,128)(2,1)}), bf16[4,2688,128]{2,1,0:T(8,128)(2,1)}) %all-reduce.6.cloned.1.call-update) | async-done | bytes 2752528 | tf_op jit(solution)/shard_map/psum | solution.py:1218
  416.0 2.6 copy.71
  418.6 4.5 %reshape_reshape.9 = f32[1,3,3,128,384]{4,3,2,1,0:T(8,128)} reshape(f32[4,288,3,128]{3,2,1,0:T(4,128)} %bitcast.123) | data formatting | bytes 3538944 | tf_op jit(solution)/shard_map/reshape;reshape | solution.py:1225
  427.0 1.6 slice.108
  428.6 1.8 maximum_select_fusion
  432.2 1.9 maximum_select_fusion.1
  434.1 2.1 convert.2
  (129 shorter events, 24.5 us)
Async XLA Ops:
  7.2 407.5 %all-reduce.6.cloned.1.call-start = ((), (), s32[]{:S(2)}) async-start(), calls=%async_computation | async-start | bytes 5505024 | tf_op jit(solution)/shard_map/psum | solution.py:1218
  8.6 5.8 %copy-start.11 = (bf16[1,384,192]{1,2,0:T(8,128)(2,1)S(1)}, bf16[1,384,192]{1,2,0:T(8,128)(2,1)}, u32[]{:S(2)}) copy-start(bf16[1,384,192]{1,2,0:T(8,128)(2,1)} %param.17) | copy-start | bytes 442372
  12.0 3.3 copy-start.9
  14.4 2.8 copy-start.14
  14.4 2.8 copy-start.15
  15.5 3.1 copy-start.5
  18.8 61.1 %copy-start = (bf16[4,2688,128]{2,1,0:T(8,128)(2,1)}, bf16[4,2688,128]{2,1,0:T(8,128)(2,1)S(1)}, u32[]{:S(2)}) copy-start(bf16[4,2688,128]{2,1,0:T(8,128)(2,1)S(1)} %constant_dynamic-update-slice_fusion.refs_5_.refs_6_) | copy-start | bytes 8257540
  19.9 18.7 %collective-permute-start.6 = (bf16[2688,128]{1,0:T(8,128)(2,1)}, bf16[2688,128]{1,0:T(8,128)(2,1)}, u32[]{:S(2)}, u32[]{:S(2)}) collective-permute-start(bf16[2688,128]{1,0:T(8,128)(2,1)} %get-tuple-element.74), channel_id=1, source_target_pairs={{0,16},{8,24},{16,0},{24,8},{1,17},{9,25},{17,1},{25,9},{2,18},{10... | collective-permute-start | bytes 2064392 | tf_op jit(solution)/shard_map/ppermute | solution.py:1127
  22.8 21.6 %collective-permute-start.4 = (bf16[2688,128]{1,0:T(8,128)(2,1)S(1)}, bf16[2688,128]{1,0:T(8,128)(2,1)}, u32[]{:S(2)}, u32[]{:S(2)}) collective-permute-start(bf16[2688,128]{1,0:T(8,128)(2,1)S(1)} %get-tuple-element.75), channel_id=1, source_target_pairs={{0,8},{8,0},{16,24},{24,16},{1,9},{9,1},{17,25},{25,17},{2,10},{10... | collective-permute-start | bytes 2064392 | tf_op jit(solution)/shard_map/ppermute | solution.py:1127
  39.5 16.9 %collective-permute-start.7 = (bf16[2688,128]{1,0:T(8,128)(2,1)}, bf16[2688,128]{1,0:T(8,128)(2,1)}, u32[]{:S(2)}, u32[]{:S(2)}) collective-permute-start(bf16[2688,128]{1,0:T(8,128)(2,1)} %bitcast_select_fusion.3), channel_id=1, source_target_pairs={{0,8},{8,0},{16,24},{24,16},{1,9},{9,1},{17,25},{25,17},{2,10},{10... | collective-permute-start | bytes 2064392 | tf_op jit(solution)/shard_map/ppermute | solution.py:1127
  41.2 3.0 copy-start.10
  44.2 20.0 %collective-permute-start = (bf16[4,256,512]{2,1,0:T(8,128)(2,1)}, bf16[4,256,512]{2,1,0:T(8,128)(2,1)}, u32[]{:S(2)}, u32[]{:S(2)}) collective-permute-start(bf16[4,256,512]{2,1,0:T(8,128)(2,1)} %get-tuple-element.108), channel_id=1, source_target_pairs={{0,1},{1,0},{2,3},{3,2},{4,5},{5,4},{6,7},{7,6},{8,9},{9,8},{10,11... | collective-permute-start | bytes 3145736 | tf_op jit(solution)/shard_map/ppermute | solution.py:1162
  44.4 17.2 %copy-start.4 = (bf16[6,1,16,16,512]{4,3,2,1,0:T(8,128)(2,1)S(1)}, bf16[6,1,16,16,512]{4,3,2,1,0:T(8,128)(2,1)}, u32[]{:S(2)}) copy-start(bf16[6,1,16,16,512]{4,3,2,1,0:T(8,128)(2,1)} %param.22) | copy-start | bytes 4718596
  59.0 16.4 %collective-permute-start.10 = (bf16[2688,128]{1,0:T(8,128)(2,1)}, bf16[2688,128]{1,0:T(8,128)(2,1)S(1)}, u32[]{:S(2)}, u32[]{:S(2)}) collective-permute-start(bf16[2688,128]{1,0:T(8,128)(2,1)} %get-tuple-element.77), channel_id=1, source_target_pairs={{0,16},{8,24},{16,0},{24,8},{1,17},{9,25},{17,1},{25,9},{2,18},{10... | collective-permute-start | bytes 2064392 | tf_op jit(solution)/shard_map/ppermute | solution.py:1127
  63.7 17.4 %collective-permute-start.20 = (bf16[4,256,512]{2,1,0:T(8,128)(2,1)}, bf16[4,256,512]{2,1,0:T(8,128)(2,1)}, u32[]{:S(2)}, u32[]{:S(2)}) collective-permute-start(bf16[4,256,512]{2,1,0:T(8,128)(2,1)} %get-tuple-element.92), channel_id=1, source_target_pairs={{0,1},{1,0},{2,3},{3,2},{4,5},{5,4},{6,7},{7,6},{8,9},{9,8},{10,11... | collective-permute-start | bytes 3145736 | tf_op jit(solution)/shard_map/ppermute | solution.py:1162
  63.7 18.2 %collective-permute-start.5 = (bf16[2688,128]{1,0:T(8,128)(2,1)}, bf16[2688,128]{1,0:T(8,128)(2,1)S(1)}, u32[]{:S(2)}, u32[]{:S(2)}) collective-permute-start(bf16[2688,128]{1,0:T(8,128)(2,1)} %collective-permute-done.4.refs_6_.refs_7_), channel_id=1, source_target_pairs={{0,1},{1,0},{2,3},{3,2},{4,5},{5,4},{6,7},{7,6},{8,9},{9,8},{10,11... | collective-permute-start | bytes 2064392 | tf_op jit(solution)/shard_map/ppermute | solution.py:1130
  64.2 18.9 %collective-permute-start.9 = (bf16[2688,128]{1,0:T(8,128)(2,1)}, bf16[2688,128]{1,0:T(8,128)(2,1)S(1)}, u32[]{:S(2)}, u32[]{:S(2)}) collective-permute-start(bf16[2688,128]{1,0:T(8,128)(2,1)} %collective-permute-done.6.refs_10_.refs_13_.refs_12_.refs_11_), channel_id=1, source_target_pairs={{0,1},{1,0},{2,3},{3,2},{4,5},{5,4},{6,7},{7,6},{8,9},{9,8},{10,11... | collective-permute-start | bytes 2064392 | tf_op jit(solution)/shard_map/ppermute | solution.py:1130
  66.9 14.2 %copy-start.6 = (bf16[2688,128]{1,0:T(8,128)(2,1)S(1)}, bf16[2688,128]{1,0:T(8,128)(2,1)}, u32[]{:S(2)}) copy-start(bf16[2688,128]{1,0:T(8,128)(2,1)} %get-tuple-element.76) | copy-start | bytes 2064388
  66.9 16.3 %collective-permute-start.1 = (bf16[2,256,512]{2,1,0:T(8,128)(2,1)S(1)}, bf16[2,256,512]{2,1,0:T(8,128)(2,1)S(1)}, u32[]{:S(2)}, u32[]{:S(2)}) collective-permute-start(bf16[2,256,512]{2,1,0:T(8,128)(2,1)S(1)} %get-tuple-element.106), channel_id=1, source_target_pairs={{0,2},{1,3},{3,1},{4,6},{6,4},{7,5},{8,10},{9,11},{11,9},{12,14},{... | collective-permute-start | bytes 1572872 | tf_op jit(solution)/shard_map/ppermute | solution.py:1173
  75.4 32.9 %copy-start.7 = (bf16[2688,128]{1,0:T(8,128)(2,1)}, bf16[2688,128]{1,0:T(8,128)(2,1)S(1)}, u32[]{:S(2)}) copy-start(bf16[2688,128]{1,0:T(8,128)(2,1)S(1)} %collective-permute-done.10.refs_12_.refs_15_.refs_14_.refs_13_) | copy-start | bytes 2064388
  75.4 18.2 %collective-permute-start.2 = (bf16[2,256,512]{2,1,0:T(8,128)(2,1)S(1)}, bf16[2,256,512]{2,1,0:T(8,128)(2,1)S(1)}, u32[]{:S(2)}, u32[]{:S(2)}) collective-permute-start(bf16[2,256,512]{2,1,0:T(8,128)(2,1)S(1)} %get-tuple-element.107), channel_id=1, source_target_pairs={{0,4},{1,5},{2,6},{5,1},{6,2},{7,3},{8,12},{9,13},{10,14},{13,9},{... | collective-permute-start | bytes 1572872 | tf_op jit(solution)/shard_map/ppermute | solution.py:1173
  81.1 23.0 %collective-permute-start.14 = (bf16[2688,128]{1,0:T(8,128)(2,1)S(1)}, bf16[2688,128]{1,0:T(8,128)(2,1)}, u32[]{:S(2)}, u32[]{:S(2)}) collective-permute-start(bf16[2688,128]{1,0:T(8,128)(2,1)S(1)} %copy-done.6), channel_id=1, source_target_pairs={{0,16},{8,24},{16,0},{24,8},{1,17},{9,25},{17,1},{25,9},{2,18},{10... | collective-permute-start | bytes 2064392 | tf_op jit(solution)/shard_map/ppermute | solution.py:1127
  81.8 22.4 %copy-start.16 = (bf16[2688,128]{1,0:T(8,128)(2,1)}, bf16[2688,128]{1,0:T(8,128)(2,1)S(1)}, u32[]{:S(2)}) copy-start(bf16[2688,128]{1,0:T(8,128)(2,1)S(1)} %collective-permute-done.5.refs_7_.refs_8_) | copy-start | bytes 2064388
  81.9 22.3 %collective-permute-start.12 = (bf16[2688,128]{1,0:T(8,128)(2,1)S(1)}, bf16[2688,128]{1,0:T(8,128)(2,1)}, u32[]{:S(2)}, u32[]{:S(2)}) collective-permute-start(bf16[2688,128]{1,0:T(8,128)(2,1)S(1)} %fusion.1), channel_id=1, source_target_pairs={{0,8},{8,0},{16,24},{24,16},{1,9},{9,1},{17,25},{25,17},{2,10},{10... | collective-permute-start | bytes 2064392 | tf_op jit(solution)/shard_map/ppermute | solution.py:1127
  83.1 21.6 %copy-start.17 = (bf16[2688,128]{1,0:T(8,128)(2,1)}, bf16[2688,128]{1,0:T(8,128)(2,1)S(1)}, u32[]{:S(2)}) copy-start(bf16[2688,128]{1,0:T(8,128)(2,1)S(1)} %collective-permute-done.9.refs_11_.refs_14_.refs_13_.refs_12_) | copy-start | bytes 2064388
  83.1 36.8 %collective-permute-start.8 = (bf16[2688,128]{1,0:T(8,128)(2,1)}, bf16[2688,128]{1,0:T(8,128)(2,1)S(1)}, u32[]{:S(2)}, u32[]{:S(2)}) collective-permute-start(bf16[2688,128]{1,0:T(8,128)(2,1)} %collective-permute-done.7.refs_8_.refs_9_), channel_id=1, source_target_pairs={{0,1},{1,0},{2,3},{3,2},{4,5},{5,4},{6,7},{7,6},{8,9},{9,8},{10,11... | collective-permute-start | bytes 2064392 | tf_op jit(solution)/shard_map/ppermute | solution.py:1130
  83.2 21.5 %copy-start.20 = (bf16[2,256,512]{2,1,0:T(8,128)(2,1)}, bf16[2,256,512]{2,1,0:T(8,128)(2,1)S(1)}, u32[]{:S(2)}) copy-start(bf16[2,256,512]{2,1,0:T(8,128)(2,1)S(1)} %collective-permute-done.1) | copy-start | bytes 1572868
  83.2 39.8 %collective-permute-start.11 = (bf16[2688,128]{1,0:T(8,128)(2,1)S(1)}, bf16[2688,128]{1,0:T(8,128)(2,1)S(1)}, u32[]{:S(2)}, u32[]{:S(2)}) collective-permute-start(bf16[2688,128]{1,0:T(8,128)(2,1)S(1)} %collective-permute-done.10.refs_12_.refs_15_.refs_14_.refs_13_), channel_id=1, source_target_pairs={{0,1},{1,0},{2,3},{3,2},{4,5},{5,4},{6,7},{7,6},{8,9},{9,8},{10,11... | collective-permute-start | bytes 2064392 | tf_op jit(solution)/shard_map/ppermute | solution.py:1130
  93.6 11.1 %copy-start.21 = (bf16[2,256,512]{2,1,0:T(8,128)(2,1)}, bf16[2,256,512]{2,1,0:T(8,128)(2,1)S(1)}, u32[]{:S(2)}) copy-start(bf16[2,256,512]{2,1,0:T(8,128)(2,1)S(1)} %collective-permute-done.2) | copy-start | bytes 1572868
  93.6 17.5 %collective-permute-start.3 = (bf16[2,256,512]{2,1,0:T(8,128)(2,1)}, bf16[2,256,512]{2,1,0:T(8,128)(2,1)S(1)}, u32[]{:S(2)}, u32[]{:S(2)}) collective-permute-start(bf16[2,256,512]{2,1,0:T(8,128)(2,1)} %get-tuple-element.104), channel_id=1, source_target_pairs={{0,6},{2,4},{3,5},{4,2},{5,3},{7,1},{8,14},{10,12},{11,13},{12,10}... | collective-permute-start | bytes 1572872 | tf_op jit(solution)/shard_map/ppermute | solution.py:1173
  104.1 46.0 %collective-permute-start.15 = (bf16[2688,128]{1,0:T(8,128)(2,1)}, bf16[2688,128]{1,0:T(8,128)(2,1)}, u32[]{:S(2)}, u32[]{:S(2)}) collective-permute-start(bf16[2688,128]{1,0:T(8,128)(2,1)} %collective-permute-done.14.refs_17_.refs_16_), channel_id=1, source_target_pairs={{0,1},{1,0},{2,3},{3,2},{4,5},{5,4},{6,7},{7,6},{8,9},{9,8},{10,11... | collective-permute-start | bytes 2064392 | tf_op jit(solution)/shard_map/ppermute | solution.py:1130
  104.2 45.9 %collective-permute-start.13 = (bf16[2688,128]{1,0:T(8,128)(2,1)}, bf16[2688,128]{1,0:T(8,128)(2,1)}, u32[]{:S(2)}, u32[]{:S(2)}) collective-permute-start(bf16[2688,128]{1,0:T(8,128)(2,1)} %collective-permute-done.12.refs_11_.refs_10_), channel_id=1, source_target_pairs={{0,1},{1,0},{2,3},{3,2},{4,5},{5,4},{6,7},{7,6},{8,9},{9,8},{10,11... | collective-permute-start | bytes 2064392 | tf_op jit(solution)/shard_map/ppermute | solution.py:1130
  111.1 16.6 %copy-start.22 = (bf16[2,256,512]{2,1,0:T(8,128)(2,1)}, bf16[2,256,512]{2,1,0:T(8,128)(2,1)S(1)}, u32[]{:S(2)}) copy-start(bf16[2,256,512]{2,1,0:T(8,128)(2,1)S(1)} %collective-permute-done.3) | copy-start | bytes 1572868
  111.1 99.3 %collective-permute-start.21 = (bf16[2,256,512]{2,1,0:T(8,128)(2,1)}, bf16[2,256,512]{2,1,0:T(8,128)(2,1)}, u32[]{:S(2)}, u32[]{:S(2)}) collective-permute-start(bf16[2,256,512]{2,1,0:T(8,128)(2,1)} %get-tuple-element.90), channel_id=1, source_target_pairs={{0,2},{1,3},{3,1},{4,6},{6,4},{7,5},{8,10},{9,11},{11,9},{12,14},{... | collective-permute-start | bytes 1572872 | tf_op jit(solution)/shard_map/ppermute | solution.py:1173
  119.9 3.0 copy-start.18
  119.9 92.0 %collective-permute-start.22 = (bf16[2,256,512]{2,1,0:T(8,128)(2,1)}, bf16[2,256,512]{2,1,0:T(8,128)(2,1)}, u32[]{:S(2)}, u32[]{:S(2)}) collective-permute-start(bf16[2,256,512]{2,1,0:T(8,128)(2,1)} %get-tuple-element.91), channel_id=1, source_target_pairs={{0,4},{1,5},{2,6},{5,1},{6,2},{7,3},{8,12},{9,13},{10,14},{13,9},{... | collective-permute-start | bytes 1572872 | tf_op jit(solution)/shard_map/ppermute | solution.py:1173
  123.8 88.1 %collective-permute-start.23 = (bf16[2,256,512]{2,1,0:T(8,128)(2,1)}, bf16[2,256,512]{2,1,0:T(8,128)(2,1)}, u32[]{:S(2)}, u32[]{:S(2)}) collective-permute-start(bf16[2,256,512]{2,1,0:T(8,128)(2,1)} %get-tuple-element.88), channel_id=1, source_target_pairs={{0,6},{2,4},{3,5},{4,2},{5,3},{7,1},{8,14},{10,12},{11,13},{12,10}... | collective-permute-start | bytes 1572872 | tf_op jit(solution)/shard_map/ppermute | solution.py:1173
  207.9 107.0 %collective-permute-start.18 = (bf16[2,256,512]{2,1,0:T(8,128)(2,1)}, bf16[2,256,512]{2,1,0:T(8,128)(2,1)}, u32[]{:S(2)}, u32[]{:S(2)}) collective-permute-start(bf16[2,256,512]{2,1,0:T(8,128)(2,1)} %bitcast.33), channel_id=1, source_target_pairs={{1,7},{2,4},{3,5},{4,2},{5,3},{6,0},{9,15},{10,12},{11,13},{12,10}... | collective-permute-start | bytes 1572872 | tf_op jit(solution)/shard_map/ppermute | solution.py:1183
  209.1 107.0 %collective-permute-start.17 = (bf16[2,256,512]{2,1,0:T(8,128)(2,1)}, bf16[2,256,512]{2,1,0:T(8,128)(2,1)}, u32[]{:S(2)}, u32[]{:S(2)}) collective-permute-start(bf16[2,256,512]{2,1,0:T(8,128)(2,1)} %bitcast.31), channel_id=1, source_target_pairs={{1,5},{2,6},{3,7},{4,0},{5,1},{6,2},{9,13},{10,14},{11,15},{12,8},... | collective-permute-start | bytes 1572872 | tf_op jit(solution)/shard_map/ppermute | solution.py:1183
  210.5 105.7 %collective-permute-start.16 = (bf16[2,256,512]{2,1,0:T(8,128)(2,1)}, bf16[2,256,512]{2,1,0:T(8,128)(2,1)}, u32[]{:S(2)}, u32[]{:S(2)}) collective-permute-start(bf16[2,256,512]{2,1,0:T(8,128)(2,1)} %bitcast.29), channel_id=1, source_target_pairs={{1,3},{2,0},{3,1},{4,6},{5,7},{6,4},{9,11},{10,8},{11,9},{12,14},{... | collective-permute-start | bytes 1572872 | tf_op jit(solution)/shard_map/ppermute | solution.py:1183
  312.3 15.6 %collective-permute-start.26 = (bf16[2,256,512]{2,1,0:T(8,128)(2,1)}, bf16[2,256,512]{2,1,0:T(8,128)(2,1)S(1)}, u32[]{:S(2)}, u32[]{:S(2)}) collective-permute-start(bf16[2,256,512]{2,1,0:T(8,128)(2,1)} %bitcast.58), channel_id=1, source_target_pairs={{1,7},{2,4},{3,5},{4,2},{5,3},{6,0},{9,15},{10,12},{11,13},{12,10}... | collective-permute-start | bytes 1572872 | tf_op jit(solution)/shard_map/ppermute | solution.py:1183
  313.6 64.0 %collective-permute-start.25 = (bf16[2,256,512]{2,1,0:T(8,128)(2,1)S(1)}, bf16[2,256,512]{2,1,0:T(8,128)(2,1)}, u32[]{:S(2)}, u32[]{:S(2)}) collective-permute-start(bf16[2,256,512]{2,1,0:T(8,128)(2,1)S(1)} %bitcast.157), channel_id=1, source_target_pairs={{1,5},{2,6},{3,7},{4,0},{5,1},{6,2},{9,13},{10,14},{11,15},{12,8},... | collective-permute-start | bytes 1572872 | tf_op jit(solution)/shard_map/ppermute | solution.py:1183
  314.9 62.6 %collective-permute-start.24 = (bf16[2,256,512]{2,1,0:T(8,128)(2,1)S(1)}, bf16[2,256,512]{2,1,0:T(8,128)(2,1)S(1)}, u32[]{:S(2)}, u32[]{:S(2)}) collective-permute-start(bf16[2,256,512]{2,1,0:T(8,128)(2,1)S(1)} %bitcast.155), channel_id=1, source_target_pairs={{1,3},{2,0},{3,1},{4,6},{5,7},{6,4},{9,11},{10,8},{11,9},{12,14},{... | collective-permute-start | bytes 1572872 | tf_op jit(solution)/shard_map/ppermute | solution.py:1183
  319.8 108.8 %collective-permute-start.19 = (bf16[4,256,512]{2,1,0:T(8,128)(2,1)}, bf16[4,256,512]{2,1,0:T(8,128)(2,1)}, u32[]{:S(2)}, u32[]{:S(2)}) collective-permute-start(bf16[4,256,512]{2,1,0:T(8,128)(2,1)} %get-tuple-element.95), channel_id=1, source_target_pairs={{0,1},{1,0},{2,3},{3,2},{4,5},{5,4},{6,7},{7,6},{8,9},{9,8},{10,11... | collective-permute-start | bytes 3145736 | tf_op jit(solution)/shard_map/ppermute | solution.py:1162
  379.3 1.6 copy-start.12
  380.9 50.8 %collective-permute-start.27 = (bf16[4,256,512]{2,1,0:T(8,128)(2,1)}, bf16[4,256,512]{2,1,0:T(8,128)(2,1)}, u32[]{:S(2)}, u32[]{:S(2)}) collective-permute-start(bf16[4,256,512]{2,1,0:T(8,128)(2,1)} %get-tuple-element.79), channel_id=1, source_target_pairs={{0,1},{1,0},{2,3},{3,2},{4,5},{5,4},{6,7},{7,6},{8,9},{9,8},{10,11... | collective-permute-start | bytes 3145736 | tf_op jit(solution)/shard_map/ppermute | solution.py:1162
  418.6 4.5 %copy-start.1 = (bf16[4,2688,128]{2,1,0:T(8,128)(2,1)S(1)}, bf16[4,2688,128]{2,1,0:T(8,128)(2,1)}, u32[]{:S(2)}) copy-start(bf16[4,2688,128]{2,1,0:T(8,128)(2,1)} %all-reduce.6.cloned.1.call-done) | copy-start | bytes 8257540
  430.5 1.7 copy-start.3
  (4 other events, 5.6 us)
Sparse Core Ops, SparseCore 0:
  315.0 99.6 all-reduce.5

commit v2 on v0

--- a/solution.py
+++ b/solution.py
@@ -1,14 +1,23 @@
+import functools
 import math
 
 import jax
 import jax.numpy as jnp
+import numpy as np
 from jax import lax
+from jax.experimental import pallas as pl
+from jax.experimental.pallas import tpu as pltpu
 from jax.sharding import PartitionSpec as P
 
 CL = 128
 CG = 384
 CS = 192
+CH = 512
 NORMS = 1088
+F32 = jnp.float32
+BF = jnp.bfloat16
+IM = 4
+UN = 2
 
 
 EPS = 1e-05
@@ -239,7 +248,7 @@
     )
 
 
-def on_device(
+def general_device(
     images_in,
     conv_local,
     conv_cross,
@@ -372,6 +381,1160 @@
     )
 
 
+PARTS = 4
+ANY = pl.BlockSpec(memory_space=pl.ANY)
+VMEM = pl.BlockSpec(memory_space=pltpu.VMEM)
+SMEM = pl.BlockSpec(memory_space=pltpu.SMEM)
+VMEM_LIMIT = 63 * 2**20
+
+
+def dft_np(side):
+    spatial = np.arange(side)
+    spectral = np.arange(side // 2 + 1)
+    turns = spatial[:, None, None, None] * spatial[None, None, :, None] + spectral[None, :, None, None] * spatial[None, None, None, :]
+    angle = (turns % side).reshape(side * spectral.size, side * side) * (2.0 * np.pi / side)
+    fold = np.broadcast_to(np.where((spectral == 0) | (2 * spectral == side), 1.0, 2.0), (side, spectral.size)).reshape(-1, 1)
+    forward = np.concatenate([np.cos(angle), -np.sin(angle)]) / side
+    inverse = np.concatenate([np.cos(angle) * fold, -np.sin(angle) * fold]).T / side
+    return forward, inverse
+
+
+def dot(a, b):
+    return lax.dot_general(a, b, (((1,), (0,)), ((), ())), preferred_element_type=F32)
+
+
+def dot_nt(a, b):
+    return lax.dot_general(a, b, (((1,), (1,)), ((), ())), preferred_element_type=F32)
+
+
+def dot_tn(a, b):
+    return lax.dot_general(a, b, (((0,), (0,)), ((), ())), preferred_element_type=F32)
+
+
+def silu_of_half(h):
+    return h + h * jnp.tanh(h)
+
+
+def twice_slope(h):
+    t = jnp.tanh(h)
+    return (1.0 + t) * (1.0 + h * (1.0 - t))
+
+
+QUARTERS, QROWS = 4, 2640
+LAYOUT = {
+    "local": (0, 1152, 1),
+    "cross": (1152, 288, 3),
+    "reduce": (2016, 48, 3),
+    "spectral": (2160, 96, 3),
+    "expand": (2448, 48, 3),
+    "norms": (2592, 16, 3),
+}
+
+
+def pieces(name, start, count, block=0):
+    base, rows, _ = LAYOUT[name]
+    found = []
+    while count:
+        quarter, offset = divmod(start, rows)
+        take = min(count, rows - offset)
+        found.append((quarter, base + block * rows + offset, take))
+        start, count = start + take, count - take
+    return found
+
+
+def stack_rows(parts):
+    return parts[0] if len(parts) == 1 else jnp.concatenate(parts, axis=0)
+
+
+def stack_cols(parts):
+    return parts[0] if len(parts) == 1 else jnp.concatenate(parts, axis=1)
+
+
+def read(w, name, start, count):
+    blocks = LAYOUT[name][2]
+    return stack_cols([stack_rows([w[q, r : r + n] for q, r, n in pieces(name, start, count, j)]) for j in range(blocks)])
+
+
+def write(w, name, start, value):
+    for j in range(LAYOUT[name][2]):
+        done = 0
+        for q, r, n in pieces(name, start, value.shape[0], j):
+            w[q, r : r + n] = value[done : done + n, j * 128 : (j + 1) * 128].astype(w.dtype)
+            done += n
+
+
+def norm_rows(w):
+    base = LAYOUT["norms"][0]
+    return stack_cols([w[j // 3, base + 16 * (j % 3) : base + 16 * (j % 3) + 16] for j in range(9)]).astype(F32)[:, :NORMS]
+
+
+def read_norms(w):
+    rows = norm_rows(w)
+    return rows[0:1] + rows[1:2], rows[2:3] + rows[3:4]
+
+
+def norm_block(vectors):
+    rows = stack_rows([*vectors, jnp.zeros((16 - len(vectors), NORMS), F32)])
+    return stack_cols([rows, jnp.zeros((16, 12 * 128 - NORMS), F32)]).astype(BF)
+
+
+def write_norms(w, vectors):
+    base = LAYOUT["norms"][0]
+    rows = norm_block(vectors)
+    for j in range(12):
+        w[j // 3, base + 16 * (j % 3) : base + 16 * (j % 3) + 16] = rows[:, j * 128 : (j + 1) * 128]
+
+
+TERMS = {
+    "local": (0, 9 * CH, 1),
+    "cross": (9 * CH, 9 * CL, 3),
+    "reduce": (9 * (CH + CG), CS, 3),
+    "spectral": (9 * (CH + CG) + 3 * CS, CG, 3),
+    "expand": (9 * (CH + CG) + 3 * (CS + CG), CS, 3),
+    "norms": (9 * (CH + CG) + 3 * (2 * CS + CG), 16, 12),
+}
+
+
+def put_terms(w, name, start, value):
+    base, rows, blocks = TERMS[name]
+    count = value.shape[0]
+    for j in range(blocks):
+        first = base + j * rows + start
+        w[pl.ds(first if isinstance(first, int) else pl.multiple_of(first, 128), count)] = value[:, j * 128 : (j + 1) * 128].astype(BF)
+
+
+def put_norm_terms(w, vectors):
+    base = TERMS["norms"][0]
+    rows = norm_block(vectors)
+    for j in range(12):
+        w[base + 16 * j : base + 16 * (j + 1)] = rows[:, j * 128 : (j + 1) * 128]
+
+
+def get_terms(w, name, columns):
+    base, rows, blocks = TERMS[name]
+    return stack_cols([w[base + j * rows : base + (j + 1) * rows] for j in range(blocks)]).astype(F32)[:, :columns]
+
+
+def conv_matrix(w):
+    return stack_rows([stack_cols([read(w, "local", k * CH, CL), read(w, "cross", k * CL, CL)]) for k in range(9)])
+
+
+def global_matrix(w):
+    return stack_cols([read(w, "local", k * CH + CL, CG) for k in range(9)])
+
+
+def global_by_row(w):
+    return stack_rows([stack_cols([read(w, "local", (dh * 3 + dw) * CH + CL, CG) for dw in range(3)]) for dh in range(3)])
+
+
+def conv_by_column(w):
+    return stack_rows(
+        [
+            stack_cols([part for k in (dw, 3 + dw, 6 + dw) for part in (read(w, "local", k * CH, CL), read(w, "cross", k * CL, CL))])
+            for dw in range(3)
+        ]
+    )
+
+
+def pack_kernel(place, local, cross, reduce_w, spectral, expand, gains, biases, own, send, packed, sem):
+    packed_rows = lambda name, value: write(packed, name, 0, value)
+    packed_rows("local", local[...])
+    packed_rows("cross", cross[...])
+    packed_rows("reduce", reduce_w[...])
+    packed_rows("spectral", spectral[...])
+    packed_rows("expand", expand[...])
+    halves = []
+    for values in (gains[...], biases[...]):
+        high = values.astype(BF)
+        halves += [high.astype(F32), values - high.astype(F32)]
+    write_norms(packed, halves)
+    core = place[1]
+    copies = [pltpu.make_async_copy(packed.at[2 * half + core], send.at[half], sem.at[half]) for half in range(2)]
+    copies += [pltpu.make_async_copy(packed.at[q], own.at[pl.ds(q * QROWS, QROWS)], sem.at[2 + q]) for q in range(QUARTERS)]
+    for c in copies:
+        c.start()
+    for c in copies:
+        c.wait()
+
+
+def pack_call(place, *weights):
+    shape = jax.ShapeDtypeStruct
+    return pl.pallas_call(
+        pack_kernel,
+        out_shape=[shape((QUARTERS * QROWS, 128), BF), shape((2, QROWS, 128), BF)],
+        in_specs=[SMEM] + [VMEM] * 7,
+        out_specs=[ANY] * 2,
+        scratch_shapes=[pltpu.VMEM((QUARTERS, QROWS, 128), BF), pltpu.SemaphoreType.DMA((2 + QUARTERS,))],
+        name="pack_weights",
+        compiler_params=pltpu.CompilerParams(vmem_limit_bytes=VMEM_LIMIT),
+    )(place, *weights)
+
+
+def relay_kernel(skip, *refs):
+    y1, x1 = refs[:2]
+    over_x, over_y, stage, sem_in, sem_out = refs[2 + skip :]
+    loads = [pltpu.make_async_copy(y1.at[0], stage.at[0], sem_in.at[0]), pltpu.make_async_copy(x1.at[1], stage.at[1], sem_in.at[1])]
+    stores = [pltpu.make_async_copy(stage.at[i], ref.at[0], sem_out.at[i]) for i, ref in enumerate((over_x, over_y))]
+    for c in loads:
+        c.start()
+    for load, store in zip(loads, stores):
+        load.wait()
+        store.start()
+    for c in stores:
+        c.wait()
+
+
+def relay_call(y1, x1, after):
+    dma = pltpu.SemaphoreType.DMA
+    return pl.pallas_call(
+        functools.partial(relay_kernel, len(after)),
+        out_shape=[jax.ShapeDtypeStruct((1, QROWS, 128), BF)] * 2,
+        in_specs=[ANY] * (2 + len(after)),
+        out_specs=[ANY] * 2,
+        scratch_shapes=[pltpu.VMEM((2, QROWS, 128), BF), dma((2,)), dma((2,))],
+        name="relay_weights",
+    )(y1, x1, *after)
+
+
+def unpack_kernel(packed, local, cross, reduce_w, spectral, expand, gains, biases):
+    local[...] = get_terms(packed, "local", CL)
+    cross[...] = get_terms(packed, "cross", CG)
+    reduce_w[...] = get_terms(packed, "reduce", CG)
+    spectral[...] = get_terms(packed, "spectral", CG)
+    expand[...] = get_terms(packed, "expand", CG)
+    rows = get_terms(packed, "norms", NORMS)
+    biases[...] = rows[0:1]
+    gains[...] = rows[1:2]
+
+
+def unpack_call(packed):
+    shape = jax.ShapeDtypeStruct
+    dims = ((9 * CH, CL), (9 * CL, CG), (CS, CG), (CG, CG), (CS, CG), (1, NORMS), (1, NORMS))
+    return pl.pallas_call(
+        unpack_kernel,
+        out_shape=[shape(d, F32) for d in dims],
+        in_specs=[VMEM],
+        out_specs=[VMEM] * 7,
+        name="unpack_terms",
+        compiler_params=pltpu.CompilerParams(vmem_limit_bytes=VMEM_LIMIT),
+    )(packed)
+
+
+def spread_kernel(batches, place, images, other, *refs):
+    parts, sem = refs[:PARTS], refs[-1]
+    core, z = place[1], place[2]
+    copies = []
+    for k, part in enumerate(parts):
+        i = jnp.clip((z ^ k) - (1 - core), 0, batches // 2 - 1)
+        copies.append(pltpu.make_async_copy(images.at[2 * i + 1 - core], part.at[0], sem.at[k, 0]))
+        copies.append(pltpu.make_async_copy(other.at[i], part.at[1], sem.at[k, 1]))
+    for c in copies:
+        c.start()
+    for c in copies:
+        c.wait()
+
+
+def spread_call(place, images, other, through=(), after=()):
+    batches, pixels, channels = images.shape
+    skip = len(through) + len(after)
+
+    def kernel(place, images, other, *refs):
+        spread_kernel(batches, place, images, other, *refs[skip:])
+
+    return pl.pallas_call(
+        kernel,
+        out_shape=[jax.ShapeDtypeStruct((2, pixels, channels), BF)] * PARTS + [jax.ShapeDtypeStruct(x.shape, x.dtype) for x in through],
+        in_specs=[SMEM, VMEM, VMEM] + [ANY] * skip,
+        out_specs=[ANY] * (PARTS + len(through)),
+        scratch_shapes=[pltpu.SemaphoreType.DMA((PARTS, 2))],
+        input_output_aliases={3 + i: PARTS + i for i in range(len(through))},
+        name="spread_images",
+        compiler_params=pltpu.CompilerParams(vmem_limit_bytes=VMEM_LIMIT),
+    )(place, images, other, *through, *after)
+
+
+def second_images(p0, p1, p2, p3, out, stage, sem_in, sem_out):
+    pixels = out.shape[1]
+    loads = [pltpu.make_async_copy(p.at[pl.ds(pixels, pixels)], stage.at[k], sem_in.at[k]) for k, p in enumerate((p0, p1, p2, p3))]
+    for c in loads:
+        c.start()
+    stores = [pltpu.make_async_copy(stage.at[k], out.at[k], sem_out.at[k]) for k in range(PARTS)]
+    for load, store in zip(loads, stores):
+        load.wait()
+        store.start()
+    for c in stores:
+        c.wait()
+
+
+def second_images_call(parts):
+    rows, channels = parts[0].shape
+    dma = pltpu.SemaphoreType.DMA
+    return pl.pallas_call(
+        second_images,
+        out_shape=jax.ShapeDtypeStruct((PARTS, rows // 2, channels), BF),
+        in_specs=[ANY] * PARTS,
+        out_specs=ANY,
+        scratch_shapes=[pltpu.VMEM((PARTS, rows // 2, channels), BF), dma((PARTS,)), dma((PARTS,))],
+        name="second_images",
+    )(*parts)
+
+
+def collect_kernel(batches, place, p0, p1, p2, p3, other, out, stage, sem):
+    core, z = place[1], place[2]
+    parts = (p0, p1, p2, p3)
+    pixels = p0.shape[0] // 2
+    copies = []
+    for k, part in enumerate(parts):
+        copies.append(pltpu.make_async_copy(part.at[pl.ds(0, pixels)], stage.at[k, 0], sem.at[k, 0]))
+        copies.append(pltpu.make_async_copy(other.at[k], stage.at[k, 1], sem.at[k, 1]))
+    for c in copies:
+        c.start()
+    for k in range(PARTS):
+        for j in range(2):
+            copies[2 * k + j].wait()
+            batch = 2 * (z ^ k) + (1 - core if j else core) - 1
+
+            @pl.when(jnp.logical_and(batch >= 0, batch < batches))
+            def _():
+                out[batch] = stage[k, j].astype(out.dtype)
+
+
+def collect_call(place, batches, parts, other, dtype):
+    rows, channels = parts[0].shape
+    return pl.pallas_call(
+        functools.partial(collect_kernel, batches),
+        out_shape=jax.ShapeDtypeStruct((batches, rows // 2, channels), dtype),
+        in_specs=[SMEM] + [ANY] * (PARTS + 1),
+        out_specs=VMEM,
+        scratch_shapes=[pltpu.VMEM((PARTS, 2, rows // 2, channels), BF), pltpu.SemaphoreType.DMA((PARTS, 2))],
+        name="collect_images",
+        compiler_params=pltpu.CompilerParams(vmem_limit_bytes=VMEM_LIMIT),
+    )(place, *parts, other)
+
+
+SOURCES = (
+    (("own", "own"), ("x1", "x1"), ("y1", "y1"), ("x2", "y2")),
+    (("x1", "x1"), ("own", "own"), ("x2", "y2"), ("y1", "y1")),
+    (("y1", "y1"), ("x2", "y2"), ("own", "own"), ("x1", "x1")),
+    (("x2", "y2"), ("y1", "y1"), ("x1", "x1"), ("own", "own")),
+)
+
+
+def load_weights(place, arrived, low, high, w, sems):
+    rank, core = place[0], place[1]
+    for s in range(low, high):
+        for r, sources in enumerate(SOURCES):
+
+            @pl.when(rank == r)
+            def _():
+                for half, name in enumerate(sources[s]):
+                    for other in range(2):
+                        quarter = 2 * half + (1 - core if other else core)
+                        if name == "own":
+                            src = arrived["own"].at[pl.ds(pl.multiple_of(quarter * QROWS, 16), QROWS)]
+                        else:
+                            src = arrived[name][other].at[half if name in ("x1", "y1") else 0]
+                        pltpu.make_async_copy(src, w.at[s - low, quarter], sems.at[s - low, 2 * half + other]).start()
+
+
+def wait_weights(own, index, w, sems):
+    for n in range(4):
+        pltpu.make_async_copy(own.at[pl.ds(0, QROWS)], w.at[index, 0], sems.at[index, n]).wait()
+
+
+def moments_of(v):
+    mean = jnp.mean(v, axis=0, keepdims=True)
+    centred = v - mean
+    return mean, jnp.sum(centred * centred, axis=0, keepdims=True)
+
+
+def combined(mean_ref, square_ref, rows):
+    images = mean_ref.shape[0]
+    means = [mean_ref[b] for b in range(images)]
+    mean = sum(means) / images
+    total = sum(square_ref[b] + rows * (means[b] - mean) ** 2 for b in range(images))
+    return mean, lax.rsqrt(total / (images * rows) + EPS)
+
+
+def halves(gain, bias, mean, inv):
+    scale = 0.5 * gain * inv
+    return scale, 0.5 * bias - mean * scale
+
+
+def beside(v, column, by, side):
+    if by < 0:
+        return jnp.where(column == 0, 0.0, pltpu.roll(v, 1, 0))
+    return jnp.where(column == side - 1, 0.0, pltpu.roll(v, v.shape[0] - 1, 0))
+
+
+def three_columns(dst, b, x, column, side):
+    pixels = x.shape[0]
+    wide = x.astype(F32)
+    for i, v in enumerate((beside(wide, column, -1, side).astype(BF), x, beside(wide, column, 1, side).astype(BF))):
+        dst[i, b, 0:side] = jnp.zeros((side, CL), BF)
+        dst[i, b, side : side + pixels] = v
+        dst[i, b, side + pixels : 2 * side + pixels] = jnp.zeros((side, CL), BF)
+
+
+def three_rows(x, side, images):
+    pixels = x.shape[0] // images
+    none = jnp.zeros((side, x.shape[1]), x.dtype)
+    back, on = [], []
+    for i in range(images):
+        back += [none, x[i * pixels : (i + 1) * pixels - side]]
+        on += [x[i * pixels + side : (i + 1) * pixels], none]
+    return stack_rows(back), x, stack_rows(on)
+
+
+def nine(src, b, side, flipped):
+    pixels = side * side
+    parts = []
+    for dh in range(3):
+        for dw in range(3):
+            i, j = (2 - dh, 2 - dw) if flipped else (dh, dw)
+            parts.append(src[j, b, i * side : i * side + pixels])
+    return parts
+
+
+def part_copies(whole, parts, sems):
+    rows = whole.shape[0] // len(parts)
+    return [pltpu.make_async_copy(whole.at[pl.ds(k * rows, rows)], ref, sems.at[k]) for k, ref in enumerate(parts)]
+
+
+def needed(low, high):
+    return sorted({name for sources in SOURCES for s in range(low, high) for name in sources[s]} - {"own"})
+
+
+class Space:
+    def __init__(self, **named):
+        self.__dict__.update(named)
+
+
+def geometry(side, images):
+    pixels, modes = side * side, side * (side // 2 + 1)
+    column = lambda: lax.broadcasted_iota(jnp.int32, (pixels, 1), 0) % side
+    wide = lambda: lax.broadcasted_iota(jnp.int32, (IM * pixels, 1), 0) % side
+    return Space(
+        side=side,
+        images=images,
+        pixels=pixels,
+        modes=modes,
+        steps=images // IM,
+        column=column,
+        wide=wide,
+        rows_of=lambda b: pl.ds(pl.multiple_of(b * (IM * pixels), IM * pixels), IM * pixels),
+        modes_of=lambda b: pl.ds(pl.multiple_of(b * (IM * modes), IM * modes), IM * modes),
+        image_rows=lambda b, i: pl.ds(pl.multiple_of(b * (IM * pixels) + i * pixels, pixels), pixels),
+    )
+
+
+def forward_section(geo, v, ws, a, o, odd):
+    column, wide = geo.column(), geo.wide()
+    side, pixels, modes = geo.side, geo.pixels, geo.modes
+    gain, bias = read_norms(ws)
+
+    def reduce_step(b, _):
+        r = geo.rows_of(b)
+        for i in range(IM):
+            three_columns(v.xp, b * IM + i, a[geo.image_rows(b, i), 0:CL], column, side)
+        x = dot_nt(a[r, CL:CH], read(ws, "reduce", 0, CS))
+        v.q[r] = x
+        v.mu1[b], v.sq1[b] = moments_of(x)
+        return 0
+
+    lax.fori_loop(0, geo.steps, reduce_step, 0, unroll=UN)
+    mean1, inv1 = combined(v.mu1, v.sq1, IM * pixels)
+    scale1, shift1 = halves(gain[:, :CS], bias[:, :CS], mean1, inv1)
+
+    def spectral_step(b, _):
+        r, rs = geo.rows_of(b), geo.modes_of(b)
+        h = v.q[r] * scale1 + shift1
+        v.h1[r] = h.astype(BF)
+        act = silu_of_half(h)
+        v.t[r] = act
+        act = act.astype(BF)
+        spec = [dot(v.mf[...], act[i * pixels : (i + 1) * pixels]).astype(BF) for i in range(IM)]
+        real = stack_rows([x[:modes] for x in spec])
+        imaginary = stack_rows([x[modes:] for x in spec])
+        v.sv[0, rs] = real
+        v.sv[1, rs] = imaginary
+        mix = dot(real, read(ws, "spectral", 0, CS)) + dot(imaginary, read(ws, "spectral", CS, CS))
+        v.f[rs] = mix
+        v.mu2[b], v.sq2[b] = moments_of(mix)
+        taps = stack_rows([stack_cols(nine(v.xp, b * IM + i, side, False)) for i in range(IM)])
+        v.p[r] = dot(taps, conv_matrix(ws))
+        return 0
+
+    lax.fori_loop(0, geo.steps, spectral_step, 0, unroll=UN)
+    mean2, inv2 = combined(v.mu2, v.sq2, IM * modes)
+    scale2, shift2 = halves(gain[:, CS : CS + CG], bias[:, CS : CS + CG], mean2, inv2)
+
+    def join_step(b, _):
+        r, rs = geo.rows_of(b), geo.modes_of(b)
+        h = v.f[rs] * scale2 + shift2
+        v.h2[rs] = h.astype(BF)
+        e = silu_of_half(h)
+        er, ei = e[:, :CS].astype(BF), e[:, CS:].astype(BF)
+        back = []
+        for i in range(IM):
+            m = slice(i * modes, (i + 1) * modes)
+            back.append(dot(v.mi[...], stack_rows([er[m], ei[m]])))
+        j = (v.t[r] + stack_rows(back)).astype(BF)
+        v.jv[r] = j
+        pre_global = v.p[r, CL:CH] + dot(j, read(ws, "expand", 0, CS))
+        y = dot(stack_cols(three_rows(a[r, CL:CH], side, IM)), global_by_row(ws))
+        pre_local = v.p[r, 0:CL] + beside(y[:, :CL], wide, -1, side) + y[:, CL : 2 * CL] + beside(y[:, 2 * CL :], wide, 1, side)
+        v.p[r, 0:CL] = pre_local
+        v.p[r, CL:CH] = pre_global
+        ml, sl = moments_of(pre_local)
+        mg, sg = moments_of(pre_global)
+        v.mu3[b] = stack_cols([ml, mg])
+        v.sq3[b] = stack_cols([sl, sg])
+        return 0
+
+    lax.fori_loop(0, geo.steps, join_step, 0, unroll=UN)
+    mean3, inv3 = combined(v.mu3, v.sq3, IM * pixels)
+    scale3, shift3 = halves(gain[:, CS + CG :], bias[:, CS + CG :], mean3, inv3)
+
+    def end_step(b, _):
+        r = geo.rows_of(b)
+        h = v.p[r] * scale3 + shift3
+        v.h3[r] = h.astype(BF)
+        y = silu_of_half(h)
+        if odd is not None:
+            y = y + jnp.where(odd, o[r].astype(F32), 0.0)
+        o[r] = y.astype(BF)
+        return 0
+
+    lax.fori_loop(0, geo.steps, end_step, 0, unroll=UN)
+    return stack_cols([inv1, inv2, inv3])
+
+
+def norm_terms(sums, gain, bias, factor, count):
+    first, second = (jnp.sum(x, axis=0, keepdims=True) for x in sums)
+    first = 0.5 * first
+    second = (second - bias * first) / gain
+    k1 = factor / count * (second * bias / gain - first)
+    return first, second, (0.5 * factor, k1, 2.0 / count * factor * second / gain)
+
+
+def part_sums(c, d, h):
+    add = lambda x: jnp.sum(x.reshape(x.shape[0] // 8, 8, x.shape[1]), axis=0)
+    return c[0] + add(d), c[1] + add(d * h)
+
+
+def no_sums(c):
+    return jnp.zeros((8, c), F32), jnp.zeros((8, c), F32)
+
+
+def local_adjoint(geo, v, ws, dp, wide):
+    back, same, on = three_rows(dp, geo.side, IM)
+    y = dot_nt(stack_cols([on, same, back]), conv_by_column(ws))
+    return beside(y[:, :CL], wide, 1, geo.side) + y[:, CL : 2 * CL] + beside(y[:, 2 * CL :], wide, -1, geo.side)
+
+
+def global_adjoint(geo, v, ws, b):
+    taps = stack_rows([stack_cols(nine(v.xp, b * IM + i, geo.side, True)) for i in range(IM)])
+    return dot_nt(taps, global_matrix(ws))
+
+
+def backward_section(geo, v, ws, inv, g, o, even, convs):
+    column, wide = geo.column(), geo.wide()
+    side, pixels, modes = geo.side, geo.pixels, geo.modes
+    n1, n2 = float(geo.images * pixels), float(geo.images * modes)
+    gain, bias = read_norms(ws)
+    g1, g2, g3 = gain[:, :CS], gain[:, CS : CS + CG], gain[:, CS + CG :]
+    b1, b2, b3 = bias[:, :CS], bias[:, CS : CS + CG], bias[:, CS + CG :]
+    c1, c2, c3 = g1 * inv[:, :CS], g2 * inv[:, CS : CS + CG], g3 * inv[:, CS + CG :]
+
+    def end_step(b, c):
+        r = geo.rows_of(b)
+        h = v.h3[r].astype(F32)
+        d = g[r].astype(F32) * twice_slope(h)
+        v.p[r] = d
+        return part_sums(c, d, h)
+
+    first3, second3, k3 = norm_terms(lax.fori_loop(0, geo.steps, end_step, no_sums(CH), unroll=UN), g3, b3, c3, n1)
+
+    def join_step(b, c):
+        r, rs = geo.rows_of(b), geo.modes_of(b)
+        dp = (k3[0] * v.p[r] + (k3[1] - k3[2] * v.h3[r].astype(F32))).astype(BF)
+        v.dpv[r] = dp
+        djv = dot_nt(dp[:, CL:], read(ws, "expand", 0, CS))
+        v.dj[r] = djv
+        djv = djv.astype(BF)
+        de = [dot(v.mit[...], djv[i * pixels : (i + 1) * pixels]) for i in range(IM)]
+        de = stack_cols([stack_rows([x[:modes] for x in de]), stack_rows([x[modes:] for x in de])])
+        h = v.h2[rs].astype(F32)
+        d = de * twice_slope(h)
+        v.du2[rs] = d
+        if convs:
+            for i in range(IM):
+                three_columns(v.xp, b * IM + i, dp[i * pixels : (i + 1) * pixels, :CL], column, side)
+            v.p[r, 0:CL] = local_adjoint(geo, v, ws, dp, wide)
+        return part_sums(c, d, h)
+
+    first2, second2, k2 = norm_terms(lax.fori_loop(0, geo.steps, join_step, no_sums(CG), unroll=UN), g2, b2, c2, n2)
+
+    def spectral_step(b, c):
+        r, rs = geo.rows_of(b), geo.modes_of(b)
+        df = (k2[0] * v.du2[rs] + (k2[1] - k2[2] * v.h2[rs].astype(F32))).astype(BF)
+        v.dfv[rs] = df
+        ds = dot_nt(df, read(ws, "spectral", 0, CG))
+        dr, di = ds[:, :CS].astype(BF), ds[:, CS:].astype(BF)
+        back = []
+        for i in range(IM):
+            m = slice(i * modes, (i + 1) * modes)
+            back.append(dot(v.mft[...], stack_rows([dr[m], di[m]])))
+        dt = v.dj[r] + stack_rows(back)
+        h = v.h1[r].astype(F32)
+        d = dt * twice_slope(h)
+        v.du1[r] = d
+        if convs:
+            v.p[r, CL:CH] = global_adjoint(geo, v, ws, b)
+        return part_sums(c, d, h)
+
+    first1, second1, k1 = norm_terms(lax.fori_loop(0, geo.steps, spectral_step, no_sums(CS), unroll=UN), g1, b1, c1, n1)
+
+    def reduce_step(b, c):
+        r = geo.rows_of(b)
+        dq = (k1[0] * v.du1[r] + (k1[1] - k1[2] * v.h1[r].astype(F32))).astype(BF)
+        v.dqv[r] = dq
+        if convs:
+            dx = stack_cols([v.p[r, 0:CL], v.p[r, CL:CH] + dot(dq, read(ws, "reduce", 0, CS))])
+            if even is not None:
+                dx = dx + jnp.where(even, o[r].astype(F32), 0.0)
+            o[r] = dx.astype(BF)
+        return c
+
+    lax.fori_loop(0, geo.steps, reduce_step, 0, unroll=UN)
+    return stack_cols([first1, first2, first3]), stack_cols([second1, second2, second3])
+
+
+def weight_terms(geo, v, norms):
+    column, side, pixels = geo.column(), geo.side, geo.pixels
+
+    def tap_products(source, flipped, product):
+        def columns(b, _):
+            three_columns(v.xp, b, source[pl.ds(pl.multiple_of(b * pixels, pixels), pixels), 0:CL], column, side)
+            return 0
+
+        lax.fori_loop(0, geo.images, columns, 0)
+
+        def one_row(dh, _):
+            def gather(b, _):
+                r = pl.ds(pl.multiple_of(b * pixels, pixels), pixels)
+                first = pl.multiple_of((2 - dh if flipped else dh) * side, side)
+                for dw in range(3):
+                    v.taps[r, dw * CL : (dw + 1) * CL] = v.xp[2 - dw if flipped else dw, b, pl.ds(first, pixels)]
+                return 0
+
+            lax.fori_loop(0, geo.images, gather, 0)
+            product(dh)
+            return 0
+
+        lax.fori_loop(0, 3, one_row, 0)
+
+    def from_gradient(dh):
+        u = dot_tn(v.ain[:, CL:], v.taps[...])
+        for dw in range(3):
+            put_terms(v.terms, "local", (dh * 3 + dw) * CH + CL, u[:, dw * CL : (dw + 1) * CL])
+
+    def from_input(dh):
+        u = dot_tn(v.taps[...], v.dpv[...])
+        for dw in range(3):
+            tap = slice(dw * CL, (dw + 1) * CL)
+            put_terms(v.terms, "local", (dh * 3 + dw) * CH, u[tap, :CL])
+            put_terms(v.terms, "cross", (dh * 3 + dw) * CL, u[tap, CL:])
+
+    tap_products(v.dpv, True, from_gradient)
+    tap_products(v.ain, False, from_input)
+    put_terms(v.terms, "reduce", 0, dot_tn(v.dqv[...], v.ain[:, CL:]))
+    put_terms(v.terms, "spectral", 0, dot_tn(v.sv[0], v.dfv[...]))
+    put_terms(v.terms, "spectral", CS, dot_tn(v.sv[1], v.dfv[...]))
+    put_terms(v.terms, "expand", 0, dot_tn(v.jv[...], v.dpv[:, CL:]))
+    put_norm_terms(v.terms, norms)
+
+
+def fill_parts(parts, whole, sems):
+    rows = whole.shape[0] // len(parts)
+    return [pltpu.make_async_copy(ref, whole.at[pl.ds(k * rows, rows)], sems.at[k]) for k, ref in enumerate(parts)]
+
+
+def start_all(copies):
+    for c in copies:
+        c.start()
+
+
+def wait_all(copies):
+    for c in copies:
+        c.wait()
+
+
+DMA = pltpu.SemaphoreType.DMA
+
+
+class Arguments:
+    def __init__(self):
+        self.ins, self.specs, self.outs, self.out_specs, self.scratch, self.aliases = [], [], [], [], [], {}
+        self.names = [[], [], []]
+
+    def take(self, name, value, spec):
+        many = isinstance(value, (list, tuple))
+        values = list(value) if many else [value]
+        self.names[0].append((name, len(values) if many else None))
+        at = len(self.ins)
+        self.ins += values
+        self.specs += [spec] * len(values)
+        return at
+
+    def give(self, name, shape, dtype, spec, count=None, over=None):
+        self.names[1].append((name, count))
+        for i in range(count or 1):
+            if over is not None:
+                self.aliases[over + i] = len(self.outs)
+            self.outs.append(jax.ShapeDtypeStruct(shape, dtype))
+            self.out_specs.append(spec)
+
+    def hold(self, name, kind):
+        self.names[2].append((name, None))
+        self.scratch.append(kind)
+
+    def unpack(self, refs):
+        refs, space = list(refs), Space()
+        for group in self.names:
+            for name, count in group:
+                setattr(space, name, refs.pop(0) if count is None else [refs.pop(0) for _ in range(count)])
+        return space
+
+    def call(self, body, name, flops, moved=20_000_000):
+        results = pl.pallas_call(
+            lambda *refs: body(self.unpack(refs)),
+            out_shape=self.outs,
+            in_specs=self.specs,
+            out_specs=self.out_specs,
+            scratch_shapes=self.scratch,
+            input_output_aliases=self.aliases,
+            name=name,
+            cost_estimate=pl.CostEstimate(flops=int(flops), bytes_accessed=moved, transcendentals=0),
+            compiler_params=pltpu.CompilerParams(vmem_limit_bytes=VMEM_LIMIT),
+        )(*self.ins)
+        results, space = list(results), Space()
+        for out_name, count in self.names[1]:
+            setattr(space, out_name, results.pop(0) if count is None else [results.pop(0) for _ in range(count)])
+        return space
+
+
+def take_weights(args, own, arrived, low, high):
+    names = needed(low, high)
+    args.take("own", own, ANY)
+    for name in names:
+        args.take("got_" + name, arrived[name], ANY)
+    args.hold("w", pltpu.VMEM((high - low, QUARTERS, QROWS, 128), BF))
+    args.hold("wsem", DMA((high - low, 4)))
+    return names
+
+
+def got_weights(v, names):
+    return {"own": v.own, **{name: getattr(v, "got_" + name) for name in names}}
+
+
+def hold_forward(args, n, m, images, pixels, side):
+    args.hold("mu1", pltpu.VMEM((images // IM, 1, CS), F32))
+    args.hold("sq1", pltpu.VMEM((images // IM, 1, CS), F32))
+    args.hold("mu2", pltpu.VMEM((images // IM, 1, CG), F32))
+    args.hold("sq2", pltpu.VMEM((images // IM, 1, CG), F32))
+    args.hold("mu3", pltpu.VMEM((images // IM, 1, CH), F32))
+    args.hold("sq3", pltpu.VMEM((images // IM, 1, CH), F32))
+
+
+def hold_work(args, n, m, images, pixels, side):
+    args.hold("xp", pltpu.VMEM((3, images, pixels + 2 * side, CL), BF))
+    args.hold("q", pltpu.VMEM((n, CS), F32))
+    args.hold("t", pltpu.VMEM((n, CS), F32))
+    args.hold("f", pltpu.VMEM((m, CG), F32))
+    args.hold("p", pltpu.VMEM((n, CH), F32))
+
+
+def hold_terms(args, n, m):
+    args.hold("dpv", pltpu.VMEM((n, CH), BF))
+    args.hold("dqv", pltpu.VMEM((n, CS), BF))
+    args.hold("dfv", pltpu.VMEM((m, CG), BF))
+    args.hold("ain", pltpu.VMEM((n, CH), BF))
+    args.hold("sv", pltpu.VMEM((2, m, CS), BF))
+    args.hold("jv", pltpu.VMEM((n, CS), BF))
+    args.hold("taps", pltpu.VMEM((n, 3 * CL), BF))
+    args.hold("terms", pltpu.VMEM((QUARTERS * QROWS, 128), BF))
+
+
+def first_call(place, inputs, own, arrived, mf, mi, after, side, images):
+    geo = geometry(side, images)
+    n, m = images * geo.pixels, images * geo.modes
+    args = Arguments()
+    args.take("place", place, SMEM)
+    args.take("inputs", inputs, ANY)
+    args.take("mf", mf, VMEM)
+    args.take("mi", mi, VMEM)
+    args.take("after", after, ANY)
+    names = take_weights(args, own, arrived, 0, 1)
+    args.give("out", (n, CH), BF, ANY)
+    args.give("h1_out", (n, CS), BF, ANY)
+    args.give("h2_out", (m, CG), BF, ANY)
+    args.give("h3_out", (n, CH), BF, ANY)
+    args.give("spec_out", (2, m, CS), BF, ANY)
+    args.give("join_out", (n, CS), BF, ANY)
+    args.give("inv_out", (1, NORMS), F32, VMEM)
+    args.hold("a", pltpu.VMEM((n, CH), BF))
+    args.hold("o", pltpu.VMEM((n, CH), BF))
+    args.hold("h1", pltpu.VMEM((n, CS), BF))
+    args.hold("h2", pltpu.VMEM((m, CG), BF))
+    args.hold("h3", pltpu.VMEM((n, CH), BF))
+    args.hold("sv", pltpu.VMEM((2, m, CS), BF))
+    args.hold("jv", pltpu.VMEM((n, CS), BF))
+    hold_work(args, n, m, images, geo.pixels, side)
+    hold_forward(args, n, m, images, geo.pixels, side)
+    args.hold("isem", DMA((PARTS,)))
+    args.hold("osem", DMA((6,)))
+
+    def body(v):
+        loads = fill_parts(v.inputs, v.a, v.isem)
+        start_all(loads)
+        load_weights(v.place, got_weights(v, names), 0, 1, v.w, v.wsem)
+        wait_all(loads)
+        wait_weights(v.own, 0, v.w, v.wsem)
+        v.inv_out[...] = forward_section(geo, v, v.w.at[0], v.a, v.o, None)
+        pairs = (
+            (v.o, v.out),
+            (v.h1, v.h1_out),
+            (v.h2, v.h2_out),
+            (v.h3, v.h3_out),
+            (v.sv, v.spec_out),
+            (v.jv, v.join_out),
+        )
+        stores = [pltpu.make_async_copy(a, b, v.osem.at[i]) for i, (a, b) in enumerate(pairs)]
+        start_all(stores)
+        wait_all(stores)
+
+    return args.call(body, "forward_0", 1, 1)
+
+
+def middle_call(place, out0, inputs, seeds, own, arrived, tables, side, images):
+    low, high = 1, 4
+    geo = geometry(side, images)
+    n, m, count = images * geo.pixels, images * geo.modes, high - low
+    args = Arguments()
+    args.take("place", place, SMEM)
+    args.take("out0", out0, ANY)
+    args.take("inputs", inputs, ANY)
+    seeds_at = args.take("seeds", seeds, ANY)
+    for name, table in zip(("mf", "mi", "mft", "mit"), tables):
+        args.take(name, table, VMEM)
+    names = take_weights(args, own, arrived, low, high)
+    args.give("grads0", (n // PARTS, CH), BF, ANY, PARTS, seeds_at)
+    args.give("grad1", (n, CH), BF, ANY)
+    args.give("own_out", (n // PARTS, CH), BF, ANY, PARTS)
+    args.give("own_grad", (n // PARTS, CH), BF, ANY, PARTS)
+    args.give("own_terms", (QUARTERS * QROWS, 128), BF, ANY)
+    args.hold("cur", pltpu.VMEM((2, n, CH), BF))
+    args.hold("hats1", pltpu.VMEM((count, n, CS), BF))
+    args.hold("hats2", pltpu.VMEM((count, m, CG), BF))
+    args.hold("hats3", pltpu.VMEM((count, n, CH), BF))
+    args.hold("inv", pltpu.VMEM((count, 1, NORMS), F32))
+    args.hold("spec", pltpu.VMEM((2, m, CS), BF))
+    args.hold("join", pltpu.VMEM((n, CS), BF))
+    hold_work(args, n, m, images, geo.pixels, side)
+    hold_forward(args, n, m, images, geo.pixels, side)
+    hold_terms(args, n, m)
+    args.hold("asem", DMA((1,)))
+    args.hold("isem", DMA((PARTS,)))
+    args.hold("gsem", DMA((PARTS,)))
+    args.hold("outsem", DMA((PARTS,)))
+    args.hold("gradsem", DMA((PARTS,)))
+    args.hold("ksem", DMA((3,)))
+    args.hold("tsem", DMA((1,)))
+    args.hold("lastsem", DMA((PARTS + 1,)))
+
+    def body(v):
+        rank = v.place[0]
+        loads = [pltpu.make_async_copy(v.out0, v.cur.at[1], v.asem.at[0])] + fill_parts(v.inputs, v.cur.at[0], v.isem)
+        start_all(loads)
+        load_weights(v.place, got_weights(v, names), low, high, v.w, v.wsem)
+        wait_all(loads)
+        rank0_out = part_copies(v.cur.at[1], v.own_out, v.outsem)
+
+        @pl.when(rank == 0)
+        def _():
+            start_all(rank0_out)
+
+        def at(index, **more):
+            return Space(**{**v.__dict__, "h1": v.hats1.at[index], "h2": v.hats2.at[index], "h3": v.hats3.at[index], **more})
+
+        def forward_one(index, _):
+            s = index + low
+            a, o = v.cur.at[s % 2], v.cur.at[(s + 1) % 2]
+            mine = rank == s
+            wait_weights(v.own, index, v.w, v.wsem)
+            keep_in = pltpu.make_async_copy(a, v.ain, v.ksem.at[0])
+
+            @pl.when(mine)
+            def _():
+                keep_in.start()
+
+            v.inv[index] = forward_section(geo, at(index, sv=v.spec, jv=v.join), v.w.at[index], a, o, s % 2 == 1)
+
+            @pl.when(mine)
+            def _():
+                keeps = [
+                    pltpu.make_async_copy(v.spec, v.sv, v.ksem.at[1]),
+                    pltpu.make_async_copy(v.join, v.jv, v.ksem.at[2]),
+                    *part_copies(o, v.own_out, v.outsem),
+                ]
+                start_all(keeps)
+                wait_all([keep_in, *keeps])
+
+            @pl.when(jnp.logical_and(rank == 0, index == 0))
+            def _():
+                wait_all(rank0_out)
+
+            return 0
+
+        lax.fori_loop(0, count, forward_one, 0)
+        loads = fill_parts(v.seeds, v.cur.at[(high - 1) % 2], v.gsem)
+        start_all(loads)
+        wait_all(loads)
+
+        @pl.when(v.place[3] == 0)
+        def _():
+            v.cur[(high - 1) % 2] = jnp.zeros((n, CH), BF)
+
+        def backward_one(step, _):
+            index = count - 1 - step
+            s = index + low
+            g, o = v.cur.at[s % 2], v.cur.at[(s + 1) % 2]
+            norms = backward_section(geo, at(index, du1=v.q, du2=v.f, dj=v.t), v.w.at[index], v.inv[index], g, o, s % 2 == 0, True)
+
+            @pl.when(rank == s)
+            def _():
+                keeps = part_copies(o, v.own_grad, v.gradsem)
+                start_all(keeps)
+                weight_terms(geo, v, norms)
+                keeps.append(pltpu.make_async_copy(v.terms, v.own_terms, v.tsem.at[0]))
+                keeps[-1].start()
+                wait_all(keeps)
+
+            return 0
+
+        lax.fori_loop(0, count, backward_one, 0)
+        stores = part_copies(v.cur.at[0], v.grads0, v.lastsem)
+        stores.append(pltpu.make_async_copy(v.cur.at[1], v.grad1, v.lastsem.at[PARTS]))
+        start_all(stores)
+        wait_all(stores)
+
+    return args.call(body, "sections_1_3", images * 6e9)
+
+
+def last_norms_call(place, first, grads0, inputs, own_terms, weights, arrived, tables, side, images):
+    geo = geometry(side, images)
+    n, m = images * geo.pixels, images * geo.modes
+    args = Arguments()
+    args.take("place", place, SMEM)
+    args.take("grads0", grads0, ANY)
+    args.take("inputs", inputs, ANY)
+    args.take("h1_in", first.h1_out, ANY)
+    args.take("h2_in", first.h2_out, ANY)
+    args.take("h3_in", first.h3_out, ANY)
+    args.take("spec_in", first.spec_out, ANY)
+    args.take("join_in", first.join_out, ANY)
+    args.take("inv", first.inv_out, VMEM)
+    for name, table in zip(("mft", "mit"), tables):
+        args.take(name, table, VMEM)
+    terms_at = args.take("terms_in", own_terms, ANY)
+    names = take_weights(args, weights, arrived, 0, 1)
+    args.give("dp", (n, CH), BF, ANY)
+    args.give("dq", (n, CS), BF, ANY)
+    args.give("own_terms", (QUARTERS * QROWS, 128), BF, ANY, None, terms_at)
+    args.hold("g", pltpu.VMEM((n, CH), BF))
+    args.hold("h1", pltpu.VMEM((n, CS), BF))
+    args.hold("h2", pltpu.VMEM((m, CG), BF))
+    args.hold("h3", pltpu.VMEM((n, CH), BF))
+    hold_work(args, n, m, images, geo.pixels, side)
+    hold_terms(args, n, m)
+    args.hold("gsem", DMA((PARTS,)))
+    args.hold("isem", DMA((PARTS,)))
+    args.hold("hsem", DMA((3,)))
+    args.hold("ksem", DMA((2,)))
+    args.hold("osem", DMA((3,)))
+
+    def body(v):
+        rank = v.place[0]
+        loads = fill_parts(v.grads0, v.g, v.gsem)
+        hats = ((v.h1_in, v.h1), (v.h2_in, v.h2), (v.h3_in, v.h3))
+        loads += [pltpu.make_async_copy(a, b, v.hsem.at[i]) for i, (a, b) in enumerate(hats)]
+        start_all(loads)
+        load_weights(v.place, got_weights(v, names), 0, 1, v.w, v.wsem)
+        kept = fill_parts(v.inputs, v.ain, v.isem)
+        kept += [pltpu.make_async_copy(v.spec_in, v.sv, v.ksem.at[0]), pltpu.make_async_copy(v.join_in, v.jv, v.ksem.at[1])]
+
+        @pl.when(rank == 0)
+        def _():
+            start_all(kept)
+
+        wait_all(loads)
+        wait_weights(v.own, 0, v.w, v.wsem)
+        space = Space(**{**v.__dict__, "du1": v.q, "du2": v.f, "dj": v.t})
+        norms = backward_section(geo, space, v.w.at[0], v.inv[...], v.g, None, None, False)
+        stores = [pltpu.make_async_copy(v.dpv, v.dp, v.osem.at[0]), pltpu.make_async_copy(v.dqv, v.dq, v.osem.at[1])]
+        start_all(stores)
+
+        @pl.when(rank == 0)
+        def _():
+            wait_all(kept)
+            weight_terms(geo, v, norms)
+            out = pltpu.make_async_copy(v.terms, v.own_terms, v.osem.at[2])
+            out.start()
+            out.wait()
+
+        wait_all(stores)
+
+    return args.call(body, "backward_0_norms", images * 400e6)
+
+
+def last_convs_call(place, back, grad1, own_grad, weights, arrived, side, images):
+    geo = geometry(side, images)
+    n, m = images * geo.pixels, images * geo.modes
+    args = Arguments()
+    args.take("place", place, SMEM)
+    args.take("dp", back.dp, ANY)
+    args.take("dq", back.dq, ANY)
+    args.take("grad1", grad1, ANY)
+    grad_at = args.take("grad_in", own_grad, ANY)
+    names = take_weights(args, weights, arrived, 0, 1)
+    args.give("own_grad", (n // PARTS, CH), BF, ANY, PARTS, grad_at)
+    args.hold("dpv", pltpu.VMEM((n, CH), BF))
+    args.hold("dqv", pltpu.VMEM((n, CS), BF))
+    args.hold("o", pltpu.VMEM((n, CH), BF))
+    args.hold("xp", pltpu.VMEM((3, images, geo.pixels + 2 * side, CL), BF))
+    args.hold("lsem", DMA((3,)))
+    args.hold("osem", DMA((PARTS,)))
+
+    def body(v):
+        @pl.when(v.place[0] == 0)
+        def _():
+            pairs = ((v.dp, v.dpv), (v.dq, v.dqv), (v.grad1, v.o))
+            loads = [pltpu.make_async_copy(a, b, v.lsem.at[i]) for i, (a, b) in enumerate(pairs)]
+            start_all(loads)
+            load_weights(v.place, got_weights(v, names), 0, 1, v.w, v.wsem)
+            wait_all(loads)
+            wait_weights(v.own, 0, v.w, v.wsem)
+            ws = v.w.at[0]
+            column, wide = geo.column(), geo.wide()
+
+            def step(b, _):
+                r = geo.rows_of(b)
+                dp = v.dpv[r]
+                for i in range(IM):
+                    three_columns(v.xp, b * IM + i, dp[i * geo.pixels : (i + 1) * geo.pixels, :CL], column, side)
+                dxl = local_adjoint(geo, v, ws, dp, wide)
+                dxg = global_adjoint(geo, v, ws, b) + dot(v.dqv[r], read(ws, "reduce", 0, CS))
+                v.o[r] = (stack_cols([dxl, dxg]) + v.o[r].astype(F32)).astype(BF)
+                return 0
+
+            lax.fori_loop(0, geo.steps, step, 0)
+            stores = part_copies(v.o, v.own_grad, v.osem)
+            start_all(stores)
+            wait_all(stores)
+
+    return args.call(body, "backward_0_convs", images * 600e6)
+
+
+def exchange_weights(send, after):
+    def over(bit, x):
+        return lax.ppermute(x, "pipe", [(i ^ bit, i) for i in range(4)])
+
+    def swap(x):
+        return lax.ppermute(x, "dp", [(i, i ^ 1) for i in range(lax.axis_size("dp"))])
+
+    got = {"x1": over(1, send), "y1": over(2, send)}
+    over_x, over_y = relay_call(got["y1"], got["x1"], after)
+    got["x2"], got["y2"] = over(1, over_x), over(2, over_y)
+    return {name: (x, swap(x)) for name, x in got.items()}
+
+
+def local_device(images_in, conv_local, conv_cross, reduce_weight, spectral_weight, expand_weight, norm_gain, norm_bias, cotangent, hole_mask):
+    batches, _, side, _, channels = images_in.shape
+    pixels = side * side
+    dp_size = lax.axis_size("dp")
+    dp_rank = lax.axis_index("dp")
+    core = dp_rank % 2
+    holders = range(1, 1 + batches)
+    holds = jnp.logical_and(dp_rank >= holders.start, dp_rank < holders.stop)
+    place = jnp.stack([lax.axis_index("pipe"), core, dp_rank // 2, holds]).astype(jnp.int32)
+    table_to, table_from = dft_np(side)
+    mf, mi = jnp.asarray(table_to, BF), jnp.asarray(table_from, BF)
+    mft, mit = jnp.asarray(table_to.T, BF), jnp.asarray(table_from.T, BF)
+
+    def swap(x):
+        return lax.ppermute(x, "dp", [(i, i ^ 1) for i in range(dp_size)])
+
+    def along_z(k, x, pairs):
+        return lax.ppermute(x, "dp", [(i, j) for i, j in pairs if i ^ j == 2 * k])
+
+    to_holders = [(i, j) for i in range(dp_size) for j in holders]
+    from_holders = [(j, i) for i, j in to_holders]
+
+    def to_batches(x, through=(), after=()):
+        other = swap(lax.dynamic_index_in_dim(x.reshape(batches // 2, 2, pixels, channels), core, 1, keepdims=False))
+        parts = spread_call(place, x, other, through, after)
+        through = parts[PARTS:]
+        parts = list(parts[:1]) + [along_z(k, parts[k], to_holders) for k in range(1, PARTS)]
+        return [part.reshape(2 * pixels, channels) for part in parts], *through
+
+    def to_images(parts, dtype):
+        parts = list(parts[:1]) + [along_z(k, parts[k], from_holders) for k in range(1, PARTS)]
+        other = swap(second_images_call(parts))
+        return collect_call(place, batches, parts, other, dtype).reshape(1, batches, 1, side, side, channels)
+
+    own, send = pack_call(
+        place,
+        conv_local.reshape(-1, CL),
+        conv_cross.reshape(-1, CG),
+        reduce_weight[0].T,
+        spectral_weight[0],
+        expand_weight[0],
+        norm_gain,
+        norm_bias,
+    )
+    inputs, send = to_batches(images_in.reshape(batches, pixels, channels), (send,))
+    hole_float = hole_mask.astype(F32)
+    hole_counts = jnp.sum(hole_float, axis=(2, 3), keepdims=True)
+    weighting = 0.25 + hole_float * pixels / (hole_counts + pixels / 8.0)
+    seed = (cotangent.astype(F32) * weighting[..., None]).astype(BF)
+
+    seeds, *_ = to_batches(seed.reshape(batches, pixels, channels), after=inputs[1:])
+    arrived = exchange_weights(send, seeds[:1])
+    first = first_call(place, inputs, own, arrived, mf, mi, seeds[1:3], side, dp_size)
+    middle = middle_call(place, first.out, inputs, seeds, own, arrived, (mf, mi, mft, mit), side, dp_size)
+    activations = to_images(middle.own_out, BF)
+    back = last_norms_call(
+        place, first, middle.grads0, inputs, middle.own_terms, own, arrived, (mft, mit), side, dp_size
+    )
+    own_grad = last_convs_call(place, back, middle.grad1, middle.own_grad, own, arrived, side, dp_size).own_grad
+    own_terms = back.own_terms
+    input_grads = to_images(own_grad, F32)
+    local, cross, reduce_w, spectral, expand, gain, bias = unpack_call(lax.psum(own_terms, "dp"))
+    return (
+        activations,
+        input_grads,
+        local.reshape(conv_local.shape),
+        cross.reshape(conv_cross.shape),
+        reduce_w.T[None],
+        spectral[None],
+        expand[None],
+        gain,
+        bias,
+    )
+
+
 def solution(mesh):
     placed = (
         P(None, "dp", None, None, None),
@@ -385,6 +1548,12 @@
         P(None, "dp", None, None, None),
         P(None, "dp", None, None),
     )
+
+    def on_device(images_in, *rest):
+        dp_size = lax.axis_size("dp")
+        fits = images_in.shape[1] == 1 and dp_size == 8 and images_in.shape[0] == dp_size - 2 and lax.axis_size("pipe") == 4
+        return (local_device if fits else general_device)(images_in, *rest)
+
     return jax.shard_map(
         on_device,
         mesh=mesh,

time: 2460 us -> 399 us (0.16)
  blocking collectives: 1110 us -> 0 us
  matrix products: 456 us -> 0 us
  local copies, waits for them, and re-layouts: 427 us -> 6.23 us
  Pallas kernels: 0 us -> 187 us
  other arithmetic: 123 us -> 1.2 us
  waiting for transfers between devices: 186 us -> 124 us
  starting transfers between devices: 112 us -> 62.7 us
    psum x81 -> x0, blocking collectives: 1110 us -> none  [the longest x27 371 us: moments(): average = lax.psum(jnp.sum(values, axis=sum_axes), 'dp') / count_all]
    dot_general x504 -> x0, matrix products: 456 us -> none  [the longest x54 123 us: conv_apply(): jnp.einsum('bhwk,kd->bhwd', patches(values), flat_kernel, preferred_eleme...]
    while x1278 -> x0, local copies, waits for them, and re-layouts: 191 us -> none
    pallas_call x0 -> x13, Pallas kernels: none -> 187 us  [the longest x4 160 us: call(): pl.pallas_call(lambda *refs: body(self.unpack(refs)), out_shape=self.outs...]
    psum x1, waiting for transfers between devices: 125 us -> 57.8 us  [local_device(): lax.psum(own_terms, 'dp')]
    dynamic_slice x45 -> x0, local copies, waits for them, and re-layouts: 51.1 us -> none  [the longest x27 34.9 us: store(): previous = lax.dynamic_index_in_dim(buffer, slot_index, 0, keepdims=False)]
    ppermute x36 -> x24, starting transfers between devices: 112 us -> 62.6 us  [the longest x12 48.8 us: along_z(): return lax.ppermute(x, 'dp', [(i, j) for i, j in pairs if i ^ j == 2 * k])]
    dot_general x18 -> x0, local copies, waits for them, and re-layouts: 47.5 us -> none  [conv_weight_grad(): jnp.einsum('bhwk,bhwd->kd', patches(values), grad_low, preferred_element_...]
  transfers between devices with their start and end apart: 37 -> 25, of which waited for: 25 -> 9; matrix products, arithmetic and copies ran while one was open for 6% -> 1% of each run, Pallas kernels for 0% -> 21%
where the time goes in v2:
time: 399 us; the launch traced here: 396 us
  Pallas kernels  187 us (47%)
  waiting for transfers between devices  124 us (31%)
  starting transfers between devices  62.7 us (16%)
  between operations  14.9 us (4%)
  local copies, waits for them, and re-layouts  6.23 us (2%)
    pallas_call x4, Pallas kernels, call(): pl.pallas_call(lambda *refs: body(self.unpack(refs)), out_shape=self.outs...  160 us
    ppermute x12, waiting for transfers between devices, along_z(): return lax.ppermute(x, 'dp', [(i, j) for i, j in pairs if i ^ j == 2 * k])  59.4 us
    psum x1, waiting for transfers between devices, local_device(): lax.psum(own_terms, 'dp')  57.8 us
    ppermute x12, starting transfers between devices, along_z(): return lax.ppermute(x, 'dp', [(i, j) for i, j in pairs if i ^ j == 2 * k])  48.8 us
  transfers between devices with their start and end apart: 25, of which 9 were waited for; matrix products, arithmetic and copies ran while one was open for 1% of the time, Pallas kernels for 21%

profile of v2, /device:TPU:0, one launch (start us, length us, event | category | flops | bytes accessed | tf_op | source)
XLA Modules:
  0.0 396.1 jit_solution(12850440621691325362)
XLA Ops:
  7.3 1.3 dynamic-slice_bitcast_fusion.1
  8.6 0.5 collective-permute-start
  9.7 1.1 copy-done
  10.9 0.9 dynamic-slice_bitcast_fusion
  11.9 0.6 pad_add_fusion.place.refs_0_
  12.4 4.0 %pack_weights.1 = (bf16[10560,128]{1,0:T(8,128)(2,1)}, bf16[2,2640,128]{2,1,0:T(8,128)(2,1)}) custom-call(s32[4]{0:T(128)} %pad_add_fusion.place.refs_0_, bf16[4608,128]{1,0:T(8,128)(2,1)} %bitcast.65, bf16[1152,384]{1,0:T(8,128)(2,1)} %bitcast.66, bf16[192,384]{1,0:T(8,128)(2,1)} %bitcast.68, bf16[384,384]{1,0:T(8,128)(2,1)} %bitcast.67, ...), custom_call_target="tpu_custom_call" | custom-call | tf_op jit(solution)/shard_map/pack_weights/pallas_call | solution.py:562
  16.5 3.0 spread_images.2
  19.5 3.0 collective-permute-start.7
  22.5 1.5 collective-permute-start.9
  24.0 3.5 collective-permute-start.1
  27.5 5.3 %collective-permute-start.2 = (bf16[2,256,512]{2,1,0:T(8,128)(2,1)}, bf16[2,256,512]{2,1,0:T(8,128)(2,1)}, u32[]{:S(2)}, u32[]{:S(2)}) collective-permute-start(bf16[2,256,512]{2,1,0:T(8,128)(2,1)} %get-tuple-element.60), channel_id=1, source_target_pairs={{0,4},{1,5},{2,6},{5,1},{6,2},{7,3},{8,12},{9,13},{10,14},{13,9},{... | collective-permute-start | bytes 1572872 | tf_op jit(solution)/shard_map/ppermute | solution.py:1480
  32.8 2.1 collective-permute-start.3
  34.9 5.3 %collective-permute-done.1 = bf16[2,256,512]{2,1,0:T(8,128)(2,1)S(1)} collective-permute-done((bf16[2,256,512]{2,1,0:T(8,128)(2,1)}, bf16[2,256,512]{2,1,0:T(8,128)(2,1)S(1)}, u32[]{:S(2)}, u32[]{:S(2)}) %collective-permute-start.1) | collective-permute-done | bytes 524320 | tf_op jit(solution)/shard_map/ppermute | solution.py:1480
  40.2 9.7 %collective-permute-done.2 = bf16[2,256,512]{2,1,0:T(8,128)(2,1)} collective-permute-done((bf16[2,256,512]{2,1,0:T(8,128)(2,1)}, bf16[2,256,512]{2,1,0:T(8,128)(2,1)}, u32[]{:S(2)}, u32[]{:S(2)}) %collective-permute-start.2) | collective-permute-done | bytes 524320 | tf_op jit(solution)/shard_map/ppermute | solution.py:1480
  49.9 5.6 %collective-permute-done.3 = bf16[2,256,512]{2,1,0:T(8,128)(2,1)} collective-permute-done((bf16[2,256,512]{2,1,0:T(8,128)(2,1)}, bf16[2,256,512]{2,1,0:T(8,128)(2,1)}, u32[]{:S(2)}, u32[]{:S(2)}) %collective-permute-start.3) | collective-permute-done | bytes 524320 | tf_op jit(solution)/shard_map/ppermute | solution.py:1480
  55.5 3.0 spread_images.3
  58.5 14.0 %collective-permute-start.5 = (bf16[2,256,512]{2,1,0:T(8,128)(2,1)}, bf16[2,256,512]{2,1,0:T(8,128)(2,1)S(1)}, u32[]{:S(2)}, u32[]{:S(2)}) collective-permute-start(bf16[2,256,512]{2,1,0:T(8,128)(2,1)} %get-tuple-element.62), channel_id=1, source_target_pairs={{0,2},{1,3},{3,1},{4,6},{6,4},{7,5},{8,10},{9,11},{11,9},{12,14},{... | collective-permute-start | bytes 1572872 | tf_op jit(solution)/shard_map/ppermute | solution.py:1480
  72.5 2.2 relay_weights.1
  74.7 0.6 collective-permute-start.10
  75.3 0.5 collective-permute-start.13
  76.1 7.0 %collective-permute-done.5 = bf16[2,256,512]{2,1,0:T(8,128)(2,1)S(1)} collective-permute-done((bf16[2,256,512]{2,1,0:T(8,128)(2,1)}, bf16[2,256,512]{2,1,0:T(8,128)(2,1)S(1)}, u32[]{:S(2)}, u32[]{:S(2)}) %collective-permute-start.5) | collective-permute-done | bytes 524320 | tf_op jit(solution)/shard_map/ppermute | solution.py:1480
  83.1 3.6 collective-permute-start.6
  86.7 4.1 %collective-permute-done.10.refs_12_.refs_17_.refs_21_.refs_11_ = bf16[1,2640,128]{2,1,0:T(8,128)(2,1)S(1)} collective-permute-done((bf16[1,2640,128]{2,1,0:T(8,128)(2,1)}, bf16[1,2640,128]{2,1,0:T(8,128)(2,1)S(1)}, u32[]{:S(2)}, u32[]{:S(2)}) %collective-permute-start.10) | collective-permute-done | bytes 675872 | tf_op jit(solution)/shard_map/ppermute | solution.py:1452
  90.8 2.4 collective-permute-done.13.refs_16_.refs_21_.refs_25_.refs_15_
  93.1 1.9 collective-permute-done.6
  95.1 12.7 %collective-permute-start.15 = (bf16[2,256,512]{2,1,0:T(8,128)(2,1)}, bf16[2,256,512]{2,1,0:T(8,128)(2,1)}, u32[]{:S(2)}, u32[]{:S(2)}) collective-permute-start(bf16[2,256,512]{2,1,0:T(8,128)(2,1)} %get-tuple-element.70), channel_id=1, source_target_pairs={{0,6},{2,4},{3,5},{4,2},{5,3},{7,1},{8,14},{10,12},{11,13},{12,10}... | collective-permute-start | bytes 1572872 | tf_op jit(solution)/shard_map/ppermute | solution.py:1480
  107.8 0.8 copy-done.3
  108.6 0.9 copy-done.4
  109.5 19.2 %forward_0.1 = (bf16[2048,512]{1,0:T(8,128)(2,1)}, bf16[2048,192]{1,0:T(8,128)(2,1)}, bf16[1152,384]{1,0:T(8,128)(2,1)}, bf16[2048,512]{1,0:T(8,128)(2,1)}, bf16...) custom-call(s32[4]{0:T(128)} %pad_add_fusion.place.refs_0_, bf16[512,512]{1,0:T(8,128)(2,1)} %bitcast.55, ...), custom_call_target="tpu_custom_call" | custom-call | flops 1 | bytes 1 | tf_op jit(solution)/shard_map/forward_0/pallas_call | solution.py:1111
  128.7 100.8 %sections_1_3.1 = (bf16[512,512]{1,0:T(8,128)(2,1)}, bf16[512,512]{1,0:T(8,128)(2,1)}, bf16[512,512]{1,0:T(8,128)(2,1)}, bf16[512,512]{1,0:T(8,128)(2,1)}, bf16[...) custom-call(s32[4]{0:T(128)} %pad_add_fusion.place.refs_0_, ...), custom_call_target="tpu_custom_call", output_to_operand_aliasing={{0}: (6, {}), {1}: (7, {}), {2}: (8, {}), {3}: (9, {})} | custom-call | flops 48000000000 | bytes 20000000 | tf_op jit(solution)/shard_map/sections_1_3/pallas_call | solution.py:1111
  229.5 1.3 collective-permute-start.16
  230.8 1.3 collective-permute-start.17
  232.1 1.3 collective-permute-start.18
  233.4 27.4 %backward_0_norms.1 = (bf16[2048,512]{1,0:T(8,128)(2,1)}, bf16[2048,192]{1,0:T(8,128)(2,1)}, bf16[10560,128]{1,0:T(8,128)(2,1)}) custom-call(s32[4]{0:T(128)} %pad_add_fusion.place.refs_0_, bf16[512,512]{1,0:T(8,128)(2,1)} %get-tuple-element.75.refs_1_, bf16[512,512]{1,0:T(8,128)(2,1)} %get-tuple-element.76.refs_2_, ...), custom_call_target="tpu_custom_call", output_to_operand_aliasing={{2}: (17, {})} | custom-call | flops 3200000000 | bytes 20000000 | tf_op jit(solution)/shard_map/backward_0_norms/pallas_call | solution.py:1111
  260.7 12.4 %backward_0_convs.1 = (bf16[512,512]{1,0:T(8,128)(2,1)}, bf16[512,512]{1,0:T(8,128)(2,1)}, bf16[512,512]{1,0:T(8,128)(2,1)}, bf16[512,512]{1,0:T(8,128)(2,1)}) custom-call(s32[4]{0:T(128)} %pad_add_fusion.place.refs_0_, bf16[2048,512]{1,0:T(8,128)(2,1)} %get-tuple-element.86.refs_1_, ...), custom_call_target="tpu_custom_call", output_to_operand_aliasing={{0}: (4, {}), {1}: (5, {}), {2}: (6, {}), {3}: (7, {})} | custom-call | flops 4800000000 | bytes 20000000 | tf_op jit(solution)/shard_map/backward_0_convs/pallas_call | solution.py:1111
  273.1 1.3 collective-permute-start.20
  274.4 1.3 collective-permute-start.21
  275.8 1.3 collective-permute-start.22
  277.1 2.0 second_images.2
  279.1 6.1 %collective-permute-start.19 = (bf16[4,256,512]{2,1,0:T(8,128)(2,1)}, bf16[4,256,512]{2,1,0:T(8,128)(2,1)}, u32[]{:S(2)}, u32[]{:S(2)}) collective-permute-start(bf16[4,256,512]{2,1,0:T(8,128)(2,1)} %second_images.2), channel_id=1, source_target_pairs={{0,1},{1,0},{2,3},{3,2},{4,5},{5,4},{6,7},{7,6},{8,9},{9,8},{10,11... | collective-permute-start | bytes 3145736 | tf_op jit(solution)/shard_map/ppermute | solution.py:1477
  285.2 29.9 %collective-permute-done.20.p1 = bf16[512,512]{1,0:T(8,128)(2,1)S(1)} collective-permute-done((bf16[512,512]{1,0:T(8,128)(2,1)}, bf16[512,512]{1,0:T(8,128)(2,1)S(1)}, u32[]{:S(2)}, u32[]{:S(2)}) %collective-permute-start.20) | collective-permute-done | bytes 524320 | tf_op jit(solution)/shard_map/ppermute | solution.py:1480
  315.1 0.8 copy-done.9
  316.2 2.0 second_images.3
  318.2 1.3 collective-permute-start.23
  319.5 57.8 %all-reduce.2.cloned.1.call-done.packed = bf16[10560,128]{1,0:T(8,128)(2,1)} async-done(((bf16[10560,128]{1,0:T(8,128)(2,1)}), bf16[10560,128]{1,0:T(8,128)(2,1)}) %all-reduce.2.cloned.1.call-update) | async-done | bytes 2703376 | tf_op jit(solution)/shard_map/psum | solution.py:1524
  377.2 4.2 %unpack_terms.1 = (f32[4608,128]{1,0:T(8,128)}, f32[1152,384]{1,0:T(8,128)}, f32[192,384]{1,0:T(8,128)}, f32[384,384]{1,0:T(8,128)}, f32[192,384]{1,0:T(8,128)}, /*index=5*/f32[1,1088]{1,0:T(1,128)}, f32[1,1088]{1,0:T(1,128)}) custom-call(bf16[10560,128]{1,0:T(8,128)(2,1)} %all-reduce.2.cloned.1.call-done.packed), custom_call_target="tpu_custom_call" | custom-call | tf_op jit(solution)/shard_map/unpack_terms/pallas_call | solution.py:613
  381.5 3.4 collect_images.2
  384.9 3.9 collect_images.3
  (51 shorter events, 1.4 us)
Async XLA Ops:
  7.2 1.9 copy-start.13
  7.2 2.1 copy-start.12
  7.2 370.0 %all-reduce.2.cloned.1.call-start = ((), (), s32[]{:S(2)}) async-start(), calls=%async_computation | async-start | bytes 5406720 | tf_op jit(solution)/shard_map/psum | solution.py:1524
  8.6 7.9 %collective-permute-start = (bf16[3,256,512]{2,1,0:T(8,128)(2,1)S(1)}, bf16[3,256,512]{2,1,0:T(8,128)(2,1)}, u32[]{:S(2)}, u32[]{:S(2)}) collective-permute-start(bf16[3,256,512]{2,1,0:T(8,128)(2,1)S(1)} %dynamic-slice_bitcast_fusion.1), channel_id=1, source_target_pairs={{0,1},{1,0},{2,3},{3,2},{4,5},{5,4},{6,7},{7,6},{8,9},{9,8},{10,11... | collective-permute-start | bytes 2359304 | tf_op jit(solution)/shard_map/ppermute | solution.py:1477
  9.7 1.1 copy-start
  11.8 21.0 %collective-permute-start.4 = (bf16[3,256,512]{2,1,0:T(8,128)(2,1)}, bf16[3,256,512]{2,1,0:T(8,128)(2,1)}, u32[]{:S(2)}, u32[]{:S(2)}) collective-permute-start(bf16[3,256,512]{2,1,0:T(8,128)(2,1)} %dynamic-slice_bitcast_fusion), channel_id=1, source_target_pairs={{0,1},{1,0},{2,3},{3,2},{4,5},{5,4},{6,7},{7,6},{8,9},{9,8},{10,11... | collective-permute-start | bytes 2359304 | tf_op jit(solution)/shard_map/ppermute | solution.py:1477
  19.5 53.0 %collective-permute-start.7 = (bf16[2,2640,128]{2,1,0:T(8,128)(2,1)}, bf16[2,2640,128]{2,1,0:T(8,128)(2,1)}, u32[]{:S(2)}, u32[]{:S(2)}) collective-permute-start(bf16[2,2640,128]{2,1,0:T(8,128)(2,1)} %get-tuple-element.65), channel_id=1, source_target_pairs={{8,0},{0,8},{24,16},{16,24},{9,1},{1,9},{25,17},{17,25},{10,2},{2,... | collective-permute-start | bytes 4055048 | tf_op jit(solution)/shard_map/ppermute | solution.py:1452
  22.5 50.0 %collective-permute-start.9 = (bf16[2,2640,128]{2,1,0:T(8,128)(2,1)}, bf16[2,2640,128]{2,1,0:T(8,128)(2,1)}, u32[]{:S(2)}, u32[]{:S(2)}) collective-permute-start(bf16[2,2640,128]{2,1,0:T(8,128)(2,1)} %get-tuple-element.65), channel_id=1, source_target_pairs={{16,0},{24,8},{0,16},{8,24},{17,1},{25,9},{1,17},{9,25},{18,2},{26... | collective-permute-start | bytes 4055048 | tf_op jit(solution)/shard_map/ppermute | solution.py:1452
  24.0 16.2 %collective-permute-start.1 = (bf16[2,256,512]{2,1,0:T(8,128)(2,1)}, bf16[2,256,512]{2,1,0:T(8,128)(2,1)S(1)}, u32[]{:S(2)}, u32[]{:S(2)}) collective-permute-start(bf16[2,256,512]{2,1,0:T(8,128)(2,1)} %get-tuple-element.59), channel_id=1, source_target_pairs={{0,2},{1,3},{3,1},{4,6},{6,4},{7,5},{8,10},{9,11},{11,9},{12,14},{... | collective-permute-start | bytes 1572872 | tf_op jit(solution)/shard_map/ppermute | solution.py:1480
  27.5 22.4 %collective-permute-start.2 = (bf16[2,256,512]{2,1,0:T(8,128)(2,1)}, bf16[2,256,512]{2,1,0:T(8,128)(2,1)}, u32[]{:S(2)}, u32[]{:S(2)}) collective-permute-start(bf16[2,256,512]{2,1,0:T(8,128)(2,1)} %get-tuple-element.60), channel_id=1, source_target_pairs={{0,4},{1,5},{2,6},{5,1},{6,2},{7,3},{8,12},{9,13},{10,14},{13,9},{... | collective-permute-start | bytes 1572872 | tf_op jit(solution)/shard_map/ppermute | solution.py:1480
  32.8 22.7 %collective-permute-start.3 = (bf16[2,256,512]{2,1,0:T(8,128)(2,1)}, bf16[2,256,512]{2,1,0:T(8,128)(2,1)}, u32[]{:S(2)}, u32[]{:S(2)}) collective-permute-start(bf16[2,256,512]{2,1,0:T(8,128)(2,1)} %get-tuple-element.61), channel_id=1, source_target_pairs={{0,6},{2,4},{3,5},{4,2},{5,3},{7,1},{8,14},{10,12},{11,13},{12,10}... | collective-permute-start | bytes 1572872 | tf_op jit(solution)/shard_map/ppermute | solution.py:1480
  40.2 15.3 %copy-start.5 = (bf16[2,256,512]{2,1,0:T(8,128)(2,1)}, bf16[2,256,512]{2,1,0:T(8,128)(2,1)S(1)}, u32[]{:S(2)}) copy-start(bf16[2,256,512]{2,1,0:T(8,128)(2,1)S(1)} %collective-permute-done.1) | copy-start | bytes 1572868
  58.5 24.6 %collective-permute-start.5 = (bf16[2,256,512]{2,1,0:T(8,128)(2,1)}, bf16[2,256,512]{2,1,0:T(8,128)(2,1)S(1)}, u32[]{:S(2)}, u32[]{:S(2)}) collective-permute-start(bf16[2,256,512]{2,1,0:T(8,128)(2,1)} %get-tuple-element.62), channel_id=1, source_target_pairs={{0,2},{1,3},{3,1},{4,6},{6,4},{7,5},{8,10},{9,11},{11,9},{12,14},{... | collective-permute-start | bytes 1572872 | tf_op jit(solution)/shard_map/ppermute | solution.py:1480
  74.7 16.0 %collective-permute-start.10 = (bf16[1,2640,128]{2,1,0:T(8,128)(2,1)}, bf16[1,2640,128]{2,1,0:T(8,128)(2,1)S(1)}, u32[]{:S(2)}, u32[]{:S(2)}) collective-permute-start(bf16[1,2640,128]{2,1,0:T(8,128)(2,1)} %get-tuple-element.67), channel_id=1, source_target_pairs={{8,0},{0,8},{24,16},{16,24},{9,1},{1,9},{25,17},{17,25},{10,2},{2,... | collective-permute-start | bytes 2027528 | tf_op jit(solution)/shard_map/ppermute | solution.py:1452
  75.3 32.4 %collective-permute-start.8 = (bf16[2,2640,128]{2,1,0:T(8,128)(2,1)}, bf16[2,2640,128]{2,1,0:T(8,128)(2,1)}, u32[]{:S(2)}, u32[]{:S(2)}) collective-permute-start(bf16[2,2640,128]{2,1,0:T(8,128)(2,1)} %collective-permute-done.7.refs_1_.refs_10_.refs_15_.refs_19_.refs_9_), channel_id=1, source_target_pairs={{0,1},{1,0},{2,3},{3,2},{4,5},{5,4},{6,7},{7,6},{8,9},{9,8},{10,11... | collective-permute-start | bytes 4055048 | tf_op jit(solution)/shard_map/ppermute | solution.py:1455
  75.3 17.8 %collective-permute-start.13 = (bf16[1,2640,128]{2,1,0:T(8,128)(2,1)}, bf16[1,2640,128]{2,1,0:T(8,128)(2,1)S(1)}, u32[]{:S(2)}, u32[]{:S(2)}) collective-permute-start(bf16[1,2640,128]{2,1,0:T(8,128)(2,1)} %get-tuple-element.68), channel_id=1, source_target_pairs={{16,0},{24,8},{0,16},{8,24},{17,1},{25,9},{1,17},{9,25},{18,2},{26... | collective-permute-start | bytes 2027528 | tf_op jit(solution)/shard_map/ppermute | solution.py:1452
  75.8 31.9 %collective-permute-start.12 = (bf16[2,2640,128]{2,1,0:T(8,128)(2,1)}, bf16[2,2640,128]{2,1,0:T(8,128)(2,1)}, u32[]{:S(2)}, u32[]{:S(2)}) collective-permute-start(bf16[2,2640,128]{2,1,0:T(8,128)(2,1)} %collective-permute-done.9.refs_0_.refs_14_.refs_19_.refs_23_.refs_13_), channel_id=1, source_target_pairs={{0,1},{1,0},{2,3},{3,2},{4,5},{5,4},{6,7},{7,6},{8,9},{9,8},{10,11... | collective-permute-start | bytes 4055048 | tf_op jit(solution)/shard_map/ppermute | solution.py:1455
  83.1 26.4 %copy-start.6 = (bf16[2,256,512]{2,1,0:T(8,128)(2,1)}, bf16[2,256,512]{2,1,0:T(8,128)(2,1)S(1)}, u32[]{:S(2)}) copy-start(bf16[2,256,512]{2,1,0:T(8,128)(2,1)S(1)} %collective-permute-done.5) | copy-start | bytes 1572868
  83.1 11.9 %collective-permute-start.6 = (bf16[2,256,512]{2,1,0:T(8,128)(2,1)}, bf16[2,256,512]{2,1,0:T(8,128)(2,1)S(1)}, u32[]{:S(2)}, u32[]{:S(2)}) collective-permute-start(bf16[2,256,512]{2,1,0:T(8,128)(2,1)} %get-tuple-element.63), channel_id=1, source_target_pairs={{0,4},{1,5},{2,6},{5,1},{6,2},{7,3},{8,12},{9,13},{10,14},{13,9},{... | collective-permute-start | bytes 1572872 | tf_op jit(solution)/shard_map/ppermute | solution.py:1480
  90.8 18.7 %copy-start.1 = (bf16[1,2640,128]{2,1,0:T(8,128)(2,1)}, bf16[1,2640,128]{2,1,0:T(8,128)(2,1)S(1)}, u32[]{:S(2)}) copy-start(bf16[1,2640,128]{2,1,0:T(8,128)(2,1)S(1)} %collective-permute-done.10.refs_12_.refs_17_.refs_21_.refs_11_) | copy-start | bytes 2027524
  90.8 17.0 %collective-permute-start.11 = (bf16[1,2640,128]{2,1,0:T(8,128)(2,1)S(1)}, bf16[1,2640,128]{2,1,0:T(8,128)(2,1)S(1)}, u32[]{:S(2)}, u32[]{:S(2)}) collective-permute-start(bf16[1,2640,128]{2,1,0:T(8,128)(2,1)S(1)} %collective-permute-done.10.refs_12_.refs_17_.refs_21_.refs_11_), channel_id=1, source_target_pairs={{0,1},{1,0},{2,3},{3,2},{4,5},{5,4},{6,7},{7,6},{8,9},{9,8},{10,11... | collective-permute-start | bytes 2027528 | tf_op jit(solution)/shard_map/ppermute | solution.py:1455
  93.1 14.6 %copy-start.2 = (bf16[1,2640,128]{2,1,0:T(8,128)(2,1)}, bf16[1,2640,128]{2,1,0:T(8,128)(2,1)S(1)}, u32[]{:S(2)}) copy-start(bf16[1,2640,128]{2,1,0:T(8,128)(2,1)S(1)} %collective-permute-done.13.refs_16_.refs_21_.refs_25_.refs_15_) | copy-start | bytes 2027524
  93.1 14.6 %collective-permute-start.14 = (bf16[1,2640,128]{2,1,0:T(8,128)(2,1)S(1)}, bf16[1,2640,128]{2,1,0:T(8,128)(2,1)S(1)}, u32[]{:S(2)}, u32[]{:S(2)}) collective-permute-start(bf16[1,2640,128]{2,1,0:T(8,128)(2,1)S(1)} %collective-permute-done.13.refs_16_.refs_21_.refs_25_.refs_15_), channel_id=1, source_target_pairs={{0,1},{1,0},{2,3},{3,2},{4,5},{5,4},{6,7},{7,6},{8,9},{9,8},{10,11... | collective-permute-start | bytes 2027528 | tf_op jit(solution)/shard_map/ppermute | solution.py:1455
  95.0 14.5 %copy-start.7 = (bf16[2,256,512]{2,1,0:T(8,128)(2,1)}, bf16[2,256,512]{2,1,0:T(8,128)(2,1)S(1)}, u32[]{:S(2)}) copy-start(bf16[2,256,512]{2,1,0:T(8,128)(2,1)S(1)} %collective-permute-done.6) | copy-start | bytes 1572868
  95.1 33.6 %collective-permute-start.15 = (bf16[2,256,512]{2,1,0:T(8,128)(2,1)}, bf16[2,256,512]{2,1,0:T(8,128)(2,1)}, u32[]{:S(2)}, u32[]{:S(2)}) collective-permute-start(bf16[2,256,512]{2,1,0:T(8,128)(2,1)} %get-tuple-element.70), channel_id=1, source_target_pairs={{0,6},{2,4},{3,5},{4,2},{5,3},{7,1},{8,14},{10,12},{11,13},{12,10}... | collective-permute-start | bytes 1572872 | tf_op jit(solution)/shard_map/ppermute | solution.py:1480
  107.8 0.9 copy-start.3
  108.6 0.9 copy-start.4
  229.5 46.3 %collective-permute-start.16 = (bf16[512,512]{1,0:T(8,128)(2,1)}, bf16[512,512]{1,0:T(8,128)(2,1)S(1)}, u32[]{:S(2)}, u32[]{:S(2)}) collective-permute-start(bf16[512,512]{1,0:T(8,128)(2,1)} %get-tuple-element.72), channel_id=1, source_target_pairs={{2,0},{3,1},{1,3},{6,4},{4,6},{5,7},{10,8},{11,9},{9,11},{14,12},{... | collective-permute-start | bytes 1572872 | tf_op jit(solution)/shard_map/ppermute | solution.py:1480
  230.8 46.3 %collective-permute-start.17 = (bf16[512,512]{1,0:T(8,128)(2,1)}, bf16[512,512]{1,0:T(8,128)(2,1)}, u32[]{:S(2)}, u32[]{:S(2)}) collective-permute-start(bf16[512,512]{1,0:T(8,128)(2,1)} %get-tuple-element.73), channel_id=1, source_target_pairs={{4,0},{5,1},{6,2},{1,5},{2,6},{3,7},{12,8},{13,9},{14,10},{9,13},{... | collective-permute-start | bytes 1572872 | tf_op jit(solution)/shard_map/ppermute | solution.py:1480
  232.1 45.0 %collective-permute-start.18 = (bf16[512,512]{1,0:T(8,128)(2,1)}, bf16[512,512]{1,0:T(8,128)(2,1)}, u32[]{:S(2)}, u32[]{:S(2)}) collective-permute-start(bf16[512,512]{1,0:T(8,128)(2,1)} %get-tuple-element.74), channel_id=1, source_target_pairs={{6,0},{4,2},{5,3},{2,4},{3,5},{1,7},{14,8},{12,10},{13,11},{10,12}... | collective-permute-start | bytes 1572872 | tf_op jit(solution)/shard_map/ppermute | solution.py:1480
  273.1 41.9 %collective-permute-start.20 = (bf16[512,512]{1,0:T(8,128)(2,1)}, bf16[512,512]{1,0:T(8,128)(2,1)S(1)}, u32[]{:S(2)}, u32[]{:S(2)}) collective-permute-start(bf16[512,512]{1,0:T(8,128)(2,1)} %get-tuple-element.94), channel_id=1, source_target_pairs={{2,0},{3,1},{1,3},{6,4},{4,6},{5,7},{10,8},{11,9},{9,11},{14,12},{... | collective-permute-start | bytes 1572872 | tf_op jit(solution)/shard_map/ppermute | solution.py:1480
  274.4 40.7 %collective-permute-start.21 = (bf16[512,512]{1,0:T(8,128)(2,1)}, bf16[512,512]{1,0:T(8,128)(2,1)S(1)}, u32[]{:S(2)}, u32[]{:S(2)}) collective-permute-start(bf16[512,512]{1,0:T(8,128)(2,1)} %get-tuple-element.95), channel_id=1, source_target_pairs={{4,0},{5,1},{6,2},{1,5},{2,6},{3,7},{12,8},{13,9},{14,10},{9,13},{... | collective-permute-start | bytes 1572872 | tf_op jit(solution)/shard_map/ppermute | solution.py:1480
  275.7 1.4 copy-start.8
  275.8 39.3 %collective-permute-start.22 = (bf16[512,512]{1,0:T(8,128)(2,1)}, bf16[512,512]{1,0:T(8,128)(2,1)S(1)}, u32[]{:S(2)}, u32[]{:S(2)}) collective-permute-start(bf16[512,512]{1,0:T(8,128)(2,1)} %get-tuple-element.96), channel_id=1, source_target_pairs={{6,0},{4,2},{5,3},{2,4},{3,5},{1,7},{14,8},{12,10},{13,11},{10,12}... | collective-permute-start | bytes 1572872 | tf_op jit(solution)/shard_map/ppermute | solution.py:1480
  279.1 102.4 %collective-permute-start.19 = (bf16[4,256,512]{2,1,0:T(8,128)(2,1)}, bf16[4,256,512]{2,1,0:T(8,128)(2,1)}, u32[]{:S(2)}, u32[]{:S(2)}) collective-permute-start(bf16[4,256,512]{2,1,0:T(8,128)(2,1)} %second_images.2), channel_id=1, source_target_pairs={{0,1},{1,0},{2,3},{3,2},{4,5},{5,4},{6,7},{7,6},{8,9},{9,8},{10,11... | collective-permute-start | bytes 3145736 | tf_op jit(solution)/shard_map/ppermute | solution.py:1477
  315.1 0.8 copy-start.9
  315.1 1.0 copy-start.10
  315.1 1.1 copy-start.11
  318.2 66.7 %collective-permute-start.23 = (bf16[4,256,512]{2,1,0:T(8,128)(2,1)}, bf16[4,256,512]{2,1,0:T(8,128)(2,1)}, u32[]{:S(2)}, u32[]{:S(2)}) collective-permute-start(bf16[4,256,512]{2,1,0:T(8,128)(2,1)} %second_images.3), channel_id=1, source_target_pairs={{0,1},{1,0},{2,3},{3,2},{4,5},{5,4},{6,7},{7,6},{8,9},{9,8},{10,11... | collective-permute-start | bytes 3145736 | tf_op jit(solution)/shard_map/ppermute | solution.py:1477
Sparse Core Ops, SparseCore 0:
  277.2 99.9 all-reduce.1

commit v3 on v2

--- a/solution.py
+++ b/solution.py
@@ -596,7 +596,8 @@
     )(y1, x1, *after)
 
 
-def unpack_kernel(packed, local, cross, reduce_w, spectral, expand, gains, biases):
+def unpack_kernel(packed, *refs):
+    local, cross, reduce_w, spectral, expand, gains, biases = refs[-7:]
     local[...] = get_terms(packed, "local", CL)
     cross[...] = get_terms(packed, "cross", CG)
     reduce_w[...] = get_terms(packed, "reduce", CG)
@@ -607,17 +608,17 @@
     gains[...] = rows[1:2]
 
 
-def unpack_call(packed):
+def unpack_call(packed, after):
     shape = jax.ShapeDtypeStruct
     dims = ((9 * CH, CL), (9 * CL, CG), (CS, CG), (CG, CG), (CS, CG), (1, NORMS), (1, NORMS))
     return pl.pallas_call(
         unpack_kernel,
         out_shape=[shape(d, F32) for d in dims],
-        in_specs=[VMEM],
+        in_specs=[VMEM] + [ANY] * len(after),
         out_specs=[VMEM] * 7,
         name="unpack_terms",
         compiler_params=pltpu.CompilerParams(vmem_limit_bytes=VMEM_LIMIT),
-    )(packed)
+    )(packed, *after)
 
 
 def spread_kernel(batches, place, images, other, *refs):
@@ -1510,7 +1511,7 @@
     weighting = 0.25 + hole_float * pixels / (hole_counts + pixels / 8.0)
     seed = (cotangent.astype(F32) * weighting[..., None]).astype(BF)
 
-    seeds, *_ = to_batches(seed.reshape(batches, pixels, channels), after=inputs[1:])
+    seeds, *_ = to_batches(seed.reshape(batches, pixels, channels))
     arrived = exchange_weights(send, seeds[:1])
     first = first_call(place, inputs, own, arrived, mf, mi, seeds[1:3], side, dp_size)
     middle = middle_call(place, first.out, inputs, seeds, own, arrived, (mf, mi, mft, mit), side, dp_size)
@@ -1521,7 +1522,9 @@
     own_grad = last_convs_call(place, back, middle.grad1, middle.own_grad, own, arrived, side, dp_size).own_grad
     own_terms = back.own_terms
     input_grads = to_images(own_grad, F32)
-    local, cross, reduce_w, spectral, expand, gain, bias = unpack_call(lax.psum(own_terms, "dp"))
+    local, cross, reduce_w, spectral, expand, gain, bias = unpack_call(
+        lax.psum(own_terms, "dp"), (activations, input_grads)
+    )
     return (
         activations,
         input_grads,

time: 399 us -> 378 us (0.947)
  starting transfers between devices: 62.7 us -> 51.7 us
  waiting for transfers between devices: 124 us -> 114 us
    ppermute x12, starting transfers between devices: 48.8 us -> 38.8 us  [along_z(): return lax.ppermute(x, 'dp', [(i, j) for i, j in pairs if i ^ j == 2 * k])]
    ppermute x12, waiting for transfers between devices: 59.4 us -> 49.6 us  [along_z(): return lax.ppermute(x, 'dp', [(i, j) for i, j in pairs if i ^ j == 2 * k])]
    ppermute x4, waiting for transfers between devices: 6.44 us -> 15.3 us  [over(): return lax.ppermute(x, 'pipe', [(i ^ bit, i) for i in range(4)])]
    psum x1, waiting for transfers between devices: 57.8 us -> 49 us  [local_device(): lax.psum(own_terms, 'dp')]
  transfers between devices with their start and end apart: 25 -> 25, of which waited for: 9 -> 7; matrix products, arithmetic and copies ran while one was open for 1% -> 1% of each run, Pallas kernels for 21% -> 21%
where the time goes in v3:
time: 378 us; the launch traced here: 375 us
  Pallas kernels  187 us (49%)
  waiting for transfers between devices  114 us (30%)
  starting transfers between devices  51.7 us (14%)
  between operations  14.9 us (4%)
  local copies, waits for them, and re-layouts  4.13 us (1%)
    pallas_call x4, Pallas kernels, call(): pl.pallas_call(lambda *refs: body(self.unpack(refs)), out_shape=self.outs...  160 us
    ppermute x12, waiting for transfers between devices, along_z(): return lax.ppermute(x, 'dp', [(i, j) for i, j in pairs if i ^ j == 2 * k])  49.6 us
    psum x1, waiting for transfers between devices, local_device(): lax.psum(own_terms, 'dp')  49 us
    ppermute x12, starting transfers between devices, along_z(): return lax.ppermute(x, 'dp', [(i, j) for i, j in pairs if i ^ j == 2 * k])  38.8 us
    ppermute x4, waiting for transfers between devices, over(): return lax.ppermute(x, 'pipe', [(i ^ bit, i) for i in range(4)])  15.3 us
  transfers between devices with their start and end apart: 25, of which 7 were waited for; matrix products, arithmetic and copies ran while one was open for 1% of the time, Pallas kernels for 21%

profile of v3, /device:TPU:0, one launch (start us, length us, event | category | flops | bytes accessed | tf_op | source)
XLA Modules:
  0.0 374.8 jit_solution(8137195290232035495)
XLA Ops:
  7.2 1.2 dynamic-slice_bitcast_fusion.1
  8.4 0.5 collective-permute-start
  9.0 0.7 pad_add_fusion.place.refs_0_
  9.6 4.0 %pack_weights.1 = (bf16[10560,128]{1,0:T(8,128)(2,1)}, bf16[2,2640,128]{2,1,0:T(8,128)(2,1)}) custom-call(s32[4]{0:T(128)} %pad_add_fusion.place.refs_0_, bf16[4608,128]{1,0:T(8,128)(2,1)} %bitcast.59, bf16[1152,384]{1,0:T(8,128)(2,1)} %bitcast.60, bf16[192,384]{1,0:T(8,128)(2,1)} %bitcast.62, bf16[384,384]{1,0:T(8,128)(2,1)} %bitcast.61, ...), custom_call_target="tpu_custom_call" | custom-call | tf_op jit(solution)/shard_map/pack_weights/pallas_call | solution.py:562
  13.7 0.1 convert_reduce_fusion
  13.9 3.0 spread_images.2
  16.9 2.6 collective-permute-start.7
  19.5 1.8 multiply_convert_fusion
  21.3 1.6 collective-permute-start.9
  23.0 4.3 %collective-permute-start.1 = (bf16[2,256,512]{2,1,0:T(8,128)(2,1)}, bf16[2,256,512]{2,1,0:T(8,128)(2,1)}, u32[]{:S(2)}, u32[]{:S(2)}) collective-permute-start(bf16[2,256,512]{2,1,0:T(8,128)(2,1)} %get-tuple-element.59), channel_id=1, source_target_pairs={{0,2},{1,3},{3,1},{4,6},{6,4},{7,5},{8,10},{9,11},{11,9},{12,14},{... | collective-permute-start | bytes 1572872 | tf_op jit(solution)/shard_map/ppermute | solution.py:1481
  27.3 4.5 %collective-permute-start.2 = (bf16[2,256,512]{2,1,0:T(8,128)(2,1)}, bf16[2,256,512]{2,1,0:T(8,128)(2,1)}, u32[]{:S(2)}, u32[]{:S(2)}) collective-permute-start(bf16[2,256,512]{2,1,0:T(8,128)(2,1)} %get-tuple-element.60), channel_id=1, source_target_pairs={{0,4},{1,5},{2,6},{5,1},{6,2},{7,3},{8,12},{9,13},{10,14},{13,9},{... | collective-permute-start | bytes 1572872 | tf_op jit(solution)/shard_map/ppermute | solution.py:1481
  31.8 2.1 collective-permute-start.3
  33.9 3.0 spread_images.3
  37.0 13.2 %collective-permute-done.7.refs_1_.refs_10_.refs_15_.refs_19_.refs_9_ = bf16[2,2640,128]{2,1,0:T(8,128)(2,1)} collective-permute-done((bf16[2,2640,128]{2,1,0:T(8,128)(2,1)}, bf16[2,2640,128]{2,1,0:T(8,128)(2,1)}, u32[]{:S(2)}, u32[]{:S(2)}) %collective-permute-start.7) | collective-permute-done | bytes 1351712 | tf_op jit(solution)/shard_map/ppermute | solution.py:1453
  50.1 3.7 %collective-permute-start.5 = (bf16[2,256,512]{2,1,0:T(8,128)(2,1)}, bf16[2,256,512]{2,1,0:T(8,128)(2,1)S(1)}, u32[]{:S(2)}, u32[]{:S(2)}) collective-permute-start(bf16[2,256,512]{2,1,0:T(8,128)(2,1)} %get-tuple-element.62), channel_id=1, source_target_pairs={{0,2},{1,3},{3,1},{4,6},{6,4},{7,5},{8,10},{9,11},{11,9},{12,14},{... | collective-permute-start | bytes 1572872 | tf_op jit(solution)/shard_map/ppermute | solution.py:1481
  53.9 2.2 relay_weights.1
  56.1 1.6 collective-permute-start.10
  57.6 1.5 collective-permute-start.13
  59.2 0.5 collective-permute-start.12
  59.7 7.1 %collective-permute-done.5 = bf16[2,256,512]{2,1,0:T(8,128)(2,1)S(1)} collective-permute-done((bf16[2,256,512]{2,1,0:T(8,128)(2,1)}, bf16[2,256,512]{2,1,0:T(8,128)(2,1)S(1)}, u32[]{:S(2)}, u32[]{:S(2)}) %collective-permute-start.5) | collective-permute-done | bytes 524320 | tf_op jit(solution)/shard_map/ppermute | solution.py:1481
  66.8 5.0 %collective-permute-start.6 = (bf16[2,256,512]{2,1,0:T(8,128)(2,1)}, bf16[2,256,512]{2,1,0:T(8,128)(2,1)S(1)}, u32[]{:S(2)}, u32[]{:S(2)}) collective-permute-start(bf16[2,256,512]{2,1,0:T(8,128)(2,1)} %get-tuple-element.63), channel_id=1, source_target_pairs={{0,4},{1,5},{2,6},{5,1},{6,2},{7,3},{8,12},{9,13},{10,14},{13,9},{... | collective-permute-start | bytes 1572872 | tf_op jit(solution)/shard_map/ppermute | solution.py:1481
  71.8 1.0 collective-permute-done.10.refs_12_.refs_17_.refs_21_.refs_11_
  72.8 1.2 collective-permute-done.13.refs_16_.refs_21_.refs_25_.refs_15_
  74.0 9.9 %collective-permute-done.6 = bf16[2,256,512]{2,1,0:T(8,128)(2,1)S(1)} collective-permute-done((bf16[2,256,512]{2,1,0:T(8,128)(2,1)}, bf16[2,256,512]{2,1,0:T(8,128)(2,1)S(1)}, u32[]{:S(2)}, u32[]{:S(2)}) %collective-permute-start.6) | collective-permute-done | bytes 524320 | tf_op jit(solution)/shard_map/ppermute | solution.py:1481
  83.9 11.4 %collective-permute-start.15 = (bf16[2,256,512]{2,1,0:T(8,128)(2,1)}, bf16[2,256,512]{2,1,0:T(8,128)(2,1)}, u32[]{:S(2)}, u32[]{:S(2)}) collective-permute-start(bf16[2,256,512]{2,1,0:T(8,128)(2,1)} %get-tuple-element.70), channel_id=1, source_target_pairs={{0,6},{2,4},{3,5},{4,2},{5,3},{7,1},{8,14},{10,12},{11,13},{12,10}... | collective-permute-start | bytes 1572872 | tf_op jit(solution)/shard_map/ppermute | solution.py:1481
  95.4 0.8 copy-done.3
  96.2 0.9 copy-done.4
  97.1 19.1 %forward_0.1 = (bf16[2048,512]{1,0:T(8,128)(2,1)}, bf16[2048,192]{1,0:T(8,128)(2,1)}, bf16[1152,384]{1,0:T(8,128)(2,1)}, bf16[2048,512]{1,0:T(8,128)(2,1)}, bf16...) custom-call(s32[4]{0:T(128)} %pad_add_fusion.place.refs_0_, bf16[512,512]{1,0:T(8,128)(2,1)} %bitcast.50, ...), custom_call_target="tpu_custom_call" | custom-call | flops 1 | bytes 1 | tf_op jit(solution)/shard_map/forward_0/pallas_call | solution.py:1112
  116.3 100.8 %sections_1_3.1 = (bf16[512,512]{1,0:T(8,128)(2,1)}, bf16[512,512]{1,0:T(8,128)(2,1)}, bf16[512,512]{1,0:T(8,128)(2,1)}, bf16[512,512]{1,0:T(8,128)(2,1)}, bf16[...) custom-call(s32[4]{0:T(128)} %pad_add_fusion.place.refs_0_, ...), custom_call_target="tpu_custom_call", output_to_operand_aliasing={{0}: (6, {}), {1}: (7, {}), {2}: (8, {}), {3}: (9, {})} | custom-call | flops 48000000000 | bytes 20000000 | tf_op jit(solution)/shard_map/sections_1_3/pallas_call | solution.py:1112
  217.0 1.3 collective-permute-start.16
  218.3 1.3 collective-permute-start.17
  219.6 1.3 collective-permute-start.18
  220.9 27.4 %backward_0_norms.1 = (bf16[2048,512]{1,0:T(8,128)(2,1)}, bf16[2048,192]{1,0:T(8,128)(2,1)}, bf16[10560,128]{1,0:T(8,128)(2,1)}) custom-call(s32[4]{0:T(128)} %pad_add_fusion.place.refs_0_, bf16[512,512]{1,0:T(8,128)(2,1)} %get-tuple-element.75.refs_1_, bf16[512,512]{1,0:T(8,128)(2,1)} %get-tuple-element.76.refs_2_, ...), custom_call_target="tpu_custom_call", output_to_operand_aliasing={{2}: (17, {})} | custom-call | flops 3200000000 | bytes 20000000 | tf_op jit(solution)/shard_map/backward_0_norms/pallas_call | solution.py:1112
  248.3 12.4 %backward_0_convs.1 = (bf16[512,512]{1,0:T(8,128)(2,1)}, bf16[512,512]{1,0:T(8,128)(2,1)}, bf16[512,512]{1,0:T(8,128)(2,1)}, bf16[512,512]{1,0:T(8,128)(2,1)}) custom-call(s32[4]{0:T(128)} %pad_add_fusion.place.refs_0_, bf16[2048,512]{1,0:T(8,128)(2,1)} %get-tuple-element.86.refs_1_, ...), custom_call_target="tpu_custom_call", output_to_operand_aliasing={{0}: (4, {}), {1}: (5, {}), {2}: (6, {}), {3}: (7, {})} | custom-call | flops 4800000000 | bytes 20000000 | tf_op jit(solution)/shard_map/backward_0_convs/pallas_call | solution.py:1112
  260.7 1.3 collective-permute-start.20
  262.0 1.3 collective-permute-start.21
  263.3 1.3 collective-permute-start.22
  264.7 2.0 second_images.2
  266.7 4.5 %collective-permute-start.19 = (bf16[4,256,512]{2,1,0:T(8,128)(2,1)}, bf16[4,256,512]{2,1,0:T(8,128)(2,1)}, u32[]{:S(2)}, u32[]{:S(2)}) collective-permute-start(bf16[4,256,512]{2,1,0:T(8,128)(2,1)} %second_images.2), channel_id=1, source_target_pairs={{0,1},{1,0},{2,3},{3,2},{4,5},{5,4},{6,7},{7,6},{8,9},{9,8},{10,11... | collective-permute-start | bytes 3145736 | tf_op jit(solution)/shard_map/ppermute | solution.py:1478
  271.2 32.5 %collective-permute-done.20.p1 = bf16[512,512]{1,0:T(8,128)(2,1)S(1)} collective-permute-done((bf16[512,512]{1,0:T(8,128)(2,1)}, bf16[512,512]{1,0:T(8,128)(2,1)S(1)}, u32[]{:S(2)}, u32[]{:S(2)}) %collective-permute-start.20) | collective-permute-done | bytes 524320 | tf_op jit(solution)/shard_map/ppermute | solution.py:1481
  303.7 0.8 copy-done.8
  304.5 0.2 copy-done.9
  304.7 0.2 copy-done.10
  304.8 2.0 second_images.3
  306.9 3.4 collect_images.2
  310.3 3.9 %collect_images.3 = f32[6,256,512]{2,1,0:T(8,128)} custom-call(s32[4]{0:T(128)} %pad_add_fusion.place.refs_0_, bf16[512,512]{1,0:T(8,128)(2,1)} %get-tuple-element.93.p0, bf16[512,512]{1,0:T(8,128)(2,1)} %copy-done.8, bf16[512,512]{1,0:T(8,128)(2,1)} %copy-done.9, bf16[512,512]{1,0:T(8,128)(2,1)} %copy-done.10, ...), custom_call_target="tpu_custom_call" | custom-call | tf_op jit(solution)/shard_map/collect_images/pallas_call | solution.py:705
  314.3 49.0 %all-reduce.2.cloned.1.call-done.packed = bf16[10560,128]{1,0:T(8,128)(2,1)} async-done(((bf16[10560,128]{1,0:T(8,128)(2,1)}), bf16[10560,128]{1,0:T(8,128)(2,1)}) %all-reduce.2.cloned.1.call-update) | async-done | bytes 2703376 | tf_op jit(solution)/shard_map/psum | solution.py:1526
  363.3 4.2 %unpack_terms.1 = (f32[4608,128]{1,0:T(8,128)}, f32[1152,384]{1,0:T(8,128)}, f32[192,384]{1,0:T(8,128)}, f32[384,384]{1,0:T(8,128)}, f32[192,384]{1,0:T(8,128)}, /*index=5*/f32[1,1088]{1,0:T(1,128)}, f32[1,1088]{1,0:T(1,128)}) custom-call(bf16[10560,128]{1,0:T(8,128)(2,1)} %all-reduce.2.cloned.1.call-done.packed, bf16[1,6,1,16,16,512]{5,4,3,2,1,0:T(8,128)(2,1)} %bitcast.46, ...), custom_call_target="tpu_custom_call" | custom-call | tf_op jit(solution)/shard_map/unpack_terms/pallas_call | solution.py:614
  (49 shorter events, 0.4 us)
Async XLA Ops:
  7.2 356.1 %all-reduce.2.cloned.1.call-start = ((), (), s32[]{:S(2)}) async-start(), calls=%async_computation | async-start | bytes 5406720 | tf_op jit(solution)/shard_map/psum | solution.py:1526
  8.4 5.2 %copy-start.12 = (s32[6,1,16,16]{3,2,1,0:T(8,128)S(1)}, s32[6,1,16,16]{3,2,1,0:T(8,128)}, u32[]{:S(2)}) copy-start(s32[6,1,16,16]{3,2,1,0:T(8,128)} %param.23) | copy-start | bytes 18436
  8.4 5.4 %collective-permute-start = (bf16[3,256,512]{2,1,0:T(8,128)(2,1)S(1)}, bf16[3,256,512]{2,1,0:T(8,128)(2,1)}, u32[]{:S(2)}, u32[]{:S(2)}) collective-permute-start(bf16[3,256,512]{2,1,0:T(8,128)(2,1)S(1)} %dynamic-slice_bitcast_fusion.1), channel_id=1, source_target_pairs={{0,1},{1,0},{2,3},{3,2},{4,5},{5,4},{6,7},{7,6},{8,9},{9,8},{10,11... | collective-permute-start | bytes 2359304 | tf_op jit(solution)/shard_map/ppermute | solution.py:1478
  16.9 33.2 %collective-permute-start.7 = (bf16[2,2640,128]{2,1,0:T(8,128)(2,1)}, bf16[2,2640,128]{2,1,0:T(8,128)(2,1)}, u32[]{:S(2)}, u32[]{:S(2)}) collective-permute-start(bf16[2,2640,128]{2,1,0:T(8,128)(2,1)} %get-tuple-element.65), channel_id=1, source_target_pairs={{8,0},{0,8},{24,16},{16,24},{9,1},{1,9},{25,17},{17,25},{10,2},{2,... | collective-permute-start | bytes 4055048 | tf_op jit(solution)/shard_map/ppermute | solution.py:1453
  21.3 1.6 copy-start
  21.3 32.5 %collective-permute-start.9 = (bf16[2,2640,128]{2,1,0:T(8,128)(2,1)}, bf16[2,2640,128]{2,1,0:T(8,128)(2,1)}, u32[]{:S(2)}, u32[]{:S(2)}) collective-permute-start(bf16[2,2640,128]{2,1,0:T(8,128)(2,1)} %get-tuple-element.65), channel_id=1, source_target_pairs={{16,0},{24,8},{0,16},{8,24},{17,1},{25,9},{1,17},{9,25},{18,2},{26... | collective-permute-start | bytes 4055048 | tf_op jit(solution)/shard_map/ppermute | solution.py:1453
  23.0 8.9 %collective-permute-start.4 = (bf16[3,256,512]{2,1,0:T(8,128)(2,1)S(1)}, bf16[3,256,512]{2,1,0:T(8,128)(2,1)S(1)}, u32[]{:S(2)}, u32[]{:S(2)}) collective-permute-start(bf16[3,256,512]{2,1,0:T(8,128)(2,1)S(1)} %dynamic-slice_bitcast_fusion), channel_id=1, source_target_pairs={{0,1},{1,0},{2,3},{3,2},{4,5},{5,4},{6,7},{7,6},{8,9},{9,8},{10,11... | collective-permute-start | bytes 2359304 | tf_op jit(solution)/shard_map/ppermute | solution.py:1478
  23.0 34.6 %collective-permute-start.1 = (bf16[2,256,512]{2,1,0:T(8,128)(2,1)}, bf16[2,256,512]{2,1,0:T(8,128)(2,1)}, u32[]{:S(2)}, u32[]{:S(2)}) collective-permute-start(bf16[2,256,512]{2,1,0:T(8,128)(2,1)} %get-tuple-element.59), channel_id=1, source_target_pairs={{0,2},{1,3},{3,1},{4,6},{6,4},{7,5},{8,10},{9,11},{11,9},{12,14},{... | collective-permute-start | bytes 1572872 | tf_op jit(solution)/shard_map/ppermute | solution.py:1481
  27.3 31.8 %collective-permute-start.2 = (bf16[2,256,512]{2,1,0:T(8,128)(2,1)}, bf16[2,256,512]{2,1,0:T(8,128)(2,1)}, u32[]{:S(2)}, u32[]{:S(2)}) collective-permute-start(bf16[2,256,512]{2,1,0:T(8,128)(2,1)} %get-tuple-element.60), channel_id=1, source_target_pairs={{0,4},{1,5},{2,6},{5,1},{6,2},{7,3},{8,12},{9,13},{10,14},{13,9},{... | collective-permute-start | bytes 1572872 | tf_op jit(solution)/shard_map/ppermute | solution.py:1481
  31.8 2.1 copy-start.11
  31.8 27.3 %collective-permute-start.3 = (bf16[2,256,512]{2,1,0:T(8,128)(2,1)}, bf16[2,256,512]{2,1,0:T(8,128)(2,1)}, u32[]{:S(2)}, u32[]{:S(2)}) collective-permute-start(bf16[2,256,512]{2,1,0:T(8,128)(2,1)} %get-tuple-element.61), channel_id=1, source_target_pairs={{0,6},{2,4},{3,5},{4,2},{5,3},{7,1},{8,14},{10,12},{11,13},{12,10}... | collective-permute-start | bytes 1572872 | tf_op jit(solution)/shard_map/ppermute | solution.py:1481
  50.1 16.7 %collective-permute-start.5 = (bf16[2,256,512]{2,1,0:T(8,128)(2,1)}, bf16[2,256,512]{2,1,0:T(8,128)(2,1)S(1)}, u32[]{:S(2)}, u32[]{:S(2)}) collective-permute-start(bf16[2,256,512]{2,1,0:T(8,128)(2,1)} %get-tuple-element.62), channel_id=1, source_target_pairs={{0,2},{1,3},{3,1},{4,6},{6,4},{7,5},{8,10},{9,11},{11,9},{12,14},{... | collective-permute-start | bytes 1572872 | tf_op jit(solution)/shard_map/ppermute | solution.py:1481
  56.1 16.7 %collective-permute-start.10 = (bf16[1,2640,128]{2,1,0:T(8,128)(2,1)}, bf16[1,2640,128]{2,1,0:T(8,128)(2,1)S(1)}, u32[]{:S(2)}, u32[]{:S(2)}) collective-permute-start(bf16[1,2640,128]{2,1,0:T(8,128)(2,1)} %get-tuple-element.67), channel_id=1, source_target_pairs={{8,0},{0,8},{24,16},{16,24},{9,1},{1,9},{25,17},{17,25},{10,2},{2,... | collective-permute-start | bytes 2027528 | tf_op jit(solution)/shard_map/ppermute | solution.py:1453
  57.6 16.4 %collective-permute-start.13 = (bf16[1,2640,128]{2,1,0:T(8,128)(2,1)}, bf16[1,2640,128]{2,1,0:T(8,128)(2,1)S(1)}, u32[]{:S(2)}, u32[]{:S(2)}) collective-permute-start(bf16[1,2640,128]{2,1,0:T(8,128)(2,1)} %get-tuple-element.68), channel_id=1, source_target_pairs={{16,0},{24,8},{0,16},{8,24},{17,1},{25,9},{1,17},{9,25},{18,2},{26... | collective-permute-start | bytes 2027528 | tf_op jit(solution)/shard_map/ppermute | solution.py:1453
  59.2 36.2 %collective-permute-start.8 = (bf16[2,2640,128]{2,1,0:T(8,128)(2,1)}, bf16[2,2640,128]{2,1,0:T(8,128)(2,1)}, u32[]{:S(2)}, u32[]{:S(2)}) collective-permute-start(bf16[2,2640,128]{2,1,0:T(8,128)(2,1)} %collective-permute-done.7.refs_1_.refs_10_.refs_15_.refs_19_.refs_9_), channel_id=1, source_target_pairs={{0,1},{1,0},{2,3},{3,2},{4,5},{5,4},{6,7},{7,6},{8,9},{9,8},{10,11... | collective-permute-start | bytes 4055048 | tf_op jit(solution)/shard_map/ppermute | solution.py:1456
  59.2 36.2 %collective-permute-start.12 = (bf16[2,2640,128]{2,1,0:T(8,128)(2,1)}, bf16[2,2640,128]{2,1,0:T(8,128)(2,1)}, u32[]{:S(2)}, u32[]{:S(2)}) collective-permute-start(bf16[2,2640,128]{2,1,0:T(8,128)(2,1)} %collective-permute-done.9.refs_0_.refs_14_.refs_19_.refs_23_.refs_13_), channel_id=1, source_target_pairs={{0,1},{1,0},{2,3},{3,2},{4,5},{5,4},{6,7},{7,6},{8,9},{9,8},{10,11... | collective-permute-start | bytes 4055048 | tf_op jit(solution)/shard_map/ppermute | solution.py:1456
  66.8 30.3 %copy-start.5 = (bf16[2,256,512]{2,1,0:T(8,128)(2,1)}, bf16[2,256,512]{2,1,0:T(8,128)(2,1)S(1)}, u32[]{:S(2)}) copy-start(bf16[2,256,512]{2,1,0:T(8,128)(2,1)S(1)} %collective-permute-done.5) | copy-start | bytes 1572868
  66.8 17.1 %collective-permute-start.6 = (bf16[2,256,512]{2,1,0:T(8,128)(2,1)}, bf16[2,256,512]{2,1,0:T(8,128)(2,1)S(1)}, u32[]{:S(2)}, u32[]{:S(2)}) collective-permute-start(bf16[2,256,512]{2,1,0:T(8,128)(2,1)} %get-tuple-element.63), channel_id=1, source_target_pairs={{0,4},{1,5},{2,6},{5,1},{6,2},{7,3},{8,12},{9,13},{10,14},{13,9},{... | collective-permute-start | bytes 1572872 | tf_op jit(solution)/shard_map/ppermute | solution.py:1481
  72.8 24.3 %copy-start.1 = (bf16[1,2640,128]{2,1,0:T(8,128)(2,1)}, bf16[1,2640,128]{2,1,0:T(8,128)(2,1)S(1)}, u32[]{:S(2)}) copy-start(bf16[1,2640,128]{2,1,0:T(8,128)(2,1)S(1)} %collective-permute-done.10.refs_12_.refs_17_.refs_21_.refs_11_) | copy-start | bytes 2027524
  72.8 22.5 %collective-permute-start.11 = (bf16[1,2640,128]{2,1,0:T(8,128)(2,1)S(1)}, bf16[1,2640,128]{2,1,0:T(8,128)(2,1)S(1)}, u32[]{:S(2)}, u32[]{:S(2)}) collective-permute-start(bf16[1,2640,128]{2,1,0:T(8,128)(2,1)S(1)} %collective-permute-done.10.refs_12_.refs_17_.refs_21_.refs_11_), channel_id=1, source_target_pairs={{0,1},{1,0},{2,3},{3,2},{4,5},{5,4},{6,7},{7,6},{8,9},{9,8},{10,11... | collective-permute-start | bytes 2027528 | tf_op jit(solution)/shard_map/ppermute | solution.py:1456
  74.0 21.3 %copy-start.2 = (bf16[1,2640,128]{2,1,0:T(8,128)(2,1)}, bf16[1,2640,128]{2,1,0:T(8,128)(2,1)S(1)}, u32[]{:S(2)}) copy-start(bf16[1,2640,128]{2,1,0:T(8,128)(2,1)S(1)} %collective-permute-done.13.refs_16_.refs_21_.refs_25_.refs_15_) | copy-start | bytes 2027524
  74.0 21.4 %collective-permute-start.14 = (bf16[1,2640,128]{2,1,0:T(8,128)(2,1)S(1)}, bf16[1,2640,128]{2,1,0:T(8,128)(2,1)S(1)}, u32[]{:S(2)}, u32[]{:S(2)}) collective-permute-start(bf16[1,2640,128]{2,1,0:T(8,128)(2,1)S(1)} %collective-permute-done.13.refs_16_.refs_21_.refs_25_.refs_15_), channel_id=1, source_target_pairs={{0,1},{1,0},{2,3},{3,2},{4,5},{5,4},{6,7},{7,6},{8,9},{9,8},{10,11... | collective-permute-start | bytes 2027528 | tf_op jit(solution)/shard_map/ppermute | solution.py:1456
  83.9 13.2 %copy-start.6 = (bf16[2,256,512]{2,1,0:T(8,128)(2,1)}, bf16[2,256,512]{2,1,0:T(8,128)(2,1)S(1)}, u32[]{:S(2)}) copy-start(bf16[2,256,512]{2,1,0:T(8,128)(2,1)S(1)} %collective-permute-done.6) | copy-start | bytes 1572868
  83.9 32.3 %collective-permute-start.15 = (bf16[2,256,512]{2,1,0:T(8,128)(2,1)}, bf16[2,256,512]{2,1,0:T(8,128)(2,1)}, u32[]{:S(2)}, u32[]{:S(2)}) collective-permute-start(bf16[2,256,512]{2,1,0:T(8,128)(2,1)} %get-tuple-element.70), channel_id=1, source_target_pairs={{0,6},{2,4},{3,5},{4,2},{5,3},{7,1},{8,14},{10,12},{11,13},{12,10}... | collective-permute-start | bytes 1572872 | tf_op jit(solution)/shard_map/ppermute | solution.py:1481
  95.4 0.9 copy-start.3
  96.2 0.9 copy-start.4
  217.0 46.3 %collective-permute-start.16 = (bf16[512,512]{1,0:T(8,128)(2,1)}, bf16[512,512]{1,0:T(8,128)(2,1)S(1)}, u32[]{:S(2)}, u32[]{:S(2)}) collective-permute-start(bf16[512,512]{1,0:T(8,128)(2,1)} %get-tuple-element.72), channel_id=1, source_target_pairs={{2,0},{3,1},{1,3},{6,4},{4,6},{5,7},{10,8},{11,9},{9,11},{14,12},{... | collective-permute-start | bytes 1572872 | tf_op jit(solution)/shard_map/ppermute | solution.py:1481
  218.3 46.3 %collective-permute-start.17 = (bf16[512,512]{1,0:T(8,128)(2,1)}, bf16[512,512]{1,0:T(8,128)(2,1)}, u32[]{:S(2)}, u32[]{:S(2)}) collective-permute-start(bf16[512,512]{1,0:T(8,128)(2,1)} %get-tuple-element.73), channel_id=1, source_target_pairs={{4,0},{5,1},{6,2},{1,5},{2,6},{3,7},{12,8},{13,9},{14,10},{9,13},{... | collective-permute-start | bytes 1572872 | tf_op jit(solution)/shard_map/ppermute | solution.py:1481
  219.6 45.0 %collective-permute-start.18 = (bf16[512,512]{1,0:T(8,128)(2,1)}, bf16[512,512]{1,0:T(8,128)(2,1)}, u32[]{:S(2)}, u32[]{:S(2)}) collective-permute-start(bf16[512,512]{1,0:T(8,128)(2,1)} %get-tuple-element.74), channel_id=1, source_target_pairs={{6,0},{4,2},{5,3},{2,4},{3,5},{1,7},{14,8},{12,10},{13,11},{10,12}... | collective-permute-start | bytes 1572872 | tf_op jit(solution)/shard_map/ppermute | solution.py:1481
  260.7 43.0 %collective-permute-start.20 = (bf16[512,512]{1,0:T(8,128)(2,1)}, bf16[512,512]{1,0:T(8,128)(2,1)S(1)}, u32[]{:S(2)}, u32[]{:S(2)}) collective-permute-start(bf16[512,512]{1,0:T(8,128)(2,1)} %get-tuple-element.94), channel_id=1, source_target_pairs={{2,0},{3,1},{1,3},{6,4},{4,6},{5,7},{10,8},{11,9},{9,11},{14,12},{... | collective-permute-start | bytes 1572872 | tf_op jit(solution)/shard_map/ppermute | solution.py:1481
  262.0 41.7 %collective-permute-start.21 = (bf16[512,512]{1,0:T(8,128)(2,1)}, bf16[512,512]{1,0:T(8,128)(2,1)S(1)}, u32[]{:S(2)}, u32[]{:S(2)}) collective-permute-start(bf16[512,512]{1,0:T(8,128)(2,1)} %get-tuple-element.95), channel_id=1, source_target_pairs={{4,0},{5,1},{6,2},{1,5},{2,6},{3,7},{12,8},{13,9},{14,10},{9,13},{... | collective-permute-start | bytes 1572872 | tf_op jit(solution)/shard_map/ppermute | solution.py:1481
  263.3 1.4 copy-start.7
  263.3 40.4 %collective-permute-start.22 = (bf16[512,512]{1,0:T(8,128)(2,1)}, bf16[512,512]{1,0:T(8,128)(2,1)S(1)}, u32[]{:S(2)}, u32[]{:S(2)}) collective-permute-start(bf16[512,512]{1,0:T(8,128)(2,1)} %get-tuple-element.96), channel_id=1, source_target_pairs={{6,0},{4,2},{5,3},{2,4},{3,5},{1,7},{14,8},{12,10},{13,11},{10,12}... | collective-permute-start | bytes 1572872 | tf_op jit(solution)/shard_map/ppermute | solution.py:1481
  266.7 40.2 %collective-permute-start.19 = (bf16[4,256,512]{2,1,0:T(8,128)(2,1)}, bf16[4,256,512]{2,1,0:T(8,128)(2,1)}, u32[]{:S(2)}, u32[]{:S(2)}) collective-permute-start(bf16[4,256,512]{2,1,0:T(8,128)(2,1)} %second_images.2), channel_id=1, source_target_pairs={{0,1},{1,0},{2,3},{3,2},{4,5},{5,4},{6,7},{7,6},{8,9},{9,8},{10,11... | collective-permute-start | bytes 3145736 | tf_op jit(solution)/shard_map/ppermute | solution.py:1478
  303.7 0.8 copy-start.8
  303.7 1.0 copy-start.9
  303.7 1.1 copy-start.10
  306.8 3.5 collective-permute-start.23
Sparse Core Ops, SparseCore 0:
  264.8 98.4 all-reduce.1

commit v4 on v3

--- a/solution.py
+++ b/solution.py
@@ -1020,7 +1020,7 @@
             three_columns(v.xp, b, source[pl.ds(pl.multiple_of(b * pixels, pixels), pixels), 0:CL], column, side)
             return 0
 
-        lax.fori_loop(0, geo.images, columns, 0)
+        lax.fori_loop(0, geo.images, columns, 0, unroll=4)
 
         def one_row(dh, _):
             def gather(b, _):
@@ -1030,7 +1030,7 @@
                     v.taps[r, dw * CL : (dw + 1) * CL] = v.xp[2 - dw if flipped else dw, b, pl.ds(first, pixels)]
                 return 0
 
-            lax.fori_loop(0, geo.images, gather, 0)
+            lax.fori_loop(0, geo.images, gather, 0, unroll=4)
             product(dh)
             return 0
 
@@ -1440,7 +1440,7 @@
                 v.o[r] = (stack_cols([dxl, dxg]) + v.o[r].astype(F32)).astype(BF)
                 return 0
 
-            lax.fori_loop(0, geo.steps, step, 0)
+            lax.fori_loop(0, geo.steps, step, 0, unroll=UN)
             stores = part_copies(v.o, v.own_grad, v.osem)
             start_all(stores)
             wait_all(stores)

time: 378 us -> 367 us (0.971)
  Pallas kernels: 187 us -> 176 us
    pallas_call x4, Pallas kernels: 160 us -> 148 us  [call(): pl.pallas_call(lambda *refs: body(self.unpack(refs)), out_shape=self.outs...]
  transfers between devices with their start and end apart: 25 -> 25, of which waited for: 7 -> 7; matrix products, arithmetic and copies ran while one was open for 1% -> 1% of each run, Pallas kernels for 21% -> 22%
where the time goes in v4:
time: 367 us; the launch traced here: 363 us
  Pallas kernels  176 us (48%)
  waiting for transfers between devices  114 us (31%)
  starting transfers between devices  51.8 us (14%)
  between operations  14.6 us (4%)
  local copies, waits for them, and re-layouts  4.13 us (1%)
    pallas_call x4, Pallas kernels, call(): pl.pallas_call(lambda *refs: body(self.unpack(refs)), out_shape=self.outs...  148 us
    ppermute x12, waiting for transfers between devices, along_z(): return lax.ppermute(x, 'dp', [(i, j) for i, j in pairs if i ^ j == 2 * k])  49.6 us
    psum x1, waiting for transfers between devices, local_device(): lax.psum(own_terms, 'dp')  49 us
    ppermute x12, starting transfers between devices, along_z(): return lax.ppermute(x, 'dp', [(i, j) for i, j in pairs if i ^ j == 2 * k])  38.9 us
    ppermute x4, waiting for transfers between devices, over(): return lax.ppermute(x, 'pipe', [(i ^ bit, i) for i in range(4)])  15.3 us
  transfers between devices with their start and end apart: 25, of which 7 were waited for; matrix products, arithmetic and copies ran while one was open for 1% of the time, Pallas kernels for 22%

profile of v4, /device:TPU:0, one launch (start us, length us, event | category | flops | bytes accessed | tf_op | source)
XLA Modules:
  0.0 363.0 jit_solution(381404691119240890)
XLA Ops:
  7.2 1.2 dynamic-slice_bitcast_fusion.1
  8.4 0.5 collective-permute-start
  9.0 0.7 pad_add_fusion.place.refs_0_
  9.6 4.0 %pack_weights.1 = (bf16[10560,128]{1,0:T(8,128)(2,1)}, bf16[2,2640,128]{2,1,0:T(8,128)(2,1)}) custom-call(s32[4]{0:T(128)} %pad_add_fusion.place.refs_0_, bf16[4608,128]{1,0:T(8,128)(2,1)} %bitcast.59, bf16[1152,384]{1,0:T(8,128)(2,1)} %bitcast.60, bf16[192,384]{1,0:T(8,128)(2,1)} %bitcast.62, bf16[384,384]{1,0:T(8,128)(2,1)} %bitcast.61, ...), custom_call_target="tpu_custom_call" | custom-call | tf_op jit(solution)/shard_map/pack_weights/pallas_call | solution.py:562
  13.7 0.1 convert_reduce_fusion
  13.9 3.0 spread_images.2
  16.9 2.6 collective-permute-start.7
  19.5 1.8 multiply_convert_fusion
  21.3 1.6 collective-permute-start.9
  23.0 4.3 %collective-permute-start.1 = (bf16[2,256,512]{2,1,0:T(8,128)(2,1)}, bf16[2,256,512]{2,1,0:T(8,128)(2,1)}, u32[]{:S(2)}, u32[]{:S(2)}) collective-permute-start(bf16[2,256,512]{2,1,0:T(8,128)(2,1)} %get-tuple-element.59), channel_id=1, source_target_pairs={{0,2},{1,3},{3,1},{4,6},{6,4},{7,5},{8,10},{9,11},{11,9},{12,14},{... | collective-permute-start | bytes 1572872 | tf_op jit(solution)/shard_map/ppermute | solution.py:1481
  27.3 4.5 %collective-permute-start.2 = (bf16[2,256,512]{2,1,0:T(8,128)(2,1)}, bf16[2,256,512]{2,1,0:T(8,128)(2,1)}, u32[]{:S(2)}, u32[]{:S(2)}) collective-permute-start(bf16[2,256,512]{2,1,0:T(8,128)(2,1)} %get-tuple-element.60), channel_id=1, source_target_pairs={{0,4},{1,5},{2,6},{5,1},{6,2},{7,3},{8,12},{9,13},{10,14},{13,9},{... | collective-permute-start | bytes 1572872 | tf_op jit(solution)/shard_map/ppermute | solution.py:1481
  31.8 2.1 collective-permute-start.3
  33.9 3.0 spread_images.3
  37.0 13.2 %collective-permute-done.7.refs_1_.refs_10_.refs_15_.refs_19_.refs_9_ = bf16[2,2640,128]{2,1,0:T(8,128)(2,1)} collective-permute-done((bf16[2,2640,128]{2,1,0:T(8,128)(2,1)}, bf16[2,2640,128]{2,1,0:T(8,128)(2,1)}, u32[]{:S(2)}, u32[]{:S(2)}) %collective-permute-start.7) | collective-permute-done | bytes 1351712 | tf_op jit(solution)/shard_map/ppermute | solution.py:1453
  50.1 3.7 %collective-permute-start.5 = (bf16[2,256,512]{2,1,0:T(8,128)(2,1)}, bf16[2,256,512]{2,1,0:T(8,128)(2,1)S(1)}, u32[]{:S(2)}, u32[]{:S(2)}) collective-permute-start(bf16[2,256,512]{2,1,0:T(8,128)(2,1)} %get-tuple-element.62), channel_id=1, source_target_pairs={{0,2},{1,3},{3,1},{4,6},{6,4},{7,5},{8,10},{9,11},{11,9},{12,14},{... | collective-permute-start | bytes 1572872 | tf_op jit(solution)/shard_map/ppermute | solution.py:1481
  53.9 2.2 relay_weights.1
  56.1 1.6 collective-permute-start.10
  57.6 1.5 collective-permute-start.13
  59.2 0.5 collective-permute-start.12
  59.7 7.1 %collective-permute-done.5 = bf16[2,256,512]{2,1,0:T(8,128)(2,1)S(1)} collective-permute-done((bf16[2,256,512]{2,1,0:T(8,128)(2,1)}, bf16[2,256,512]{2,1,0:T(8,128)(2,1)S(1)}, u32[]{:S(2)}, u32[]{:S(2)}) %collective-permute-start.5) | collective-permute-done | bytes 524320 | tf_op jit(solution)/shard_map/ppermute | solution.py:1481
  66.8 5.0 %collective-permute-start.6 = (bf16[2,256,512]{2,1,0:T(8,128)(2,1)}, bf16[2,256,512]{2,1,0:T(8,128)(2,1)S(1)}, u32[]{:S(2)}, u32[]{:S(2)}) collective-permute-start(bf16[2,256,512]{2,1,0:T(8,128)(2,1)} %get-tuple-element.63), channel_id=1, source_target_pairs={{0,4},{1,5},{2,6},{5,1},{6,2},{7,3},{8,12},{9,13},{10,14},{13,9},{... | collective-permute-start | bytes 1572872 | tf_op jit(solution)/shard_map/ppermute | solution.py:1481
  71.8 1.0 collective-permute-done.10.refs_12_.refs_17_.refs_21_.refs_11_
  72.8 1.2 collective-permute-done.13.refs_16_.refs_21_.refs_25_.refs_15_
  74.0 9.9 %collective-permute-done.6 = bf16[2,256,512]{2,1,0:T(8,128)(2,1)S(1)} collective-permute-done((bf16[2,256,512]{2,1,0:T(8,128)(2,1)}, bf16[2,256,512]{2,1,0:T(8,128)(2,1)S(1)}, u32[]{:S(2)}, u32[]{:S(2)}) %collective-permute-start.6) | collective-permute-done | bytes 524320 | tf_op jit(solution)/shard_map/ppermute | solution.py:1481
  83.9 11.5 %collective-permute-start.15 = (bf16[2,256,512]{2,1,0:T(8,128)(2,1)}, bf16[2,256,512]{2,1,0:T(8,128)(2,1)}, u32[]{:S(2)}, u32[]{:S(2)}) collective-permute-start(bf16[2,256,512]{2,1,0:T(8,128)(2,1)} %get-tuple-element.70), channel_id=1, source_target_pairs={{0,6},{2,4},{3,5},{4,2},{5,3},{7,1},{8,14},{10,12},{11,13},{12,10}... | collective-permute-start | bytes 1572872 | tf_op jit(solution)/shard_map/ppermute | solution.py:1481
  95.5 0.8 copy-done.3
  96.3 0.9 copy-done.4
  97.2 19.1 %forward_0.1 = (bf16[2048,512]{1,0:T(8,128)(2,1)}, bf16[2048,192]{1,0:T(8,128)(2,1)}, bf16[1152,384]{1,0:T(8,128)(2,1)}, bf16[2048,512]{1,0:T(8,128)(2,1)}, bf16...) custom-call(s32[4]{0:T(128)} %pad_add_fusion.place.refs_0_, bf16[512,512]{1,0:T(8,128)(2,1)} %bitcast.50, ...), custom_call_target="tpu_custom_call" | custom-call | flops 1 | bytes 1 | tf_op jit(solution)/shard_map/forward_0/pallas_call | solution.py:1112
  116.4 89.7 %sections_1_3.1 = (bf16[512,512]{1,0:T(8,128)(2,1)}, bf16[512,512]{1,0:T(8,128)(2,1)}, bf16[512,512]{1,0:T(8,128)(2,1)}, bf16[512,512]{1,0:T(8,128)(2,1)}, bf16[...) custom-call(s32[4]{0:T(128)} %pad_add_fusion.place.refs_0_, ...), custom_call_target="tpu_custom_call", output_to_operand_aliasing={{0}: (6, {}), {1}: (7, {}), {2}: (8, {}), {3}: (9, {})} | custom-call | flops 48000000000 | bytes 20000000 | tf_op jit(solution)/shard_map/sections_1_3/pallas_call | solution.py:1112
  206.0 1.3 collective-permute-start.16
  207.3 1.3 collective-permute-start.17
  208.6 1.3 collective-permute-start.18
  209.9 27.1 %backward_0_norms.1 = (bf16[2048,512]{1,0:T(8,128)(2,1)}, bf16[2048,192]{1,0:T(8,128)(2,1)}, bf16[10560,128]{1,0:T(8,128)(2,1)}) custom-call(s32[4]{0:T(128)} %pad_add_fusion.place.refs_0_, bf16[512,512]{1,0:T(8,128)(2,1)} %get-tuple-element.75.refs_1_, bf16[512,512]{1,0:T(8,128)(2,1)} %get-tuple-element.76.refs_2_, ...), custom_call_target="tpu_custom_call", output_to_operand_aliasing={{2}: (17, {})} | custom-call | flops 3200000000 | bytes 20000000 | tf_op jit(solution)/shard_map/backward_0_norms/pallas_call | solution.py:1112
  237.0 12.2 %backward_0_convs.1 = (bf16[512,512]{1,0:T(8,128)(2,1)}, bf16[512,512]{1,0:T(8,128)(2,1)}, bf16[512,512]{1,0:T(8,128)(2,1)}, bf16[512,512]{1,0:T(8,128)(2,1)}) custom-call(s32[4]{0:T(128)} %pad_add_fusion.place.refs_0_, bf16[2048,512]{1,0:T(8,128)(2,1)} %get-tuple-element.86.refs_1_, ...), custom_call_target="tpu_custom_call", output_to_operand_aliasing={{0}: (4, {}), {1}: (5, {}), {2}: (6, {}), {3}: (7, {})} | custom-call | flops 4800000000 | bytes 20000000 | tf_op jit(solution)/shard_map/backward_0_convs/pallas_call | solution.py:1112
  249.2 1.3 collective-permute-start.20
  250.5 1.3 collective-permute-start.21
  251.9 1.3 collective-permute-start.22
  253.2 2.0 second_images.2
  255.2 4.5 %collective-permute-start.19 = (bf16[4,256,512]{2,1,0:T(8,128)(2,1)}, bf16[4,256,512]{2,1,0:T(8,128)(2,1)}, u32[]{:S(2)}, u32[]{:S(2)}) collective-permute-start(bf16[4,256,512]{2,1,0:T(8,128)(2,1)} %second_images.2), channel_id=1, source_target_pairs={{0,1},{1,0},{2,3},{3,2},{4,5},{5,4},{6,7},{7,6},{8,9},{9,8},{10,11... | collective-permute-start | bytes 3145736 | tf_op jit(solution)/shard_map/ppermute | solution.py:1478
  259.7 32.5 %collective-permute-done.20.p1 = bf16[512,512]{1,0:T(8,128)(2,1)S(1)} collective-permute-done((bf16[512,512]{1,0:T(8,128)(2,1)}, bf16[512,512]{1,0:T(8,128)(2,1)S(1)}, u32[]{:S(2)}, u32[]{:S(2)}) %collective-permute-start.20) | collective-permute-done | bytes 524320 | tf_op jit(solution)/shard_map/ppermute | solution.py:1481
  292.2 0.8 copy-done.8
  293.0 0.2 copy-done.9
  293.2 0.2 copy-done.10
  293.3 2.0 second_images.3
  295.4 3.4 collect_images.2
  298.8 3.9 %collect_images.3 = f32[6,256,512]{2,1,0:T(8,128)} custom-call(s32[4]{0:T(128)} %pad_add_fusion.place.refs_0_, bf16[512,512]{1,0:T(8,128)(2,1)} %get-tuple-element.93.p0, bf16[512,512]{1,0:T(8,128)(2,1)} %copy-done.8, bf16[512,512]{1,0:T(8,128)(2,1)} %copy-done.9, bf16[512,512]{1,0:T(8,128)(2,1)} %copy-done.10, ...), custom_call_target="tpu_custom_call" | custom-call | tf_op jit(solution)/shard_map/collect_images/pallas_call | solution.py:705
  302.8 49.0 %all-reduce.2.cloned.1.call-done.packed = bf16[10560,128]{1,0:T(8,128)(2,1)} async-done(((bf16[10560,128]{1,0:T(8,128)(2,1)}), bf16[10560,128]{1,0:T(8,128)(2,1)}) %all-reduce.2.cloned.1.call-update) | async-done | bytes 2703376 | tf_op jit(solution)/shard_map/psum | solution.py:1526
  351.8 4.2 %unpack_terms.1 = (f32[4608,128]{1,0:T(8,128)}, f32[1152,384]{1,0:T(8,128)}, f32[192,384]{1,0:T(8,128)}, f32[384,384]{1,0:T(8,128)}, f32[192,384]{1,0:T(8,128)}, /*index=5*/f32[1,1088]{1,0:T(1,128)}, f32[1,1088]{1,0:T(1,128)}) custom-call(bf16[10560,128]{1,0:T(8,128)(2,1)} %all-reduce.2.cloned.1.call-done.packed, bf16[1,6,1,16,16,512]{5,4,3,2,1,0:T(8,128)(2,1)} %bitcast.46, ...), custom_call_target="tpu_custom_call" | custom-call | tf_op jit(solution)/shard_map/unpack_terms/pallas_call | solution.py:614
  (49 shorter events, 0.4 us)
Async XLA Ops:
  7.2 344.6 %all-reduce.2.cloned.1.call-start = ((), (), s32[]{:S(2)}) async-start(), calls=%async_computation | async-start | bytes 5406720 | tf_op jit(solution)/shard_map/psum | solution.py:1526
  8.4 5.2 %copy-start.12 = (s32[6,1,16,16]{3,2,1,0:T(8,128)S(1)}, s32[6,1,16,16]{3,2,1,0:T(8,128)}, u32[]{:S(2)}) copy-start(s32[6,1,16,16]{3,2,1,0:T(8,128)} %param.23) | copy-start | bytes 18436
  8.4 5.4 %collective-permute-start = (bf16[3,256,512]{2,1,0:T(8,128)(2,1)S(1)}, bf16[3,256,512]{2,1,0:T(8,128)(2,1)}, u32[]{:S(2)}, u32[]{:S(2)}) collective-permute-start(bf16[3,256,512]{2,1,0:T(8,128)(2,1)S(1)} %dynamic-slice_bitcast_fusion.1), channel_id=1, source_target_pairs={{0,1},{1,0},{2,3},{3,2},{4,5},{5,4},{6,7},{7,6},{8,9},{9,8},{10,11... | collective-permute-start | bytes 2359304 | tf_op jit(solution)/shard_map/ppermute | solution.py:1478
  16.9 33.2 %collective-permute-start.7 = (bf16[2,2640,128]{2,1,0:T(8,128)(2,1)}, bf16[2,2640,128]{2,1,0:T(8,128)(2,1)}, u32[]{:S(2)}, u32[]{:S(2)}) collective-permute-start(bf16[2,2640,128]{2,1,0:T(8,128)(2,1)} %get-tuple-element.65), channel_id=1, source_target_pairs={{8,0},{0,8},{24,16},{16,24},{9,1},{1,9},{25,17},{17,25},{10,2},{2,... | collective-permute-start | bytes 4055048 | tf_op jit(solution)/shard_map/ppermute | solution.py:1453
  21.3 1.6 copy-start
  21.3 32.5 %collective-permute-start.9 = (bf16[2,2640,128]{2,1,0:T(8,128)(2,1)}, bf16[2,2640,128]{2,1,0:T(8,128)(2,1)}, u32[]{:S(2)}, u32[]{:S(2)}) collective-permute-start(bf16[2,2640,128]{2,1,0:T(8,128)(2,1)} %get-tuple-element.65), channel_id=1, source_target_pairs={{16,0},{24,8},{0,16},{8,24},{17,1},{25,9},{1,17},{9,25},{18,2},{26... | collective-permute-start | bytes 4055048 | tf_op jit(solution)/shard_map/ppermute | solution.py:1453
  23.0 8.9 %collective-permute-start.4 = (bf16[3,256,512]{2,1,0:T(8,128)(2,1)S(1)}, bf16[3,256,512]{2,1,0:T(8,128)(2,1)S(1)}, u32[]{:S(2)}, u32[]{:S(2)}) collective-permute-start(bf16[3,256,512]{2,1,0:T(8,128)(2,1)S(1)} %dynamic-slice_bitcast_fusion), channel_id=1, source_target_pairs={{0,1},{1,0},{2,3},{3,2},{4,5},{5,4},{6,7},{7,6},{8,9},{9,8},{10,11... | collective-permute-start | bytes 2359304 | tf_op jit(solution)/shard_map/ppermute | solution.py:1478
  23.0 34.6 %collective-permute-start.1 = (bf16[2,256,512]{2,1,0:T(8,128)(2,1)}, bf16[2,256,512]{2,1,0:T(8,128)(2,1)}, u32[]{:S(2)}, u32[]{:S(2)}) collective-permute-start(bf16[2,256,512]{2,1,0:T(8,128)(2,1)} %get-tuple-element.59), channel_id=1, source_target_pairs={{0,2},{1,3},{3,1},{4,6},{6,4},{7,5},{8,10},{9,11},{11,9},{12,14},{... | collective-permute-start | bytes 1572872 | tf_op jit(solution)/shard_map/ppermute | solution.py:1481
  27.3 31.8 %collective-permute-start.2 = (bf16[2,256,512]{2,1,0:T(8,128)(2,1)}, bf16[2,256,512]{2,1,0:T(8,128)(2,1)}, u32[]{:S(2)}, u32[]{:S(2)}) collective-permute-start(bf16[2,256,512]{2,1,0:T(8,128)(2,1)} %get-tuple-element.60), channel_id=1, source_target_pairs={{0,4},{1,5},{2,6},{5,1},{6,2},{7,3},{8,12},{9,13},{10,14},{13,9},{... | collective-permute-start | bytes 1572872 | tf_op jit(solution)/shard_map/ppermute | solution.py:1481
  31.8 2.1 copy-start.11
  31.8 27.3 %collective-permute-start.3 = (bf16[2,256,512]{2,1,0:T(8,128)(2,1)}, bf16[2,256,512]{2,1,0:T(8,128)(2,1)}, u32[]{:S(2)}, u32[]{:S(2)}) collective-permute-start(bf16[2,256,512]{2,1,0:T(8,128)(2,1)} %get-tuple-element.61), channel_id=1, source_target_pairs={{0,6},{2,4},{3,5},{4,2},{5,3},{7,1},{8,14},{10,12},{11,13},{12,10}... | collective-permute-start | bytes 1572872 | tf_op jit(solution)/shard_map/ppermute | solution.py:1481
  50.1 16.7 %collective-permute-start.5 = (bf16[2,256,512]{2,1,0:T(8,128)(2,1)}, bf16[2,256,512]{2,1,0:T(8,128)(2,1)S(1)}, u32[]{:S(2)}, u32[]{:S(2)}) collective-permute-start(bf16[2,256,512]{2,1,0:T(8,128)(2,1)} %get-tuple-element.62), channel_id=1, source_target_pairs={{0,2},{1,3},{3,1},{4,6},{6,4},{7,5},{8,10},{9,11},{11,9},{12,14},{... | collective-permute-start | bytes 1572872 | tf_op jit(solution)/shard_map/ppermute | solution.py:1481
  56.1 16.7 %collective-permute-start.10 = (bf16[1,2640,128]{2,1,0:T(8,128)(2,1)}, bf16[1,2640,128]{2,1,0:T(8,128)(2,1)S(1)}, u32[]{:S(2)}, u32[]{:S(2)}) collective-permute-start(bf16[1,2640,128]{2,1,0:T(8,128)(2,1)} %get-tuple-element.67), channel_id=1, source_target_pairs={{8,0},{0,8},{24,16},{16,24},{9,1},{1,9},{25,17},{17,25},{10,2},{2,... | collective-permute-start | bytes 2027528 | tf_op jit(solution)/shard_map/ppermute | solution.py:1453
  57.6 16.4 %collective-permute-start.13 = (bf16[1,2640,128]{2,1,0:T(8,128)(2,1)}, bf16[1,2640,128]{2,1,0:T(8,128)(2,1)S(1)}, u32[]{:S(2)}, u32[]{:S(2)}) collective-permute-start(bf16[1,2640,128]{2,1,0:T(8,128)(2,1)} %get-tuple-element.68), channel_id=1, source_target_pairs={{16,0},{24,8},{0,16},{8,24},{17,1},{25,9},{1,17},{9,25},{18,2},{26... | collective-permute-start | bytes 2027528 | tf_op jit(solution)/shard_map/ppermute | solution.py:1453
  59.2 36.2 %collective-permute-start.8 = (bf16[2,2640,128]{2,1,0:T(8,128)(2,1)}, bf16[2,2640,128]{2,1,0:T(8,128)(2,1)}, u32[]{:S(2)}, u32[]{:S(2)}) collective-permute-start(bf16[2,2640,128]{2,1,0:T(8,128)(2,1)} %collective-permute-done.7.refs_1_.refs_10_.refs_15_.refs_19_.refs_9_), channel_id=1, source_target_pairs={{0,1},{1,0},{2,3},{3,2},{4,5},{5,4},{6,7},{7,6},{8,9},{9,8},{10,11... | collective-permute-start | bytes 4055048 | tf_op jit(solution)/shard_map/ppermute | solution.py:1456
  59.2 36.3 %collective-permute-start.12 = (bf16[2,2640,128]{2,1,0:T(8,128)(2,1)}, bf16[2,2640,128]{2,1,0:T(8,128)(2,1)}, u32[]{:S(2)}, u32[]{:S(2)}) collective-permute-start(bf16[2,2640,128]{2,1,0:T(8,128)(2,1)} %collective-permute-done.9.refs_0_.refs_14_.refs_19_.refs_23_.refs_13_), channel_id=1, source_target_pairs={{0,1},{1,0},{2,3},{3,2},{4,5},{5,4},{6,7},{7,6},{8,9},{9,8},{10,11... | collective-permute-start | bytes 4055048 | tf_op jit(solution)/shard_map/ppermute | solution.py:1456
  66.8 30.4 %copy-start.5 = (bf16[2,256,512]{2,1,0:T(8,128)(2,1)}, bf16[2,256,512]{2,1,0:T(8,128)(2,1)S(1)}, u32[]{:S(2)}) copy-start(bf16[2,256,512]{2,1,0:T(8,128)(2,1)S(1)} %collective-permute-done.5) | copy-start | bytes 1572868
  66.8 17.1 %collective-permute-start.6 = (bf16[2,256,512]{2,1,0:T(8,128)(2,1)}, bf16[2,256,512]{2,1,0:T(8,128)(2,1)S(1)}, u32[]{:S(2)}, u32[]{:S(2)}) collective-permute-start(bf16[2,256,512]{2,1,0:T(8,128)(2,1)} %get-tuple-element.63), channel_id=1, source_target_pairs={{0,4},{1,5},{2,6},{5,1},{6,2},{7,3},{8,12},{9,13},{10,14},{13,9},{... | collective-permute-start | bytes 1572872 | tf_op jit(solution)/shard_map/ppermute | solution.py:1481
  72.8 24.4 %copy-start.1 = (bf16[1,2640,128]{2,1,0:T(8,128)(2,1)}, bf16[1,2640,128]{2,1,0:T(8,128)(2,1)S(1)}, u32[]{:S(2)}) copy-start(bf16[1,2640,128]{2,1,0:T(8,128)(2,1)S(1)} %collective-permute-done.10.refs_12_.refs_17_.refs_21_.refs_11_) | copy-start | bytes 2027524
  72.8 22.6 %collective-permute-start.11 = (bf16[1,2640,128]{2,1,0:T(8,128)(2,1)S(1)}, bf16[1,2640,128]{2,1,0:T(8,128)(2,1)S(1)}, u32[]{:S(2)}, u32[]{:S(2)}) collective-permute-start(bf16[1,2640,128]{2,1,0:T(8,128)(2,1)S(1)} %collective-permute-done.10.refs_12_.refs_17_.refs_21_.refs_11_), channel_id=1, source_target_pairs={{0,1},{1,0},{2,3},{3,2},{4,5},{5,4},{6,7},{7,6},{8,9},{9,8},{10,11... | collective-permute-start | bytes 2027528 | tf_op jit(solution)/shard_map/ppermute | solution.py:1456
  74.0 21.4 %copy-start.2 = (bf16[1,2640,128]{2,1,0:T(8,128)(2,1)}, bf16[1,2640,128]{2,1,0:T(8,128)(2,1)S(1)}, u32[]{:S(2)}) copy-start(bf16[1,2640,128]{2,1,0:T(8,128)(2,1)S(1)} %collective-permute-done.13.refs_16_.refs_21_.refs_25_.refs_15_) | copy-start | bytes 2027524
  74.0 21.4 %collective-permute-start.14 = (bf16[1,2640,128]{2,1,0:T(8,128)(2,1)S(1)}, bf16[1,2640,128]{2,1,0:T(8,128)(2,1)S(1)}, u32[]{:S(2)}, u32[]{:S(2)}) collective-permute-start(bf16[1,2640,128]{2,1,0:T(8,128)(2,1)S(1)} %collective-permute-done.13.refs_16_.refs_21_.refs_25_.refs_15_), channel_id=1, source_target_pairs={{0,1},{1,0},{2,3},{3,2},{4,5},{5,4},{6,7},{7,6},{8,9},{9,8},{10,11... | collective-permute-start | bytes 2027528 | tf_op jit(solution)/shard_map/ppermute | solution.py:1456
  83.9 13.3 %copy-start.6 = (bf16[2,256,512]{2,1,0:T(8,128)(2,1)}, bf16[2,256,512]{2,1,0:T(8,128)(2,1)S(1)}, u32[]{:S(2)}) copy-start(bf16[2,256,512]{2,1,0:T(8,128)(2,1)S(1)} %collective-permute-done.6) | copy-start | bytes 1572868
  83.9 32.4 %collective-permute-start.15 = (bf16[2,256,512]{2,1,0:T(8,128)(2,1)}, bf16[2,256,512]{2,1,0:T(8,128)(2,1)}, u32[]{:S(2)}, u32[]{:S(2)}) collective-permute-start(bf16[2,256,512]{2,1,0:T(8,128)(2,1)} %get-tuple-element.70), channel_id=1, source_target_pairs={{0,6},{2,4},{3,5},{4,2},{5,3},{7,1},{8,14},{10,12},{11,13},{12,10}... | collective-permute-start | bytes 1572872 | tf_op jit(solution)/shard_map/ppermute | solution.py:1481
  95.4 0.9 copy-start.3
  96.3 0.9 copy-start.4
  206.0 45.8 %collective-permute-start.16 = (bf16[512,512]{1,0:T(8,128)(2,1)}, bf16[512,512]{1,0:T(8,128)(2,1)S(1)}, u32[]{:S(2)}, u32[]{:S(2)}) collective-permute-start(bf16[512,512]{1,0:T(8,128)(2,1)} %get-tuple-element.72), channel_id=1, source_target_pairs={{2,0},{3,1},{1,3},{6,4},{4,6},{5,7},{10,8},{11,9},{9,11},{14,12},{... | collective-permute-start | bytes 1572872 | tf_op jit(solution)/shard_map/ppermute | solution.py:1481
  207.3 45.9 %collective-permute-start.17 = (bf16[512,512]{1,0:T(8,128)(2,1)}, bf16[512,512]{1,0:T(8,128)(2,1)}, u32[]{:S(2)}, u32[]{:S(2)}) collective-permute-start(bf16[512,512]{1,0:T(8,128)(2,1)} %get-tuple-element.73), channel_id=1, source_target_pairs={{4,0},{5,1},{6,2},{1,5},{2,6},{3,7},{12,8},{13,9},{14,10},{9,13},{... | collective-permute-start | bytes 1572872 | tf_op jit(solution)/shard_map/ppermute | solution.py:1481
  208.6 44.6 %collective-permute-start.18 = (bf16[512,512]{1,0:T(8,128)(2,1)}, bf16[512,512]{1,0:T(8,128)(2,1)}, u32[]{:S(2)}, u32[]{:S(2)}) collective-permute-start(bf16[512,512]{1,0:T(8,128)(2,1)} %get-tuple-element.74), channel_id=1, source_target_pairs={{6,0},{4,2},{5,3},{2,4},{3,5},{1,7},{14,8},{12,10},{13,11},{10,12}... | collective-permute-start | bytes 1572872 | tf_op jit(solution)/shard_map/ppermute | solution.py:1481
  249.2 42.9 %collective-permute-start.20 = (bf16[512,512]{1,0:T(8,128)(2,1)}, bf16[512,512]{1,0:T(8,128)(2,1)S(1)}, u32[]{:S(2)}, u32[]{:S(2)}) collective-permute-start(bf16[512,512]{1,0:T(8,128)(2,1)} %get-tuple-element.94), channel_id=1, source_target_pairs={{2,0},{3,1},{1,3},{6,4},{4,6},{5,7},{10,8},{11,9},{9,11},{14,12},{... | collective-permute-start | bytes 1572872 | tf_op jit(solution)/shard_map/ppermute | solution.py:1481
  250.5 41.6 %collective-permute-start.21 = (bf16[512,512]{1,0:T(8,128)(2,1)}, bf16[512,512]{1,0:T(8,128)(2,1)S(1)}, u32[]{:S(2)}, u32[]{:S(2)}) collective-permute-start(bf16[512,512]{1,0:T(8,128)(2,1)} %get-tuple-element.95), channel_id=1, source_target_pairs={{4,0},{5,1},{6,2},{1,5},{2,6},{3,7},{12,8},{13,9},{14,10},{9,13},{... | collective-permute-start | bytes 1572872 | tf_op jit(solution)/shard_map/ppermute | solution.py:1481
  251.9 1.4 copy-start.7
  251.9 40.3 %collective-permute-start.22 = (bf16[512,512]{1,0:T(8,128)(2,1)}, bf16[512,512]{1,0:T(8,128)(2,1)S(1)}, u32[]{:S(2)}, u32[]{:S(2)}) collective-permute-start(bf16[512,512]{1,0:T(8,128)(2,1)} %get-tuple-element.96), channel_id=1, source_target_pairs={{6,0},{4,2},{5,3},{2,4},{3,5},{1,7},{14,8},{12,10},{13,11},{10,12}... | collective-permute-start | bytes 1572872 | tf_op jit(solution)/shard_map/ppermute | solution.py:1481
  255.2 40.2 %collective-permute-start.19 = (bf16[4,256,512]{2,1,0:T(8,128)(2,1)}, bf16[4,256,512]{2,1,0:T(8,128)(2,1)}, u32[]{:S(2)}, u32[]{:S(2)}) collective-permute-start(bf16[4,256,512]{2,1,0:T(8,128)(2,1)} %second_images.2), channel_id=1, source_target_pairs={{0,1},{1,0},{2,3},{3,2},{4,5},{5,4},{6,7},{7,6},{8,9},{9,8},{10,11... | collective-permute-start | bytes 3145736 | tf_op jit(solution)/shard_map/ppermute | solution.py:1478
  292.2 0.8 copy-start.8
  292.2 1.0 copy-start.9
  292.2 1.1 copy-start.10
  295.3 3.5 collective-permute-start.23
Sparse Core Ops, SparseCore 0:
  253.3 98.4 all-reduce.1
